TPU v7x, 32 devices: a whole 2x2x4 slice. The times are simulated.
32 devices in a mesh: groups: 2 (over x), expo: 8 (over z, y), sky: 2 (over core).
Axes of the slice: x: 2, y: 2, z: 4, core: 2. Of those that a mesh axis runs over, the one named last changes fastest.
Arguments:
- exposures: bfloat16 [384, 256, 512], P(('groups', 'expo'), 'sky'), parts along dimension 0, may hold values from -8 to 8
- slot_ids: int32 [16, 24], P('groups'), parts along dimension 0, may hold values from 0 to 128, as said below
- row_range: int32 [256, 2], P('groups'), parts along dimension 0, may hold values from 1 to 256, as said below
- bad_bands: int32 [256, 4], P('groups'), parts along dimension 0, may hold values 0 or 1
- kernel_choice: int32 [256, 4], P('groups'), parts along dimension 0, may hold values from 0 to 9
- flux_scale: float32 [256], P('groups'), parts along dimension 0, may hold values from 0.25 to 4
- vert_taps: bfloat16 [20, 21], P('groups'), parts along dimension 0, may hold values from -0.6 to 1.6
- horiz_taps: bfloat16 [20, 21], P('groups'), parts along dimension 0, may hold values from -0.6 to 1.6
Outputs:
- coadd_plane: float32 [4, 128, 512], P(('groups', 'sky'), 'expo'), parts along dimension 0
- rejected_count: int32 [4, 128, 512], P(('groups', 'sky'), 'expo'), parts along dimension 0
There are 2 independent parts, one for each index of `groups`. A program takes and returns all parts, laid end to end along the dimension named above; each array names one. Nothing has to cross between parts.
Inputs may be any that keep to these rules, and one draw needn't show every extreme that they name: `slot_ids`: each exposure number below 128 stands in exactly one slot; in each row the occupied slots come first and the others hold 128; a row has 8 to 24 occupied slots, and some row has all 24. `row_range`: column 0 is below 128 and column 1 is at least 128 and above column 0.
All inputs are finite; a program needn't handle non-finite values.
Results may differ from a plain program's by a relative error of at most 0.008.
Values may be sent and summed in bfloat16 or wider, within the bound.
No kernel may reach another device: no remote copies, remote signals or barrier semaphores. Data moves between devices by JAX's collectives and lax.ppermute only.
A program may use at most 128 MiB of HBM per device.

v0:
```python
import functools

import jax
import jax.numpy as jnp
from jax import lax
from jax.experimental import pallas as pl
from jax.experimental.pallas import tpu as pltpu
from jax.sharding import PartitionSpec as P

BAND_COLS = 128
TAPS = 21
REJECT = 4
MIN_VALID = 12

SENTINEL = 1e30
HIGHEST = lax.Precision.HIGHEST

TILE_ROWS = 16
PAD = 16
SQUARE = 4
LISTS = 2 * REJECT + 1


def sort_pair(entries, first, second, up):
    a, b = entries[first], entries[second]
    hi, lo = jnp.maximum(a, b), jnp.minimum(a, b)
    entries[first], entries[second] = (hi, lo) if up else (lo, hi)


def sorted_four(entries, up):
    entries = list(entries)
    for first, second in ((0, 1), (2, 3), (0, 2), (1, 3), (1, 2)):
        sort_pair(entries, first, second, up)
    return entries


def merged_four(left, right, up, ordered=True):
    pick = jnp.maximum if up else jnp.minimum
    entries = [pick(left[i], right[REJECT - 1 - i]) for i in range(REJECT)]
    if ordered:
        for first, second in ((0, 2), (1, 3), (0, 1), (2, 3)):
            sort_pair(entries, first, second, up)
    return entries


def valid_sum(highs, lows):
    total = None
    for value in highs + lows:
        wide = value.astype(jnp.float32)
        wide = jnp.where(jnp.abs(wide) < 0.5 * SENTINEL, wide, 0.0)
        total = wide if total is None else total + wide
    return total


def block_kernel(
    slots,
    bands,
    kernels,
    exposures_total,
    rows,
    order_ref,
    table_ref,
    flux_ref,
    slot_ref,
    vert_ref,
    horiz_ref,
    exposures_ref,
    halo_ref,
    *rest,
):
    outs = rest[: rows // TILE_ROWS]
    pictures, high, low, total, bank_v, bank_h, padded, sems = rest[rows // TILE_ROWS :]
    margin = TAPS // 2
    high_rows = rows + 2 * PAD
    chunks = rows // TILE_ROWS
    half = order_ref[0]
    place = order_ref[1]
    sky_place = order_ref[2]
    use_halo = order_ref[3]
    group = 4
    row_dev = exposures_ref.shape[1]
    last = row_dev // rows - 1
    body_rows = rows + PAD
    start = pl.multiple_of(half * (row_dev - body_rows), TILE_ROWS)
    land = pl.multiple_of(PAD - PAD * half, TILE_ROWS)
    edge = pl.multiple_of(half * body_rows, TILE_ROWS)

    def body_copy(piece):
        return pltpu.make_async_copy(
            exposures_ref.at[pl.ds(piece * group, group), pl.ds(start, body_rows), :],
            pictures.at[pl.ds(piece * group, group), pl.ds(land, body_rows), :],
            sems.at[piece],
        )

    pieces = slots // group
    halo_copy = pltpu.make_async_copy(
        halo_ref, pictures.at[:, pl.ds(edge, PAD), :], sems.at[pieces]
    )
    halo_copy.start()
    for piece in range(pieces):
        body_copy(piece).start()

    padded[...] = jnp.zeros_like(padded)
    padded[0, :kernels, :TAPS] = vert_ref[...].astype(jnp.float32)
    padded[1, :kernels, :TAPS] = horiz_ref[...].astype(jnp.float32)
    vert_lines = pltpu.roll(padded[0], PAD - margin, 1)
    horiz_lines = pltpu.roll(padded[1], BAND_COLS - margin, 1)
    offset = lax.broadcasted_iota(jnp.int32, (BAND_COLS, BAND_COLS), 1) - (
        lax.broadcasted_iota(jnp.int32, (BAND_COLS, BAND_COLS), 0)
    )
    inside = jnp.abs(offset) < BAND_COLS // 2
    for kernel in range(kernels):
        line = jnp.broadcast_to(vert_lines[kernel : kernel + 1], (rows, BAND_COLS))
        banded = pltpu.roll(line, 0, 1, stride=1, stride_axis=0)
        bank_v[kernel] = banded[:, :high_rows].astype(jnp.bfloat16)
        line = jnp.broadcast_to(horiz_lines[kernel : kernel + 1], (BAND_COLS, BAND_COLS))
        banded = pltpu.roll(line, 0, 1, stride=1, stride_axis=0)
        bank_h[kernel, :BAND_COLS] = jnp.where(inside, banded, 0.0).T.astype(jnp.bfloat16)
        bank_h[kernel, BAND_COLS:] = jnp.where(inside, 0.0, banded).T.astype(jnp.bfloat16)

    total[...] = jnp.zeros_like(total)
    halo_copy.wait()

    @pl.when(use_halo == 0)
    def _():
        pictures[:, pl.ds(edge, PAD), :] = jnp.zeros_like(halo_ref)

    first_row = sky_place * row_dev + half * rows
    row_index = first_row + lax.broadcasted_iota(jnp.int32, (rows, BAND_COLS), 0)
    lane = lax.broadcasted_iota(jnp.int32, (rows, BAND_COLS), 1)

    def one_slot(slot):
        ident = slot_ref[place, slot]
        occupied = ident < exposures_total
        k = jnp.minimum(ident, exposures_total - 1)
        span = table_ref[bands, k]
        begin = lax.rem(span, 65536)
        end = jnp.where(occupied, lax.div(span, 65536), 0)
        factor = flux_ref[k]
        codes = [table_ref[band, k] for band in range(bands)]
        chosen = [lax.rem(code, 65536) for code in codes]
        columns = []
        for band in range(bands):
            picture = pictures[slot, :, band * BAND_COLS : (band + 1) * BAND_COLS]
            vertical = jnp.dot(
                bank_v[chosen[band]], picture, preferred_element_type=jnp.float32
            )
            columns.append(vertical.astype(jnp.bfloat16))
        nothing = jnp.zeros_like(columns[0])
        for band in range(bands):
            before = columns[band - 1] if band else nothing
            after = columns[band + 1] if band + 1 < bands else nothing
            sides = jnp.where(lane < BAND_COLS // 2, after, before)
            filtered = jnp.dot(
                jnp.concatenate([columns[band], sides], 1),
                bank_h[chosen[band]],
                preferred_element_type=jnp.float32,
            )
            plane = (filtered * factor).astype(jnp.bfloat16).astype(jnp.float32)
            stop = jnp.where(codes[band] >= 65536, 0, end)
            usable = (row_index >= begin) & (row_index < stop)
            window = pl.ds(band * BAND_COLS, BAND_COLS)
            total[:, window] += jnp.where(usable, plane, 0.0)
            high[slot, :, window] = jnp.where(usable, plane, -SENTINEL).astype(jnp.bfloat16)
            low[slot, :, window] = jnp.where(usable, plane, SENTINEL).astype(jnp.bfloat16)

    for piece in range(pieces):
        body_copy(piece).wait()

        def body(step, carry):
            one_slot(piece * group + 2 * step)
            one_slot(piece * group + 2 * step + 1)
            return carry

        lax.fori_loop(0, group // 2, body, 0)

    for position, out in enumerate(outs):
        top = pl.multiple_of(order_ref[4 + position] * TILE_ROWS, TILE_ROWS)

        def tile(step, carry):
            window = pl.ds(pl.multiple_of(step * BAND_COLS, BAND_COLS), BAND_COLS)
            sides = []
            for source, up in ((high, True), (low, False)):
                best = None
                for piece in range(slots // REJECT):
                    entries = [
                        source[piece * REJECT + i, pl.ds(top, TILE_ROWS), window]
                        for i in range(REJECT)
                    ]
                    entries = sorted_four(entries, up)
                    best = entries if best is None else merged_four(best, entries, up)
                sides.append(best)
            left = total[pl.ds(top, TILE_ROWS), window] - valid_sum(*sides)
            for index, value in enumerate(sides[0] + sides[1]):
                out[index, :, window] = value
            out[2 * REJECT, :, window] = left.astype(jnp.bfloat16)
            return carry

        lax.fori_loop(0, bands, tile, 0)


def filter_block(order, table, flux, slot_ids, vert, horiz, exposures, halo, rows):
    slots, row_dev, columns = exposures.shape
    kernels = vert.shape[0]
    bands = columns // BAND_COLS
    chunks = rows // TILE_ROWS
    smem = pl.BlockSpec(memory_space=pltpu.SMEM)
    vmem = pl.BlockSpec(memory_space=pltpu.VMEM)
    anywhere = pl.BlockSpec(memory_space=pl.ANY)
    body = functools.partial(block_kernel, slots, bands, kernels, flux.shape[0], rows)
    kernel_rows = -(-kernels // 8) * 8
    return pl.pallas_call(
        body,
        out_shape=[jax.ShapeDtypeStruct((LISTS, TILE_ROWS, columns), jnp.bfloat16)] * chunks,
        in_specs=[smem, smem, smem, smem, vmem, vmem, anywhere, anywhere],
        out_specs=[vmem] * chunks,
        scratch_shapes=[
            pltpu.VMEM((slots, rows + 2 * PAD, columns), jnp.bfloat16),
            pltpu.VMEM((slots, rows, columns), jnp.bfloat16),
            pltpu.VMEM((slots, rows, columns), jnp.bfloat16),
            pltpu.VMEM((rows, columns), jnp.float32),
            pltpu.VMEM((kernels, rows, rows + 2 * PAD), jnp.bfloat16),
            pltpu.VMEM((kernels, 2 * BAND_COLS, BAND_COLS), jnp.bfloat16),
            pltpu.VMEM((2, kernel_rows, BAND_COLS), jnp.float32),
            pltpu.SemaphoreType.DMA((slots // 4 + 1,)),
        ],
        compiler_params=pltpu.CompilerParams(vmem_limit_bytes=32 * 1024 * 1024),
        cost_estimate=pl.CostEstimate(
            flops=4 * slots * rows * columns * 256, bytes_accessed=8 << 20, transcendentals=0
        ),
        name="filter_block",
    )(order, table, flux, slot_ids, vert, horiz, exposures, halo)


def merged_lists(refs, window, ordered):
    sides = []
    for base, up in ((0, True), (REJECT, False)):
        lists = [[ref[base + i, :, window] for i in range(REJECT)] for ref in refs]
        while len(lists) > 1:
            keep = ordered or len(lists) > 2
            paired = [
                merged_four(lists[i], lists[i + 1], up, keep)
                for i in range(0, len(lists) - 1, 2)
            ]
            lists = paired + (lists[-1:] if len(lists) % 2 else [])
        sides.append(lists[0])
    grand = None
    for ref in refs:
        part = ref[2 * REJECT, :, window].astype(jnp.float32) + valid_sum(
            [ref[i, :, window] for i in range(REJECT)],
            [ref[REJECT + i, :, window] for i in range(REJECT)],
        )
        grand = part if grand is None else grand + part
    return sides, grand


def merge_kernel(*refs):
    *sources, out = refs
    for band in range(out.shape[-1] // BAND_COLS):
        window = pl.ds(band * BAND_COLS, BAND_COLS)
        sides, grand = merged_lists(sources, window, True)
        for index, value in enumerate(sides[0] + sides[1]):
            out[index, :, window] = value
        out[2 * REJECT, :, window] = (grand - valid_sum(*sides)).astype(jnp.bfloat16)


def merge(parts):
    vmem = pl.BlockSpec(memory_space=pltpu.VMEM)
    return pl.pallas_call(
        merge_kernel,
        out_shape=jax.ShapeDtypeStruct(parts[0].shape, jnp.bfloat16),
        in_specs=[vmem] * len(parts),
        out_specs=vmem,
        name="merge_lists",
    )(*parts)


def finish_kernel(exposures_total, *refs):
    *sources, count_ref, coadd_ref, rejected_ref = refs
    for band in range(coadd_ref.shape[-1] // BAND_COLS):
        window = pl.ds(band * BAND_COLS, BAND_COLS)
        sides, grand = merged_lists(sources, window, False)
        extremes = valid_sum(*sides)
        count = count_ref[:, window]
        clipped = count >= MIN_VALID
        used = jnp.where(clipped, count - 2 * REJECT, count)
        kept = jnp.where(clipped, grand - extremes, grand)
        coadd_ref[:, window] = kept / jnp.maximum(used, 1).astype(jnp.float32)
        rejected_ref[:, window] = exposures_total - used


def finish(parts, count, exposures_total):
    vmem = pl.BlockSpec(memory_space=pltpu.VMEM)
    return pl.pallas_call(
        functools.partial(finish_kernel, exposures_total),
        out_shape=[
            jax.ShapeDtypeStruct(count.shape, jnp.float32),
            jax.ShapeDtypeStruct(count.shape, jnp.int32),
        ],
        in_specs=[vmem] * (len(parts) + 1),
        out_specs=[vmem, vmem],
        name="finish_pixels",
    )(*parts, count)


def usable_count(first_row, row_count, row_range, bad_bands):
    row_place = (first_row + jnp.arange(row_count, dtype=jnp.int32)).astype(jnp.float32)
    bounds = row_range.astype(jnp.float32)
    covered = (
        (row_place[None, :] >= bounds[:, 0:1]) & (row_place[None, :] < bounds[:, 1:2])
    ).astype(jnp.float32)
    clean = (bad_bands == 0).astype(jnp.float32)
    per_band = jnp.dot(covered.T, clean, precision=HIGHEST)
    return jnp.repeat(per_band, BAND_COLS, axis=1).astype(jnp.int32)


def swapped(value, axis, distance):
    count = lax.axis_size(axis)
    return lax.ppermute(value, axis, [(i, i ^ distance) for i in range(count)])


def shards(
    exposures, slot_ids, row_range, bad_bands, kernel_choice, flux_scale, vert_taps, horiz_taps
):
    slot_count, row_dev, columns = exposures.shape
    exposures_total = flux_scale.shape[0]
    expo_size = lax.axis_size("expo")
    expo_place = lax.axis_index("expo")
    sky_place = lax.axis_index("sky")
    rows = row_dev // 2
    rows_out = row_dev // expo_size
    chunks = rows // TILE_ROWS

    edge_rows = lax.dynamic_slice_in_dim(exposures, (1 - sky_place) * (row_dev - PAD), PAD, 1)
    halo = swapped(edge_rows, "sky", 1)

    table = jnp.concatenate(
        [
            kernel_choice + 65536 * (bad_bands != 0).astype(jnp.int32),
            row_range[:, 0:1] + 65536 * row_range[:, 1:2],
        ],
        1,
    ).T

    def block(half, chunk_order):
        order = jnp.stack(
            [half, expo_place, sky_place, (half != sky_place).astype(jnp.int32)] + chunk_order
        ).astype(jnp.int32)
        return filter_block(
            order, table, flux_scale, slot_ids, vert_taps, horiz_taps, exposures, halo, rows
        )

    first_row = sky_place * row_dev + expo_place * rows_out
    count = usable_count(first_row, rows_out, row_range, bad_bands)

    if rows_out == TILE_ROWS and expo_size == 2 * SQUARE:
        near = lax.div(expo_place, SQUARE)
        corner = lax.rem(expo_place, SQUARE)
        chunk_order = [corner ^ distance for distance in range(SQUARE)]
        far_own, *far_sent = block(1 - near, chunk_order)
        far_got = [swapped(part, "expo", 1 + i) for i, part in enumerate(far_sent)]
        near_own, *near_sent = block(near, chunk_order)
        near_got = [swapped(part, "expo", 1 + i) for i, part in enumerate(near_sent)]
        across = swapped(merge([far_own] + far_got), "expo", SQUARE)
        coadd_plane, rejected_count = finish(
            [near_own] + near_got + [across], count, exposures_total
        )
    else:
        natural = [jnp.int32(chunk) for chunk in range(chunks)]
        blocks = block(jnp.int32(0), natural) + block(jnp.int32(1), natural)
        whole = jnp.concatenate(blocks, 1)
        arrived = lax.all_to_all(whole, "expo", split_axis=1, concat_axis=0, tiled=True)
        arrived = arrived.reshape(expo_size, LISTS, rows_out, columns)
        coadd_plane, rejected_count = finish(
            [arrived[i] for i in range(expo_size)], count, exposures_total
        )
    return (coadd_plane[None], rejected_count[None])


def solution(mesh):
    in_specs = (
        P(("groups", "expo"), "sky", None),
        P("groups", None),
        P("groups", None),
        P("groups", None),
        P("groups", None),
        P("groups"),
        P("groups", None),
        P("groups", None),
    )
    out_specs = (P(("groups", "sky"), "expo", None), P(("groups", "sky"), "expo", None))
    return jax.shard_map(shards, mesh=mesh, in_specs=in_specs, out_specs=out_specs, check_vma=False)
```

profile of v0, /device:TPU:0, one launch (start us, length us, event | category | flops | bytes accessed | tf_op | source)
XLA Modules:
  0.0 50.2 jit_solution(8430255663871525458)
XLA Ops:
  0.6 0.0 copy-start.7
  0.6 0.0 copy-start.5
  0.7 1.0 %constant_dynamic-slice_fusion = bf16[24,16,512]{2,1,0:T(8,128)(2,1)S(1)} fusion(bf16[24,128,512]{2,1,0:T(8,128)(2,1)} %exposures_ref.3, s32[]{:T(128)S(6)} %select_n.3), kind=kLoop, calls=%fused_computation.15 | loop fusion | bytes 786436 | tf_op jit(solution)/shard_map/dynamic_slice | solution.py:334
  1.7 0.5 %collective-permute-start = (bf16[24,16,512]{2,1,0:T(8,128)(2,1)S(1)}, bf16[24,16,512]{2,1,0:T(8,128)(2,1)S(1)}, u32[]{:S(2)}, u32[]{:S(2)}) collective-permute-start(bf16[24,16,512]{2,1,0:T(8,128)(2,1)S(1)} %constant_dynamic-slice_fusion), channel_id=1, source_target_pairs={{0,1},{1,0},{2,3},{3,2},{4,5},{5,4},{6,7},{7,6},{8,9},{9,8},{10,11... | collective-permute-start | bytes 1179656 | tf_op jit(solution)/shard_map/ppermute | solution.py:319
  2.2 0.7 %select_add_fusion = s32[128,4]{0,1:T(4,128)S(1)} fusion(s32[128,4]{0,1:T(4,128)} %param.12, s32[128,4]{0,1:T(4,128)} %param.11), kind=kLoop, calls=%fused_computation.8 | loop fusion | flops 1536 | bytes 6144 | tf_op jit(solution)/shard_map/add | solution.py:339
  2.9 0.8 %multiply_add_fusion = s32[128,1]{0,1:T(1,128)S(1)} fusion(s32[128,2]{0,1:T(2,128)} %param.10), kind=kLoop, calls=%fused_computation.14 | loop fusion | flops 256 | bytes 1536 | tf_op jit(solution)/shard_map/add | solution.py:340
  3.7 0.7 %convert_element_type.21 = f32[128,2]{0,1:T(2,128)S(1)} convert(s32[128,2]{0,1:T(2,128)} %param.10) | non-fusion elementwise | flops 256 | bytes 2048 | tf_op jit(solution)/shard_map/convert_element_type | solution.py:308
  4.4 0.1 stack.61.order_ref
  4.4 0.1 stack.57.order_ref
  4.5 0.0 collective-permute-done.halo_ref
  4.6 0.0 copy-start
  4.6 1.9 %copy-done = bf16[24,128,512]{2,1,0:T(8,128)(2,1)S(1)} copy-done((bf16[24,128,512]{2,1,0:T(8,128)(2,1)S(1)}, bf16[24,128,512]{2,1,0:T(8,128)(2,1)}, u32[]{:S(2)}) %copy-start) | copy-done | bytes 3145752
  6.5 0.0 copy-start.4
  6.5 0.7 %copy-done.4 = s32[8,24]{1,0:T(8,128)S(1)} copy-done((s32[8,24]{1,0:T(8,128)S(1)}, s32[8,24]{1,0:T(8,128)}, u32[]{:S(2)}) %copy-start.4) | copy-done | bytes 792
  7.1 0.0 copy-start.6
  7.1 0.7 %copy-done.6 = bf16[10,21]{1,0:T(8,128)(2,1)S(1)} copy-done((bf16[10,21]{1,0:T(8,128)(2,1)S(1)}, bf16[10,21]{1,0:T(8,128)(2,1)}, u32[]{:S(2)}) %copy-start.6) | copy-done | bytes 444
  7.8 0.0 copy-start.8
  7.8 0.7 %copy-done.8 = bf16[10,21]{1,0:T(8,128)(2,1)S(1)} copy-done((bf16[10,21]{1,0:T(8,128)(2,1)S(1)}, bf16[10,21]{1,0:T(8,128)(2,1)}, u32[]{:S(2)}) %copy-start.8) | copy-done | bytes 444
  8.5 0.7 %copy-done.9 = f32[128]{0:T(128)S(1)} copy-done((f32[128]{0:T(128)S(1)}, f32[128]{0:T(128)}, u32[]{:S(2)}) %copy-start.9) | copy-done | bytes 536
  9.2 0.0 copy-start.1
  9.2 0.0 copy-start.17
  9.2 8.8 %filter_block.3 = (bf16[9,16,512]{2,1,0:T(8,128)(2,1)S(1)}, bf16[9,16,512]{2,1,0:T(8,128)(2,1)S(1)}, bf16[9,16,512]{2,1,0:T(8,128)(2,1)S(1)}, bf16[9,16,512]{2,1,0:T(8,128)(2,1)S(1)}) custom-call(s32[8]{0:T(128)S(1)} %stack.61.order_ref, s32[5,128]{1,0:T(8,128)S(1)} %add_bitcast_fusion.table_ref, f32[128]{0:T(128)S(1)} %copy-done.9, s32[8,24]{1,0:T(8,128)S(1)} %copy-done.4, ...), custom_call_target="tpu_custom_call" | custom-call | flops 805306368 | bytes 8388608 | tf_op jit(solution)/shard_map/filter_block/pallas_call | solution.py:212
  18.0 0.0 copy-start.3
  18.0 2.6 %collective-permute-start.4 = (bf16[9,16,512]{2,1,0:T(8,128)(2,1)S(1)}, bf16[9,16,512]{2,1,0:T(8,128)(2,1)S(1)}, u32[]{:S(2)}, u32[]{:S(2)}) collective-permute-start(bf16[9,16,512]{2,1,0:T(8,128)(2,1)S(1)} %get-tuple-element.17), channel_id=1, source_target_pairs={{0,2},{2,0},{4,6},{6,4},{8,10},{10,8},{12,14},{14,12},{1,3},{3,1},... | collective-permute-start | bytes 442376 | tf_op jit(solution)/shard_map/ppermute | solution.py:319
  20.6 1.6 %collective-permute-start.5 = (bf16[9,16,512]{2,1,0:T(8,128)(2,1)S(1)}, bf16[9,16,512]{2,1,0:T(8,128)(2,1)S(1)}, u32[]{:S(2)}, u32[]{:S(2)}) collective-permute-start(bf16[9,16,512]{2,1,0:T(8,128)(2,1)S(1)} %get-tuple-element.18), channel_id=1, source_target_pairs={{0,4},{2,6},{4,0},{6,2},{8,12},{10,14},{12,8},{14,10},{1,5},{3,7},... | collective-permute-start | bytes 442376 | tf_op jit(solution)/shard_map/ppermute | solution.py:319
  22.2 0.0 collective-permute-start.6
  22.2 0.0 copy-done.7
  22.2 0.0 copy-done.5
  22.2 0.0 copy-done.1
  22.2 8.9 %filter_block.2 = (bf16[9,16,512]{2,1,0:T(8,128)(2,1)S(1)}, bf16[9,16,512]{2,1,0:T(8,128)(2,1)S(1)}, bf16[9,16,512]{2,1,0:T(8,128)(2,1)S(1)}, bf16[9,16,512]{2,1,0:T(8,128)(2,1)S(1)}) custom-call(s32[8]{0:T(128)S(1)} %stack.57.order_ref, s32[5,128]{1,0:T(8,128)S(1)} %add_bitcast_fusion.table_ref, f32[128]{0:T(128)S(1)} %copy-done.9, s32[8,24]{1,0:T(8,128)S(1)} %copy-done.5, ...), custom_call_target="tpu_custom_call" | custom-call | flops 805306368 | bytes 8388608 | tf_op jit(solution)/shard_map/filter_block/pallas_call | solution.py:212
  31.1 0.0 copy-done.3
  31.1 0.0 copy-start.2
  31.1 0.7 %copy-done.2 = bf16[9,16,512]{2,1,0:T(8,128)(2,1)} copy-done((bf16[9,16,512]{2,1,0:T(8,128)(2,1)}, bf16[9,16,512]{2,1,0:T(8,128)(2,1)S(1)}, u32[]{:S(2)}) %copy-start.2) | copy-done | bytes 147480
  31.8 1.9 %collective-permute-start.1 = (bf16[9,16,512]{2,1,0:T(8,128)(2,1)S(1)}, bf16[9,16,512]{2,1,0:T(8,128)(2,1)S(1)}, u32[]{:S(2)}, u32[]{:S(2)}) collective-permute-start(bf16[9,16,512]{2,1,0:T(8,128)(2,1)S(1)} %get-tuple-element.13), channel_id=1, source_target_pairs={{0,2},{2,0},{4,6},{6,4},{8,10},{10,8},{12,14},{14,12},{1,3},{3,1},... | collective-permute-start | bytes 442376 | tf_op jit(solution)/shard_map/ppermute | solution.py:319
  33.7 1.6 %collective-permute-start.2 = (bf16[9,16,512]{2,1,0:T(8,128)(2,1)S(1)}, bf16[9,16,512]{2,1,0:T(8,128)(2,1)S(1)}, u32[]{:S(2)}, u32[]{:S(2)}) collective-permute-start(bf16[9,16,512]{2,1,0:T(8,128)(2,1)S(1)} %get-tuple-element.14), channel_id=1, source_target_pairs={{0,4},{2,6},{4,0},{6,2},{8,12},{10,14},{12,8},{14,10},{1,5},{3,7},... | collective-permute-start | bytes 442376 | tf_op jit(solution)/shard_map/ppermute | solution.py:319
  35.2 0.0 collective-permute-done.4.refs_1_
  35.3 0.0 copy-start.13
  35.3 0.0 collective-permute-start.3
  35.3 0.0 collective-permute-done.5.refs_2_
  35.3 0.0 copy-start.14
  35.3 0.0 collective-permute-done.6.refs_3_
  35.3 0.0 copy-start.15
  35.3 0.6 %copy-done.13 = bf16[9,16,512]{2,1,0:T(8,128)(2,1)} copy-done((bf16[9,16,512]{2,1,0:T(8,128)(2,1)}, bf16[9,16,512]{2,1,0:T(8,128)(2,1)S(1)}, u32[]{:S(2)}) %copy-start.13) | copy-done | bytes 147480
  35.9 0.0 copy-done.14
  36.0 0.1 copy-done.15
  36.0 2.1 %merge_lists.1 = bf16[9,16,512]{2,1,0:T(8,128)(2,1)} custom-call(bf16[9,16,512]{2,1,0:T(8,128)(2,1)} %copy-done.3, bf16[9,16,512]{2,1,0:T(8,128)(2,1)} %copy-done.13, bf16[9,16,512]{2,1,0:T(8,128)(2,1)} %copy-done.14, bf16[9,16,512]{2,1,0:T(8,128)(2,1)} %copy-done.15), custom_call_target="tpu_custom_call" | custom-call | tf_op jit(solution)/shard_map/merge_lists/pallas_call | solution.py:269
  38.1 2.9 %collective-permute-start.7 = (bf16[9,16,512]{2,1,0:T(8,128)(2,1)}, bf16[9,16,512]{2,1,0:T(8,128)(2,1)S(1)}, u32[]{:S(2)}, u32[]{:S(2)}) collective-permute-start(bf16[9,16,512]{2,1,0:T(8,128)(2,1)} %merge_lists.1), channel_id=1, source_target_pairs={{0,8},{2,10},{4,12},{6,14},{8,0},{10,2},{12,4},{14,6},{1,9},{3,11}... | collective-permute-start | bytes 442376 | tf_op jit(solution)/shard_map/ppermute | solution.py:319
  41.0 0.0 copy-done.17
  41.0 0.2 convolution_convert_fusion
  41.2 0.1 copy.11
  41.3 0.1 broadcast_in_dim.11
  41.4 0.6 %copy.14 = s32[2,8,4,128]{3,1,2,0:T(8,128)} copy(s32[2,8,4,128]{3,2,1,0:T(4,128)S(1)} %bitcast.23) | data formatting | bytes 65536
  42.0 0.0 collective-permute-done.1.refs_1_
  42.0 0.0 collective-permute-done.2.refs_2_
  42.0 0.0 copy-start.11
  42.1 0.0 collective-permute-done.3.refs_3_
  42.1 0.0 copy-start.12
  42.1 5.2 %collective-permute-done.7.refs_4_ = bf16[9,16,512]{2,1,0:T(8,128)(2,1)S(1)} collective-permute-done((bf16[9,16,512]{2,1,0:T(8,128)(2,1)}, bf16[9,16,512]{2,1,0:T(8,128)(2,1)S(1)}, u32[]{:S(2)}, u32[]{:S(2)}) %collective-permute-start.7) | collective-permute-done | bytes 147488 | tf_op jit(solution)/shard_map/ppermute | solution.py:319
  47.3 0.0 copy-start.16
  47.3 0.0 copy-done.10
  47.3 0.0 copy-done.11
  47.3 0.0 copy-done.12
  47.3 0.6 %copy-done.16 = bf16[9,16,512]{2,1,0:T(8,128)(2,1)} copy-done((bf16[9,16,512]{2,1,0:T(8,128)(2,1)}, bf16[9,16,512]{2,1,0:T(8,128)(2,1)S(1)}, u32[]{:S(2)}) %copy-start.16) | copy-done | bytes 147480
  47.9 2.2 %finish_pixels.1 = (f32[16,512]{1,0:T(8,128)}, s32[16,512]{1,0:T(8,128)}) custom-call(bf16[9,16,512]{2,1,0:T(8,128)(2,1)} %copy-done.2, bf16[9,16,512]{2,1,0:T(8,128)(2,1)} %copy-done.10, bf16[9,16,512]{2,1,0:T(8,128)(2,1)} %copy-done.11, bf16[9,16,512]{2,1,0:T(8,128)(2,1)} %copy-done.12, bf16[9,16,512]{2,1,0:T(8,128)(2,1)} %copy-done.16, s32[16,512]{1,0:T(8,128)} %bitcast.22), custom_call_target="tpu_custom_call" | custom-call | tf_op jit(solution)/shard_map/finish_pixels/pallas_call | solution.py:294
  (5 shorter events, 0.0 us)
Async XLA Ops:
  0.6 21.6 %copy-start.7 = (bf16[10,21]{1,0:T(8,128)(2,1)S(1)}, bf16[10,21]{1,0:T(8,128)(2,1)}, u32[]{:S(2)}) copy-start(bf16[10,21]{1,0:T(8,128)(2,1)} %vert_ref.3) | copy-start | bytes 1264
  0.6 21.6 %copy-start.5 = (s32[8,24]{1,0:T(8,128)S(1)}, s32[8,24]{1,0:T(8,128)}, u32[]{:S(2)}) copy-start(s32[8,24]{1,0:T(8,128)} %slot_ref.3) | copy-start | bytes 2308
  1.7 2.9 %collective-permute-start = (bf16[24,16,512]{2,1,0:T(8,128)(2,1)S(1)}, bf16[24,16,512]{2,1,0:T(8,128)(2,1)S(1)}, u32[]{:S(2)}, u32[]{:S(2)}) collective-permute-start(bf16[24,16,512]{2,1,0:T(8,128)(2,1)S(1)} %constant_dynamic-slice_fusion), channel_id=1, source_target_pairs={{0,1},{1,0},{2,3},{3,2},{4,5},{5,4},{6,7},{7,6},{8,9},{9,8},{10,11... | collective-permute-start | bytes 1179656 | tf_op jit(solution)/shard_map/ppermute | solution.py:319
  4.6 1.9 %copy-start = (bf16[24,128,512]{2,1,0:T(8,128)(2,1)S(1)}, bf16[24,128,512]{2,1,0:T(8,128)(2,1)}, u32[]{:S(2)}) copy-start(bf16[24,128,512]{2,1,0:T(8,128)(2,1)} %exposures_ref.3) | copy-start | bytes 9437188
  6.5 0.7 %copy-start.4 = (s32[8,24]{1,0:T(8,128)S(1)}, s32[8,24]{1,0:T(8,128)}, u32[]{:S(2)}) copy-start(s32[8,24]{1,0:T(8,128)} %slot_ref.3) | copy-start | bytes 2308
  7.1 0.7 %copy-start.6 = (bf16[10,21]{1,0:T(8,128)(2,1)S(1)}, bf16[10,21]{1,0:T(8,128)(2,1)}, u32[]{:S(2)}) copy-start(bf16[10,21]{1,0:T(8,128)(2,1)} %vert_ref.3) | copy-start | bytes 1264
  7.8 0.7 %copy-start.8 = (bf16[10,21]{1,0:T(8,128)(2,1)S(1)}, bf16[10,21]{1,0:T(8,128)(2,1)}, u32[]{:S(2)}) copy-start(bf16[10,21]{1,0:T(8,128)(2,1)} %horiz_ref.3) | copy-start | bytes 1264
  8.5 0.7 %copy-start.9 = (f32[128]{0:T(128)S(1)}, f32[128]{0:T(128)}, u32[]{:S(2)}) copy-start(f32[128]{0:T(128)} %flux_ref.3) | copy-start | bytes 1540
  9.2 13.0 %copy-start.1 = (bf16[24,128,512]{2,1,0:T(8,128)(2,1)S(1)}, bf16[24,128,512]{2,1,0:T(8,128)(2,1)}, u32[]{:S(2)}) copy-start(bf16[24,128,512]{2,1,0:T(8,128)(2,1)} %exposures_ref.3) | copy-start | bytes 9437188
  9.2 31.9 %copy-start.17 = (s32[128,4]{0,1:T(4,128)S(1)}, s32[128,4]{0,1:T(4,128)}, u32[]{:S(2)}) copy-start(s32[128,4]{0,1:T(4,128)} %param.11) | copy-start | bytes 6148
  18.0 13.1 %copy-start.3 = (bf16[9,16,512]{2,1,0:T(8,128)(2,1)}, bf16[9,16,512]{2,1,0:T(8,128)(2,1)S(1)}, u32[]{:S(2)}) copy-start(bf16[9,16,512]{2,1,0:T(8,128)(2,1)S(1)} %get-tuple-element.16.refs_0_) | copy-start | bytes 442372
  18.0 17.2 %collective-permute-start.4 = (bf16[9,16,512]{2,1,0:T(8,128)(2,1)S(1)}, bf16[9,16,512]{2,1,0:T(8,128)(2,1)S(1)}, u32[]{:S(2)}, u32[]{:S(2)}) collective-permute-start(bf16[9,16,512]{2,1,0:T(8,128)(2,1)S(1)} %get-tuple-element.17), channel_id=1, source_target_pairs={{0,2},{2,0},{4,6},{6,4},{8,10},{10,8},{12,14},{14,12},{1,3},{3,1},... | collective-permute-start | bytes 442376 | tf_op jit(solution)/shard_map/ppermute | solution.py:319
  20.6 14.7 %collective-permute-start.5 = (bf16[9,16,512]{2,1,0:T(8,128)(2,1)S(1)}, bf16[9,16,512]{2,1,0:T(8,128)(2,1)S(1)}, u32[]{:S(2)}, u32[]{:S(2)}) collective-permute-start(bf16[9,16,512]{2,1,0:T(8,128)(2,1)S(1)} %get-tuple-element.18), channel_id=1, source_target_pairs={{0,4},{2,6},{4,0},{6,2},{8,12},{10,14},{12,8},{14,10},{1,5},{3,7},... | collective-permute-start | bytes 442376 | tf_op jit(solution)/shard_map/ppermute | solution.py:319
  22.2 13.1 %collective-permute-start.6 = (bf16[9,16,512]{2,1,0:T(8,128)(2,1)S(1)}, bf16[9,16,512]{2,1,0:T(8,128)(2,1)S(1)}, u32[]{:S(2)}, u32[]{:S(2)}) collective-permute-start(bf16[9,16,512]{2,1,0:T(8,128)(2,1)S(1)} %get-tuple-element.19), channel_id=1, source_target_pairs={{0,6},{2,4},{4,2},{6,0},{8,14},{10,12},{12,10},{14,8},{1,7},{3,5},... | collective-permute-start | bytes 442376 | tf_op jit(solution)/shard_map/ppermute | solution.py:319
  31.1 0.7 %copy-start.2 = (bf16[9,16,512]{2,1,0:T(8,128)(2,1)}, bf16[9,16,512]{2,1,0:T(8,128)(2,1)S(1)}, u32[]{:S(2)}) copy-start(bf16[9,16,512]{2,1,0:T(8,128)(2,1)S(1)} %get-tuple-element.12.refs_0_) | copy-start | bytes 442372
  31.8 10.3 %collective-permute-start.1 = (bf16[9,16,512]{2,1,0:T(8,128)(2,1)S(1)}, bf16[9,16,512]{2,1,0:T(8,128)(2,1)S(1)}, u32[]{:S(2)}, u32[]{:S(2)}) collective-permute-start(bf16[9,16,512]{2,1,0:T(8,128)(2,1)S(1)} %get-tuple-element.13), channel_id=1, source_target_pairs={{0,2},{2,0},{4,6},{6,4},{8,10},{10,8},{12,14},{14,12},{1,3},{3,1},... | collective-permute-start | bytes 442376 | tf_op jit(solution)/shard_map/ppermute | solution.py:319
  33.7 8.4 %collective-permute-start.2 = (bf16[9,16,512]{2,1,0:T(8,128)(2,1)S(1)}, bf16[9,16,512]{2,1,0:T(8,128)(2,1)S(1)}, u32[]{:S(2)}, u32[]{:S(2)}) collective-permute-start(bf16[9,16,512]{2,1,0:T(8,128)(2,1)S(1)} %get-tuple-element.14), channel_id=1, source_target_pairs={{0,4},{2,6},{4,0},{6,2},{8,12},{10,14},{12,8},{14,10},{1,5},{3,7},... | collective-permute-start | bytes 442376 | tf_op jit(solution)/shard_map/ppermute | solution.py:319
  35.3 0.7 %copy-start.13 = (bf16[9,16,512]{2,1,0:T(8,128)(2,1)}, bf16[9,16,512]{2,1,0:T(8,128)(2,1)S(1)}, u32[]{:S(2)}) copy-start(bf16[9,16,512]{2,1,0:T(8,128)(2,1)S(1)} %collective-permute-done.4.refs_1_) | copy-start | bytes 442372
  35.3 6.8 %collective-permute-start.3 = (bf16[9,16,512]{2,1,0:T(8,128)(2,1)S(1)}, bf16[9,16,512]{2,1,0:T(8,128)(2,1)S(1)}, u32[]{:S(2)}, u32[]{:S(2)}) collective-permute-start(bf16[9,16,512]{2,1,0:T(8,128)(2,1)S(1)} %get-tuple-element.15), channel_id=1, source_target_pairs={{0,6},{2,4},{4,2},{6,0},{8,14},{10,12},{12,10},{14,8},{1,7},{3,5},... | collective-permute-start | bytes 442376 | tf_op jit(solution)/shard_map/ppermute | solution.py:319
  35.3 0.7 %copy-start.14 = (bf16[9,16,512]{2,1,0:T(8,128)(2,1)}, bf16[9,16,512]{2,1,0:T(8,128)(2,1)S(1)}, u32[]{:S(2)}) copy-start(bf16[9,16,512]{2,1,0:T(8,128)(2,1)S(1)} %collective-permute-done.5.refs_2_) | copy-start | bytes 442372
  35.3 0.7 %copy-start.15 = (bf16[9,16,512]{2,1,0:T(8,128)(2,1)}, bf16[9,16,512]{2,1,0:T(8,128)(2,1)S(1)}, u32[]{:S(2)}) copy-start(bf16[9,16,512]{2,1,0:T(8,128)(2,1)S(1)} %collective-permute-done.6.refs_3_) | copy-start | bytes 442372
  38.1 9.2 %collective-permute-start.7 = (bf16[9,16,512]{2,1,0:T(8,128)(2,1)}, bf16[9,16,512]{2,1,0:T(8,128)(2,1)S(1)}, u32[]{:S(2)}, u32[]{:S(2)}) collective-permute-start(bf16[9,16,512]{2,1,0:T(8,128)(2,1)} %merge_lists.1), channel_id=1, source_target_pairs={{0,8},{2,10},{4,12},{6,14},{8,0},{10,2},{12,4},{14,6},{1,9},{3,11}... | collective-permute-start | bytes 442376 | tf_op jit(solution)/shard_map/ppermute | solution.py:319
  42.0 5.3 %copy-start.10 = (bf16[9,16,512]{2,1,0:T(8,128)(2,1)}, bf16[9,16,512]{2,1,0:T(8,128)(2,1)S(1)}, u32[]{:S(2)}) copy-start(bf16[9,16,512]{2,1,0:T(8,128)(2,1)S(1)} %collective-permute-done.1.refs_1_) | copy-start | bytes 442372
  42.0 5.3 %copy-start.11 = (bf16[9,16,512]{2,1,0:T(8,128)(2,1)}, bf16[9,16,512]{2,1,0:T(8,128)(2,1)S(1)}, u32[]{:S(2)}) copy-start(bf16[9,16,512]{2,1,0:T(8,128)(2,1)S(1)} %collective-permute-done.2.refs_2_) | copy-start | bytes 442372
  42.1 5.2 %copy-start.12 = (bf16[9,16,512]{2,1,0:T(8,128)(2,1)}, bf16[9,16,512]{2,1,0:T(8,128)(2,1)S(1)}, u32[]{:S(2)}) copy-start(bf16[9,16,512]{2,1,0:T(8,128)(2,1)S(1)} %collective-permute-done.3.refs_3_) | copy-start | bytes 442372
  47.3 0.6 %copy-start.16 = (bf16[9,16,512]{2,1,0:T(8,128)(2,1)}, bf16[9,16,512]{2,1,0:T(8,128)(2,1)S(1)}, u32[]{:S(2)}) copy-start(bf16[9,16,512]{2,1,0:T(8,128)(2,1)S(1)} %collective-permute-done.7.refs_4_) | copy-start | bytes 442372
where the time goes:
time: 50.5 us; the launch traced here: 50.2 us
  Pallas kernels  22 us (44%)
  starting transfers between devices  11.1 us (22%)
  local copies, waits for them, and re-layouts  8.66 us (17%)
  waiting for transfers between devices  5.24 us (10%)
  other arithmetic  2.15 us (4%)
  between operations  0.81 us (2%)
    pallas_call x2, Pallas kernels, filter_block(): pl.pallas_call(body, out_shape=[jax.ShapeDtypeStruct((LISTS, TILE_ROWS, c...  17.7 us
    ppermute x8, starting transfers between devices, swapped(): return lax.ppermute(value, axis, [(i, i ^ distance) for i in range(count)])  11.1 us
    unnamed x37, local copies, waits for them, and re-layouts  7.29 us
    ppermute x8, waiting for transfers between devices, swapped(): return lax.ppermute(value, axis, [(i, i ^ distance) for i in range(count)])  5.24 us
    pallas_call x1, Pallas kernels, finish(): pl.pallas_call(functools.partial(finish_kernel, exposures_total), out_sha...  2.21 us
    pallas_call x1, Pallas kernels, merge(): pl.pallas_call(merge_kernel, out_shape=jax.ShapeDtypeStruct(parts[0].shap...  2.08 us
    dynamic_slice x1, local copies, waits for them, and re-layouts, shards(): lax.dynamic_slice_in_dim(exposures, (1 - sky_place) * (row_dev - PAD), PA...  1.03 us
  transfers between devices with their start and end apart: 8, of which 1 were waited for; matrix products, arithmetic and copies ran while one was open for 7% of the time, Pallas kernels for 22%

commit v1 on v0

v1 whole, which is shorter than its diff:
```python
import functools

import jax
import jax.numpy as jnp
from jax import lax
from jax.experimental import pallas as pl
from jax.experimental.pallas import tpu as pltpu
from jax.sharding import PartitionSpec as P

BAND_COLS = 128
TAPS = 21
REJECT = 4
MIN_VALID = 12

SENTINEL = 1e30

TILE_ROWS = 16
PAD = 16
SQUARE = 4
KERNEL_VMEM = 8 * 1024 * 1024
LISTS = 2 * REJECT + 1


def sort_pair(entries, first, second, up):
    a, b = entries[first], entries[second]
    hi, lo = jnp.maximum(a, b), jnp.minimum(a, b)
    entries[first], entries[second] = (hi, lo) if up else (lo, hi)


def sorted_four(entries, up):
    entries = list(entries)
    for first, second in ((0, 1), (2, 3), (0, 2), (1, 3), (1, 2)):
        sort_pair(entries, first, second, up)
    return entries


def merged_four(left, right, up, ordered=True):
    pick = jnp.maximum if up else jnp.minimum
    entries = [pick(left[i], right[REJECT - 1 - i]) for i in range(REJECT)]
    if ordered:
        for first, second in ((0, 2), (1, 3), (0, 1), (2, 3)):
            sort_pair(entries, first, second, up)
    return entries


def valid_sum(highs, lows):
    total = None
    for value in highs + lows:
        wide = value.astype(jnp.float32)
        wide = jnp.where(jnp.abs(wide) < 0.5 * SENTINEL, wide, 0.0)
        total = wide if total is None else total + wide
    return total


def banded_pair(line):
    offset = lax.broadcasted_iota(jnp.int32, (BAND_COLS, BAND_COLS), 1) - (
        lax.broadcasted_iota(jnp.int32, (BAND_COLS, BAND_COLS), 0)
    )
    inside = jnp.abs(offset) < BAND_COLS // 2
    banded = pltpu.roll(
        jnp.broadcast_to(line, (BAND_COLS, BAND_COLS)), 0, 1, stride=1, stride_axis=0
    )
    return jnp.where(inside, banded, 0.0), jnp.where(inside, 0.0, banded)


def block_kernel(
    slots,
    bands,
    kernels,
    exposures_total,
    rows_out,
    chunk_of,
    exposures_ref,
    halo_ref,
    slot_hbm,
    choice_hbm,
    bad_hbm,
    range_hbm,
    flux_hbm,
    vert_hbm,
    horiz_hbm,
    *rest,
):
    rows = exposures_ref.shape[1]
    chunks = rows // TILE_ROWS
    outs, count_ref, rest = rest[:chunks], rest[chunks], rest[chunks + 1 :]
    (
        pictures,
        high,
        low,
        total,
        bank_v,
        bank_h,
        taps,
        bad_vec,
        range_vec,
        slot_ref,
        choice_ref,
        bad_ref,
        range_ref,
        flux_ref,
        sems,
        halo_sem,
        table_sems,
    ) = rest
    margin = TAPS // 2
    group = 4
    pieces = slots // group
    place = lax.axis_index("expo")
    sky_place = lax.axis_index("sky")

    tables = [
        pltpu.make_async_copy(source, target, table_sems.at[i])
        for i, (source, target) in enumerate(
            (
                (vert_hbm, taps.at[0]),
                (horiz_hbm, taps.at[1]),
                (slot_hbm, slot_ref),
                (choice_hbm, choice_ref),
                (bad_hbm, bad_ref),
                (range_hbm, range_ref),
                (flux_hbm, flux_ref),
                (bad_hbm, bad_vec),
                (range_hbm, range_vec),
            )
        )
    ]
    for copy in tables:
        copy.start()

    def body_copy(piece):
        return pltpu.make_async_copy(
            exposures_ref.at[pl.ds(piece * group, group)],
            pictures.at[pl.ds(piece * group, group), pl.ds(0, rows), :],
            sems.at[piece],
        )

    spot = pl.multiple_of(rows + PAD * (1 - sky_place), TILE_ROWS)
    bare = pl.multiple_of(rows + PAD * sky_place, TILE_ROWS)
    halo_copy = pltpu.make_async_copy(halo_ref, pictures.at[:, pl.ds(spot, PAD), :], halo_sem)
    halo_copy.start()
    for piece in range(pieces):
        body_copy(piece).start()
    pictures[:, pl.ds(bare, PAD), :] = jnp.zeros((slots, PAD, pictures.shape[2]), jnp.bfloat16)
    total[...] = jnp.zeros_like(total)

    tables[0].wait()
    tables[1].wait()
    wide = ((0, 0), (0, BAND_COLS - TAPS))
    vert_lines = jnp.pad(taps[0].astype(jnp.float32), wide)
    vert_lines = pltpu.roll(vert_lines, BAND_COLS - margin, 1)
    horiz_lines = jnp.pad(taps[1].astype(jnp.float32), wide)
    horiz_lines = pltpu.roll(horiz_lines, BAND_COLS - margin, 1)
    for kernel in range(kernels):
        main, edge = banded_pair(vert_lines[kernel : kernel + 1])
        bank_v[kernel, :, :BAND_COLS] = main.astype(jnp.bfloat16)
        bank_v[kernel, :, BAND_COLS:] = pltpu.roll(edge, PAD, 1)[:, : 2 * PAD].astype(jnp.bfloat16)
        main, edge = banded_pair(horiz_lines[kernel : kernel + 1])
        bank_h[kernel, :BAND_COLS] = main.T.astype(jnp.bfloat16)
        bank_h[kernel, BAND_COLS:] = edge.T.astype(jnp.bfloat16)
    for copy in tables[2:]:
        copy.wait()

    first_out = sky_place * rows + place * rows_out
    out_row = first_out + lax.broadcasted_iota(jnp.int32, (rows_out, exposures_total), 0)
    covered = (out_row >= range_vec[0:1, :]) & (out_row < range_vec[1:2, :])
    for band in range(bands):
        both = covered & (bad_vec[band : band + 1, :] == 0)
        number = jnp.sum(both.astype(jnp.float32), axis=1, keepdims=True)
        count_ref[:, band * BAND_COLS : (band + 1) * BAND_COLS] = jnp.broadcast_to(
            number.astype(jnp.int32), (rows_out, BAND_COLS)
        )

    row_index = sky_place * rows + lax.broadcasted_iota(jnp.int32, (rows, BAND_COLS), 0)
    lane = lax.broadcasted_iota(jnp.int32, (rows, BAND_COLS), 1)
    nothing = jnp.zeros((rows, BAND_COLS), jnp.bfloat16)

    def one_slot(slot):
        ident = slot_ref[place, slot]
        k = jnp.minimum(ident, exposures_total - 1)
        begin = range_ref[0, k]
        end = jnp.where(ident < exposures_total, range_ref[1, k], 0)
        factor = flux_ref[k]
        chosen = [choice_ref[band, k] for band in range(bands)]
        columns = []
        for band in range(bands):
            picture = pictures[slot, :, band * BAND_COLS : (band + 1) * BAND_COLS]
            vertical = jnp.dot(bank_v[chosen[band]], picture, preferred_element_type=jnp.float32)
            columns.append(vertical.astype(jnp.bfloat16))
        for band in range(bands):
            before = columns[band - 1] if band else nothing
            after = columns[band + 1] if band + 1 < bands else nothing
            sides = jnp.where(lane < BAND_COLS // 2, after, before)
            filtered = jnp.dot(
                jnp.concatenate([columns[band], sides], 1),
                bank_h[chosen[band]],
                preferred_element_type=jnp.float32,
            )
            plane = (filtered * factor).astype(jnp.bfloat16).astype(jnp.float32)
            stop = jnp.where(bad_ref[band, k] == 0, end, 0)
            usable = (row_index >= begin) & (row_index < stop)
            window = pl.ds(band * BAND_COLS, BAND_COLS)
            total[:, window] += jnp.where(usable, plane, 0.0)
            high[slot, :, window] = jnp.where(usable, plane, -SENTINEL).astype(jnp.bfloat16)
            low[slot, :, window] = jnp.where(usable, plane, SENTINEL).astype(jnp.bfloat16)

    halo_copy.wait()
    for piece in range(pieces):
        body_copy(piece).wait()

        def body(step, carry):
            one_slot(piece * group + 2 * step)
            one_slot(piece * group + 2 * step + 1)
            return carry

        lax.fori_loop(0, group // 2, body, 0)

    for position, out in enumerate(outs):
        top = pl.multiple_of(chunk_of(place, position) * TILE_ROWS, TILE_ROWS)

        def tiles(step, carry):
            for part in range(2):
                window = pl.ds(
                    pl.multiple_of((2 * step + part) * BAND_COLS, BAND_COLS), BAND_COLS
                )
                sides = []
                for source, up in ((high, True), (low, False)):
                    best = None
                    for piece in range(slots // REJECT):
                        entries = [
                            source[piece * REJECT + i, pl.ds(top, TILE_ROWS), window]
                            for i in range(REJECT)
                        ]
                        entries = sorted_four(entries, up)
                        best = entries if best is None else merged_four(best, entries, up)
                    sides.append(best)
                left = total[pl.ds(top, TILE_ROWS), window] - valid_sum(*sides)
                for index, value in enumerate(sides[0] + sides[1]):
                    out[index, :, window] = value
                out[2 * REJECT, :, window] = left.astype(jnp.bfloat16)
            return carry

        lax.fori_loop(0, bands // 2, tiles, 0)


def filter_block(chunk_of, rows_out, exposures, halo, slot_ids, choice, bad, span, flux, vert, horiz):
    slots, rows, columns = exposures.shape
    kernels = vert.shape[0]
    bands = columns // BAND_COLS
    chunks = rows // TILE_ROWS
    hbm = pl.BlockSpec(memory_space=pltpu.HBM)
    vmem = pl.BlockSpec(memory_space=pltpu.VMEM)
    anywhere = pl.BlockSpec(memory_space=pl.ANY)
    body = functools.partial(
        block_kernel, slots, bands, kernels, flux.shape[0], rows_out, chunk_of
    )
    return pl.pallas_call(
        body,
        out_shape=[jax.ShapeDtypeStruct((LISTS, TILE_ROWS, columns), jnp.bfloat16)] * chunks
        + [jax.ShapeDtypeStruct((rows_out, columns), jnp.int32)],
        in_specs=[hbm, anywhere] + [hbm] * 7,
        out_specs=[vmem] * (chunks + 1),
        scratch_shapes=[
            pltpu.VMEM((slots, rows + 2 * PAD, columns), jnp.bfloat16),
            pltpu.VMEM((slots, rows, columns), jnp.bfloat16),
            pltpu.VMEM((slots, rows, columns), jnp.bfloat16),
            pltpu.VMEM((rows, columns), jnp.float32),
            pltpu.VMEM((kernels, rows, BAND_COLS + 2 * PAD), jnp.bfloat16),
            pltpu.VMEM((kernels, 2 * BAND_COLS, BAND_COLS), jnp.bfloat16),
            pltpu.VMEM((2,) + vert.shape, jnp.bfloat16),
            pltpu.VMEM(bad.shape, jnp.int32),
            pltpu.VMEM(span.shape, jnp.int32),
            pltpu.SMEM(slot_ids.shape, jnp.int32),
            pltpu.SMEM(choice.shape, jnp.int32),
            pltpu.SMEM(bad.shape, jnp.int32),
            pltpu.SMEM(span.shape, jnp.int32),
            pltpu.SMEM(flux.shape, jnp.float32),
            pltpu.SemaphoreType.DMA((slots // 4,)),
            pltpu.SemaphoreType.DMA,
            pltpu.SemaphoreType.DMA((9,)),
        ],
        compiler_params=pltpu.CompilerParams(vmem_limit_bytes=40 * 1024 * 1024),
        cost_estimate=pl.CostEstimate(
            flops=4 * slots * rows * columns * 256, bytes_accessed=8 << 20, transcendentals=0
        ),
        name="filter_block",
    )(exposures, halo, slot_ids, choice, bad, span, flux, vert, horiz)


def merged_lists(refs, window, ordered):
    sides = []
    for base, up in ((0, True), (REJECT, False)):
        lists = [[ref[base + i, :, window] for i in range(REJECT)] for ref in refs]
        while len(lists) > 1:
            keep = ordered or len(lists) > 2
            paired = [
                merged_four(lists[i], lists[i + 1], up, keep)
                for i in range(0, len(lists) - 1, 2)
            ]
            lists = paired + (lists[-1:] if len(lists) % 2 else [])
        sides.append(lists[0])
    grand = None
    for ref in refs:
        part = ref[2 * REJECT, :, window].astype(jnp.float32) + valid_sum(
            [ref[i, :, window] for i in range(REJECT)],
            [ref[REJECT + i, :, window] for i in range(REJECT)],
        )
        grand = part if grand is None else grand + part
    return sides, grand


def merge_kernel(*refs):
    *sources, out = refs
    for band in range(out.shape[-1] // BAND_COLS):
        window = pl.ds(band * BAND_COLS, BAND_COLS)
        sides, grand = merged_lists(sources, window, True)
        for index, value in enumerate(sides[0] + sides[1]):
            out[index, :, window] = value
        out[2 * REJECT, :, window] = (grand - valid_sum(*sides)).astype(jnp.bfloat16)


def merge(parts):
    vmem = pl.BlockSpec(memory_space=pltpu.VMEM)
    return pl.pallas_call(
        merge_kernel,
        out_shape=jax.ShapeDtypeStruct(parts[0].shape, jnp.bfloat16),
        in_specs=[vmem] * len(parts),
        out_specs=vmem,
        compiler_params=pltpu.CompilerParams(vmem_limit_bytes=KERNEL_VMEM),
        name="merge_lists",
    )(*parts)


def finish_kernel(exposures_total, *refs):
    *sources, count_ref, coadd_ref, rejected_ref = refs
    for band in range(coadd_ref.shape[-1] // BAND_COLS):
        window = pl.ds(band * BAND_COLS, BAND_COLS)
        sides, grand = merged_lists(sources, window, False)
        extremes = valid_sum(*sides)
        count = count_ref[:, window]
        clipped = count >= MIN_VALID
        used = jnp.where(clipped, count - 2 * REJECT, count)
        kept = jnp.where(clipped, grand - extremes, grand)
        coadd_ref[:, window] = kept / jnp.maximum(used, 1).astype(jnp.float32)
        rejected_ref[:, window] = exposures_total - used


def finish(parts, count, exposures_total):
    vmem = pl.BlockSpec(memory_space=pltpu.VMEM)
    return pl.pallas_call(
        functools.partial(finish_kernel, exposures_total),
        out_shape=[
            jax.ShapeDtypeStruct(count.shape, jnp.float32),
            jax.ShapeDtypeStruct(count.shape, jnp.int32),
        ],
        in_specs=[vmem] * (len(parts) + 1),
        out_specs=[vmem, vmem],
        compiler_params=pltpu.CompilerParams(vmem_limit_bytes=KERNEL_VMEM),
        name="finish_pixels",
    )(*parts, count)


def swapped(value, axis, distance):
    count = lax.axis_size(axis)
    return lax.ppermute(value, axis, [(i, i ^ distance) for i in range(count)])


def shards(
    exposures, slot_ids, row_range, bad_bands, kernel_choice, flux_scale, vert_taps, horiz_taps
):
    slot_count, row_dev, columns = exposures.shape
    exposures_total = flux_scale.shape[0]
    expo_size = lax.axis_size("expo")
    sky_place = lax.axis_index("sky")
    rows_out = row_dev // expo_size

    edge_rows = lax.dynamic_slice_in_dim(exposures, (1 - sky_place) * (row_dev - PAD), PAD, 1)
    halo = swapped(edge_rows, "sky", 1)

    def block(chunk_of):
        *lists, count = filter_block(
            chunk_of,
            rows_out,
            exposures,
            halo,
            slot_ids,
            kernel_choice.T,
            bad_bands.T,
            row_range.T,
            flux_scale,
            vert_taps,
            horiz_taps,
        )
        return lists, count

    if rows_out == TILE_ROWS and expo_size == 2 * SQUARE:
        lists, count = block(lambda place, i: place ^ i ^ SQUARE)
        far, near = lists[:SQUARE], lists[SQUARE:]
        far = far[:1] + [swapped(part, "expo", 1 + i) for i, part in enumerate(far[1:])]
        near = near[:1] + [swapped(part, "expo", 1 + i) for i, part in enumerate(near[1:])]
        across = swapped(merge(far), "expo", SQUARE)
        coadd_plane, rejected_count = finish(near + [across], count, exposures_total)
    else:
        lists, count = block(lambda place, i: i)
        whole = jnp.concatenate(lists, 1)
        arrived = lax.all_to_all(whole, "expo", split_axis=1, concat_axis=0, tiled=True)
        arrived = arrived.reshape(expo_size, LISTS, rows_out, columns)
        coadd_plane, rejected_count = finish(
            [arrived[i] for i in range(expo_size)], count, exposures_total
        )
    return (coadd_plane[None], rejected_count[None])


def solution(mesh):
    in_specs = (
        P(("groups", "expo"), "sky", None),
        P("groups", None),
        P("groups", None),
        P("groups", None),
        P("groups", None),
        P("groups"),
        P("groups", None),
        P("groups", None),
    )
    out_specs = (P(("groups", "sky"), "expo", None), P(("groups", "sky"), "expo", None))
    return jax.shard_map(shards, mesh=mesh, in_specs=in_specs, out_specs=out_specs, check_vma=False)
```

time: 50.5 us -> 44.1 us (0.87)
  Pallas kernels: 22 us -> 12.9 us
  starting transfers between devices: 11.1 us -> 14.2 us
  waiting for transfers between devices: 5.24 us -> 8.25 us
  other arithmetic: 2.15 us -> 0 us
  local copies, waits for them, and re-layouts: 8.66 us -> 7.68 us
    pallas_call x2 -> x1, Pallas kernels: 17.7 us -> 11.6 us  [filter_block(): pl.pallas_call(body, out_shape=[jax.ShapeDtypeStruct((LISTS, TILE_ROWS, c...]
    ppermute x8, starting transfers between devices: 11.1 us -> 14.2 us  [swapped(): return lax.ppermute(value, axis, [(i, i ^ distance) for i in range(count)])]
    ppermute x8, waiting for transfers between devices: 5.24 us -> 8.25 us  [swapped(): return lax.ppermute(value, axis, [(i, i ^ distance) for i in range(count)])]
    pallas_call x1, Pallas kernels: 2.08 us -> 0.31 us  [merge(): pl.pallas_call(merge_kernel, out_shape=jax.ShapeDtypeStruct(parts[0].shap...]
    add x2 -> x0, other arithmetic: 1.46 us -> none  [the longest x1 0.76 us: shards(): row_range[:, 0:1] + 65536 * row_range[:, 1:2]]
    pallas_call x1, Pallas kernels: 2.21 us -> 1.01 us  [finish(): pl.pallas_call(functools.partial(finish_kernel, exposures_total), out_sha...]
    convert_element_type x2 -> x0, other arithmetic: 0.68 us -> none  [the longest x1 0.68 us: usable_count(): bounds = row_range.astype(jnp.float32)]
    unnamed x37 -> x16, local copies, waits for them, and re-layouts: 7.29 us -> 6.64 us
  transfers between devices with their start and end apart: 8 -> 8, of which waited for: 1 -> 4; matrix products, arithmetic and copies ran while one was open for 7% -> 0% of each run, Pallas kernels for 22% -> 1%
where the time goes in v1:
time: 44.1 us; the launch traced here: 43.7 us
  starting transfers between devices  14.2 us (32%)
  Pallas kernels  12.9 us (29%)
  waiting for transfers between devices  8.25 us (19%)
  local copies, waits for them, and re-layouts  7.68 us (17%)
  between operations  0.66 us (1%)
    ppermute x8, starting transfers between devices, swapped(): return lax.ppermute(value, axis, [(i, i ^ distance) for i in range(count)])  14.2 us
    pallas_call x1, Pallas kernels, filter_block(): pl.pallas_call(body, out_shape=[jax.ShapeDtypeStruct((LISTS, TILE_ROWS, c...  11.6 us
    ppermute x8, waiting for transfers between devices, swapped(): return lax.ppermute(value, axis, [(i, i ^ distance) for i in range(count)])  8.25 us
    unnamed x16, local copies, waits for them, and re-layouts  6.64 us
    dynamic_slice x1, local copies, waits for them, and re-layouts, shards(): lax.dynamic_slice_in_dim(exposures, (1 - sky_place) * (row_dev - PAD), PA...  1.03 us
    pallas_call x1, Pallas kernels, finish(): pl.pallas_call(functools.partial(finish_kernel, exposures_total), out_sha...  1.01 us
  transfers between devices with their start and end apart: 8, of which 4 were waited for; matrix products, arithmetic and copies ran while one was open for 0% of the time, Pallas kernels for 1%

profile of v1, /device:TPU:0, one launch (start us, length us, event | category | flops | bytes accessed | tf_op | source)
XLA Modules:
  0.0 43.7 jit_solution(9742542951855068013)
XLA Ops:
  0.6 1.0 %constant_dynamic-slice_fusion = bf16[24,16,512]{2,1,0:T(8,128)(2,1)S(1)} fusion(bf16[24,128,512]{2,1,0:T(8,128)(2,1)} %exposures_ref.1, s32[]{:T(128)S(6)} %select_n.3), kind=kLoop, calls=%fused_computation | loop fusion | bytes 786436 | tf_op jit(solution)/shard_map/dynamic_slice | solution.py:377
  1.7 0.5 %collective-permute-start = (bf16[24,16,512]{2,1,0:T(8,128)(2,1)S(1)}, bf16[24,16,512]{2,1,0:T(8,128)(2,1)S(1)}, u32[]{:S(2)}, u32[]{:S(2)}) collective-permute-start(bf16[24,16,512]{2,1,0:T(8,128)(2,1)S(1)} %constant_dynamic-slice_fusion), channel_id=1, source_target_pairs={{0,1},{1,0},{2,3},{3,2},{4,5},{5,4},{6,7},{7,6},{8,9},{9,8},{10,11... | collective-permute-start | bytes 1179656 | tf_op jit(solution)/shard_map/ppermute | solution.py:365
  2.2 1.3 %collective-permute-done.halo_ref = bf16[24,16,512]{2,1,0:T(8,128)(2,1)S(1)} collective-permute-done((bf16[24,16,512]{2,1,0:T(8,128)(2,1)S(1)}, bf16[24,16,512]{2,1,0:T(8,128)(2,1)S(1)}, u32[]{:S(2)}, u32[]{:S(2)}) %collective-permute-start) | collective-permute-done | bytes 393248 | tf_op jit(solution)/shard_map/ppermute | solution.py:365
  3.5 0.0 copy-start
  3.5 1.9 %copy-done = bf16[24,128,512]{2,1,0:T(8,128)(2,1)S(1)} copy-done((bf16[24,128,512]{2,1,0:T(8,128)(2,1)S(1)}, bf16[24,128,512]{2,1,0:T(8,128)(2,1)}, u32[]{:S(2)}) %copy-start) | copy-done | bytes 3145752
  5.4 0.0 copy-start.1
  5.4 0.7 %copy-done.1 = s32[8,24]{1,0:T(8,128)S(1)} copy-done((s32[8,24]{1,0:T(8,128)S(1)}, s32[8,24]{1,0:T(8,128)}, u32[]{:S(2)}) %copy-start.1) | copy-done | bytes 792
  6.1 0.0 copy-start.2
  6.1 0.7 %copy-done.2 = bf16[10,21]{1,0:T(8,128)(2,1)S(1)} copy-done((bf16[10,21]{1,0:T(8,128)(2,1)S(1)}, bf16[10,21]{1,0:T(8,128)(2,1)}, u32[]{:S(2)}) %copy-start.2) | copy-done | bytes 444
  6.8 0.0 copy-start.3
  6.8 0.7 %copy-done.3 = bf16[10,21]{1,0:T(8,128)(2,1)S(1)} copy-done((bf16[10,21]{1,0:T(8,128)(2,1)S(1)}, bf16[10,21]{1,0:T(8,128)(2,1)}, u32[]{:S(2)}) %copy-start.3) | copy-done | bytes 444
  7.5 0.0 copy-start.4
  7.5 0.7 %copy-done.4 = s32[128,4]{0,1:T(4,128)S(1)} copy-done((s32[128,4]{0,1:T(4,128)S(1)}, s32[128,4]{0,1:T(4,128)}, u32[]{:S(2)}) %copy-start.4) | copy-done | bytes 2072
  8.2 0.0 copy-start.5
  8.2 0.7 %copy-done.5 = s32[128,4]{0,1:T(4,128)S(1)} copy-done((s32[128,4]{0,1:T(4,128)S(1)}, s32[128,4]{0,1:T(4,128)}, u32[]{:S(2)}) %copy-start.5) | copy-done | bytes 2072
  8.9 0.0 copy-start.6
  8.9 0.7 %copy-done.6 = s32[128,2]{0,1:T(2,128)S(1)} copy-done((s32[128,2]{0,1:T(2,128)S(1)}, s32[128,2]{0,1:T(2,128)}, u32[]{:S(2)}) %copy-start.6) | copy-done | bytes 1048
  9.5 0.0 copy-start.7
  9.5 0.7 %copy-done.7 = f32[128]{0:T(128)S(1)} copy-done((f32[128]{0:T(128)S(1)}, f32[128]{0:T(128)}, u32[]{:S(2)}) %copy-start.7) | copy-done | bytes 536
  10.2 11.6 %filter_block.1 = (bf16[9,16,512]{2,1,0:T(8,128)(2,1)S(1)}, bf16[9,16,512]{2,1,0:T(8,128)(2,1)S(1)}, bf16[9,16,512]{2,1,0:T(8,128)(2,1)S(1)}, bf16[9,16,512]{2,1...) custom-call(bf16[24,128,512]{2,1,0:T(8,128)(2,1)S(1)} %copy-done, ...), custom_call_target="tpu_custom_call" | custom-call | flops 1610612736 | bytes 8388608 | tf_op jit(solution)/shard_map/filter_block/pallas_call | solution.py:257
  21.8 3.0 %collective-permute-start.4 = (bf16[9,16,512]{2,1,0:T(8,128)(2,1)S(1)}, bf16[9,16,512]{2,1,0:T(8,128)(2,1)S(1)}, u32[]{:S(2)}, u32[]{:S(2)}) collective-permute-start(bf16[9,16,512]{2,1,0:T(8,128)(2,1)S(1)} %get-tuple-element.18), channel_id=1, source_target_pairs={{0,2},{2,0},{4,6},{6,4},{8,10},{10,8},{12,14},{14,12},{1,3},{3,1},... | collective-permute-start | bytes 442376 | tf_op jit(solution)/shard_map/ppermute | solution.py:365
  24.8 1.6 %collective-permute-start.5 = (bf16[9,16,512]{2,1,0:T(8,128)(2,1)S(1)}, bf16[9,16,512]{2,1,0:T(8,128)(2,1)S(1)}, u32[]{:S(2)}, u32[]{:S(2)}) collective-permute-start(bf16[9,16,512]{2,1,0:T(8,128)(2,1)S(1)} %get-tuple-element.19), channel_id=1, source_target_pairs={{0,4},{2,6},{4,0},{6,2},{8,12},{10,14},{12,8},{14,10},{1,5},{3,7},... | collective-permute-start | bytes 442376 | tf_op jit(solution)/shard_map/ppermute | solution.py:365
  26.4 0.0 collective-permute-start.6
  26.4 1.9 %collective-permute-start.1 = (bf16[9,16,512]{2,1,0:T(8,128)(2,1)S(1)}, bf16[9,16,512]{2,1,0:T(8,128)(2,1)S(1)}, u32[]{:S(2)}, u32[]{:S(2)}) collective-permute-start(bf16[9,16,512]{2,1,0:T(8,128)(2,1)S(1)} %get-tuple-element.14), channel_id=1, source_target_pairs={{0,2},{2,0},{4,6},{6,4},{8,10},{10,8},{12,14},{14,12},{1,3},{3,1},... | collective-permute-start | bytes 442376 | tf_op jit(solution)/shard_map/ppermute | solution.py:365
  28.3 1.6 %collective-permute-start.2 = (bf16[9,16,512]{2,1,0:T(8,128)(2,1)S(1)}, bf16[9,16,512]{2,1,0:T(8,128)(2,1)S(1)}, u32[]{:S(2)}, u32[]{:S(2)}) collective-permute-start(bf16[9,16,512]{2,1,0:T(8,128)(2,1)S(1)} %get-tuple-element.15), channel_id=1, source_target_pairs={{0,4},{2,6},{4,0},{6,2},{8,12},{10,14},{12,8},{14,10},{1,5},{3,7},... | collective-permute-start | bytes 442376 | tf_op jit(solution)/shard_map/ppermute | solution.py:365
  29.8 0.0 collective-permute-done.4.refs_1_
  29.8 2.6 %collective-permute-start.3 = (bf16[9,16,512]{2,1,0:T(8,128)(2,1)S(1)}, bf16[9,16,512]{2,1,0:T(8,128)(2,1)S(1)}, u32[]{:S(2)}, u32[]{:S(2)}) collective-permute-start(bf16[9,16,512]{2,1,0:T(8,128)(2,1)S(1)} %get-tuple-element.16), channel_id=1, source_target_pairs={{0,6},{2,4},{4,2},{6,0},{8,14},{10,12},{12,10},{14,8},{1,7},{3,5},... | collective-permute-start | bytes 442376 | tf_op jit(solution)/shard_map/ppermute | solution.py:365
  32.5 0.0 collective-permute-done.5.refs_2_
  32.5 1.6 %collective-permute-done.6.refs_3_ = bf16[9,16,512]{2,1,0:T(8,128)(2,1)S(1)} collective-permute-done((bf16[9,16,512]{2,1,0:T(8,128)(2,1)S(1)}, bf16[9,16,512]{2,1,0:T(8,128)(2,1)S(1)}, u32[]{:S(2)}, u32[]{:S(2)}) %collective-permute-start.6) | collective-permute-done | bytes 147488 | tf_op jit(solution)/shard_map/ppermute | solution.py:365
  34.1 0.3 merge_lists.1
  34.4 3.0 %collective-permute-start.7 = (bf16[9,16,512]{2,1,0:T(8,128)(2,1)S(1)}, bf16[9,16,512]{2,1,0:T(8,128)(2,1)S(1)}, u32[]{:S(2)}, u32[]{:S(2)}) collective-permute-start(bf16[9,16,512]{2,1,0:T(8,128)(2,1)S(1)} %merge_lists.1), channel_id=1, source_target_pairs={{0,8},{2,10},{4,12},{6,14},{8,0},{10,2},{12,4},{14,6},{1,9},{3,11}... | collective-permute-start | bytes 442376 | tf_op jit(solution)/shard_map/ppermute | solution.py:365
  37.4 0.0 collective-permute-done.1.refs_1_
  37.4 3.6 %collective-permute-done.2.refs_2_ = bf16[9,16,512]{2,1,0:T(8,128)(2,1)S(1)} collective-permute-done((bf16[9,16,512]{2,1,0:T(8,128)(2,1)S(1)}, bf16[9,16,512]{2,1,0:T(8,128)(2,1)S(1)}, u32[]{:S(2)}, u32[]{:S(2)}) %collective-permute-start.2) | collective-permute-done | bytes 147488 | tf_op jit(solution)/shard_map/ppermute | solution.py:365
  41.0 1.7 %collective-permute-done.3.refs_3_ = bf16[9,16,512]{2,1,0:T(8,128)(2,1)S(1)} collective-permute-done((bf16[9,16,512]{2,1,0:T(8,128)(2,1)S(1)}, bf16[9,16,512]{2,1,0:T(8,128)(2,1)S(1)}, u32[]{:S(2)}, u32[]{:S(2)}) %collective-permute-start.3) | collective-permute-done | bytes 147488 | tf_op jit(solution)/shard_map/ppermute | solution.py:365
  42.7 0.0 collective-permute-done.7.refs_4_
  42.7 1.0 %finish_pixels.1 = (f32[16,512]{1,0:T(8,128)}, s32[16,512]{1,0:T(8,128)}) custom-call(bf16[9,16,512]{2,1,0:T(8,128)(2,1)S(1)} %get-tuple-element.13.refs_0_, bf16[9,16,512]{2,1,0:T(8,128)(2,1)S(1)} %collective-permute-done.1.refs_1_, bf16[9,16,512]{2,1,0:T(8,128)(2,1)S(1)} %collective-permute-done.2.refs_2_, ...), custom_call_target="tpu_custom_call" | custom-call | tf_op jit(solution)/shard_map/finish_pixels/pallas_call | solution.py:350
Async XLA Ops:
  1.7 1.9 %collective-permute-start = (bf16[24,16,512]{2,1,0:T(8,128)(2,1)S(1)}, bf16[24,16,512]{2,1,0:T(8,128)(2,1)S(1)}, u32[]{:S(2)}, u32[]{:S(2)}) collective-permute-start(bf16[24,16,512]{2,1,0:T(8,128)(2,1)S(1)} %constant_dynamic-slice_fusion), channel_id=1, source_target_pairs={{0,1},{1,0},{2,3},{3,2},{4,5},{5,4},{6,7},{7,6},{8,9},{9,8},{10,11... | collective-permute-start | bytes 1179656 | tf_op jit(solution)/shard_map/ppermute | solution.py:365
  3.5 1.9 %copy-start = (bf16[24,128,512]{2,1,0:T(8,128)(2,1)S(1)}, bf16[24,128,512]{2,1,0:T(8,128)(2,1)}, u32[]{:S(2)}) copy-start(bf16[24,128,512]{2,1,0:T(8,128)(2,1)} %exposures_ref.1) | copy-start | bytes 9437188
  5.4 0.7 %copy-start.1 = (s32[8,24]{1,0:T(8,128)S(1)}, s32[8,24]{1,0:T(8,128)}, u32[]{:S(2)}) copy-start(s32[8,24]{1,0:T(8,128)} %slot_hbm.1) | copy-start | bytes 2308
  6.1 0.7 %copy-start.2 = (bf16[10,21]{1,0:T(8,128)(2,1)S(1)}, bf16[10,21]{1,0:T(8,128)(2,1)}, u32[]{:S(2)}) copy-start(bf16[10,21]{1,0:T(8,128)(2,1)} %vert_hbm.1) | copy-start | bytes 1264
  6.8 0.7 %copy-start.3 = (bf16[10,21]{1,0:T(8,128)(2,1)S(1)}, bf16[10,21]{1,0:T(8,128)(2,1)}, u32[]{:S(2)}) copy-start(bf16[10,21]{1,0:T(8,128)(2,1)} %horiz_hbm.1) | copy-start | bytes 1264
  7.5 0.7 %copy-start.4 = (s32[128,4]{0,1:T(4,128)S(1)}, s32[128,4]{0,1:T(4,128)}, u32[]{:S(2)}) copy-start(s32[128,4]{0,1:T(4,128)} %param.12) | copy-start | bytes 6148
  8.2 0.7 %copy-start.5 = (s32[128,4]{0,1:T(4,128)S(1)}, s32[128,4]{0,1:T(4,128)}, u32[]{:S(2)}) copy-start(s32[128,4]{0,1:T(4,128)} %param.11) | copy-start | bytes 6148
  8.9 0.7 %copy-start.6 = (s32[128,2]{0,1:T(2,128)S(1)}, s32[128,2]{0,1:T(2,128)}, u32[]{:S(2)}) copy-start(s32[128,2]{0,1:T(2,128)} %param.10) | copy-start | bytes 3076
  9.5 0.7 %copy-start.7 = (f32[128]{0:T(128)S(1)}, f32[128]{0:T(128)}, u32[]{:S(2)}) copy-start(f32[128]{0:T(128)} %flux_hbm.1) | copy-start | bytes 1540
  21.8 8.0 %collective-permute-start.4 = (bf16[9,16,512]{2,1,0:T(8,128)(2,1)S(1)}, bf16[9,16,512]{2,1,0:T(8,128)(2,1)S(1)}, u32[]{:S(2)}, u32[]{:S(2)}) collective-permute-start(bf16[9,16,512]{2,1,0:T(8,128)(2,1)S(1)} %get-tuple-element.18), channel_id=1, source_target_pairs={{0,2},{2,0},{4,6},{6,4},{8,10},{10,8},{12,14},{14,12},{1,3},{3,1},... | collective-permute-start | bytes 442376 | tf_op jit(solution)/shard_map/ppermute | solution.py:365
  24.8 7.7 %collective-permute-start.5 = (bf16[9,16,512]{2,1,0:T(8,128)(2,1)S(1)}, bf16[9,16,512]{2,1,0:T(8,128)(2,1)S(1)}, u32[]{:S(2)}, u32[]{:S(2)}) collective-permute-start(bf16[9,16,512]{2,1,0:T(8,128)(2,1)S(1)} %get-tuple-element.19), channel_id=1, source_target_pairs={{0,4},{2,6},{4,0},{6,2},{8,12},{10,14},{12,8},{14,10},{1,5},{3,7},... | collective-permute-start | bytes 442376 | tf_op jit(solution)/shard_map/ppermute | solution.py:365
  26.4 7.7 %collective-permute-start.6 = (bf16[9,16,512]{2,1,0:T(8,128)(2,1)S(1)}, bf16[9,16,512]{2,1,0:T(8,128)(2,1)S(1)}, u32[]{:S(2)}, u32[]{:S(2)}) collective-permute-start(bf16[9,16,512]{2,1,0:T(8,128)(2,1)S(1)} %get-tuple-element.20), channel_id=1, source_target_pairs={{0,6},{2,4},{4,2},{6,0},{8,14},{10,12},{12,10},{14,8},{1,7},{3,5},... | collective-permute-start | bytes 442376 | tf_op jit(solution)/shard_map/ppermute | solution.py:365
  26.4 11.0 %collective-permute-start.1 = (bf16[9,16,512]{2,1,0:T(8,128)(2,1)S(1)}, bf16[9,16,512]{2,1,0:T(8,128)(2,1)S(1)}, u32[]{:S(2)}, u32[]{:S(2)}) collective-permute-start(bf16[9,16,512]{2,1,0:T(8,128)(2,1)S(1)} %get-tuple-element.14), channel_id=1, source_target_pairs={{0,2},{2,0},{4,6},{6,4},{8,10},{10,8},{12,14},{14,12},{1,3},{3,1},... | collective-permute-start | bytes 442376 | tf_op jit(solution)/shard_map/ppermute | solution.py:365
  28.3 12.7 %collective-permute-start.2 = (bf16[9,16,512]{2,1,0:T(8,128)(2,1)S(1)}, bf16[9,16,512]{2,1,0:T(8,128)(2,1)S(1)}, u32[]{:S(2)}, u32[]{:S(2)}) collective-permute-start(bf16[9,16,512]{2,1,0:T(8,128)(2,1)S(1)} %get-tuple-element.15), channel_id=1, source_target_pairs={{0,4},{2,6},{4,0},{6,2},{8,12},{10,14},{12,8},{14,10},{1,5},{3,7},... | collective-permute-start | bytes 442376 | tf_op jit(solution)/shard_map/ppermute | solution.py:365
  29.8 12.9 %collective-permute-start.3 = (bf16[9,16,512]{2,1,0:T(8,128)(2,1)S(1)}, bf16[9,16,512]{2,1,0:T(8,128)(2,1)S(1)}, u32[]{:S(2)}, u32[]{:S(2)}) collective-permute-start(bf16[9,16,512]{2,1,0:T(8,128)(2,1)S(1)} %get-tuple-element.16), channel_id=1, source_target_pairs={{0,6},{2,4},{4,2},{6,0},{8,14},{10,12},{12,10},{14,8},{1,7},{3,5},... | collective-permute-start | bytes 442376 | tf_op jit(solution)/shard_map/ppermute | solution.py:365
  34.4 8.3 %collective-permute-start.7 = (bf16[9,16,512]{2,1,0:T(8,128)(2,1)S(1)}, bf16[9,16,512]{2,1,0:T(8,128)(2,1)S(1)}, u32[]{:S(2)}, u32[]{:S(2)}) collective-permute-start(bf16[9,16,512]{2,1,0:T(8,128)(2,1)S(1)} %merge_lists.1), channel_id=1, source_target_pairs={{0,8},{2,10},{4,12},{6,14},{8,0},{10,2},{12,4},{14,6},{1,9},{3,11}... | collective-permute-start | bytes 442376 | tf_op jit(solution)/shard_map/ppermute | solution.py:365

commit v2 on v1

--- a/solution.py
+++ b/solution.py
@@ -284,7 +284,16 @@
             flops=4 * slots * rows * columns * 256, bytes_accessed=8 << 20, transcendentals=0
         ),
         name="filter_block",
-    )(exposures, halo, slot_ids, choice, bad, span, flux, vert, horiz)
+    )(
+        *[
+            pltpu.with_memory_space_constraint(value, space)
+            for value, space in zip(
+                (exposures, halo, slot_ids, choice, bad, span, flux, vert, horiz),
+                (pltpu.HBM, pltpu.VMEM) + (pltpu.HBM,) * 7,
+                strict=True,
+            )
+        ]
+    )
 
 
 def merged_lists(refs, window, ordered):

time: 44.1 us -> 37.7 us (0.85)
  local copies, waits for them, and re-layouts: 7.68 us -> 1.03 us
    unnamed x16 -> x0, local copies, waits for them, and re-layouts: 6.64 us -> none
where the time goes in v2:
time: 37.7 us; the launch traced here: 37.5 us
  starting transfers between devices  14.2 us (38%)
  Pallas kernels  13.3 us (35%)
  waiting for transfers between devices  8.26 us (22%)
  local copies, waits for them, and re-layouts  1.03 us (3%)
  between operations  0.65 us (2%)
    ppermute x8, starting transfers between devices, swapped(): return lax.ppermute(value, axis, [(i, i ^ distance) for i in range(count)])  14.2 us
    pallas_call x1, Pallas kernels, filter_block(): pl.pallas_call(body, out_shape=[jax.ShapeDtypeStruct((LISTS, TILE_ROWS, c...  12 us
    ppermute x8, waiting for transfers between devices, swapped(): return lax.ppermute(value, axis, [(i, i ^ distance) for i in range(count)])  8.26 us
    dynamic_slice x1, local copies, waits for them, and re-layouts, shards(): lax.dynamic_slice_in_dim(exposures, (1 - sky_place) * (row_dev - PAD), PA...  1.03 us
    pallas_call x1, Pallas kernels, finish(): pl.pallas_call(functools.partial(finish_kernel, exposures_total), out_sha...  1.01 us
  transfers between devices with their start and end apart: 8, of which 4 were waited for; matrix products, arithmetic and copies ran while one was open for 0% of the time, Pallas kernels for 1%

profile of v2, /device:TPU:0, one launch (start us, length us, event | category | flops | bytes accessed | tf_op | source)
XLA Modules:
  0.0 37.5 jit_solution(16133779414737506220)
XLA Ops:
  0.6 1.0 %constant_dynamic-slice_fusion = bf16[24,16,512]{2,1,0:T(8,128)(2,1)S(1)} fusion(bf16[24,128,512]{2,1,0:T(8,128)(2,1)} %exposures_ref.1, s32[]{:T(128)S(6)} %select_n.3), kind=kLoop, calls=%fused_computation | loop fusion | bytes 786436 | tf_op jit(solution)/shard_map/dynamic_slice | solution.py:386
  1.7 0.5 %collective-permute-start = (bf16[24,16,512]{2,1,0:T(8,128)(2,1)S(1)}, bf16[24,16,512]{2,1,0:T(8,128)(2,1)S(1)}, u32[]{:S(2)}, u32[]{:S(2)}) collective-permute-start(bf16[24,16,512]{2,1,0:T(8,128)(2,1)S(1)} %constant_dynamic-slice_fusion), channel_id=1, source_target_pairs={{0,1},{1,0},{2,3},{3,2},{4,5},{5,4},{6,7},{7,6},{8,9},{9,8},{10,11... | collective-permute-start | bytes 1179656 | tf_op jit(solution)/shard_map/ppermute | solution.py:374
  2.2 1.3 %collective-permute-done.halo_ref = bf16[24,16,512]{2,1,0:T(8,128)(2,1)S(1)} collective-permute-done((bf16[24,16,512]{2,1,0:T(8,128)(2,1)S(1)}, bf16[24,16,512]{2,1,0:T(8,128)(2,1)S(1)}, u32[]{:S(2)}, u32[]{:S(2)}) %collective-permute-start) | collective-permute-done | bytes 393248 | tf_op jit(solution)/shard_map/ppermute | solution.py:374
  3.5 12.0 %filter_block.1 = (bf16[9,16,512]{2,1,0:T(8,128)(2,1)S(1)}, bf16[9,16,512]{2,1,0:T(8,128)(2,1)S(1)}, bf16[9,16,512]{2,1,0:T(8,128)(2,1)S(1)}, bf16[9,16,512]{2,1...) custom-call(bf16[24,128,512]{2,1,0:T(8,128)(2,1)} %exposures_ref.1, ...), custom_call_target="tpu_custom_call" | custom-call | flops 1610612736 | bytes 8388608 | tf_op jit(solution)/shard_map/filter_block/pallas_call | solution.py:257
  15.6 3.0 %collective-permute-start.4 = (bf16[9,16,512]{2,1,0:T(8,128)(2,1)S(1)}, bf16[9,16,512]{2,1,0:T(8,128)(2,1)S(1)}, u32[]{:S(2)}, u32[]{:S(2)}) collective-permute-start(bf16[9,16,512]{2,1,0:T(8,128)(2,1)S(1)} %get-tuple-element.18), channel_id=1, source_target_pairs={{0,2},{2,0},{4,6},{6,4},{8,10},{10,8},{12,14},{14,12},{1,3},{3,1},... | collective-permute-start | bytes 442376 | tf_op jit(solution)/shard_map/ppermute | solution.py:374
  18.5 1.6 %collective-permute-start.5 = (bf16[9,16,512]{2,1,0:T(8,128)(2,1)S(1)}, bf16[9,16,512]{2,1,0:T(8,128)(2,1)S(1)}, u32[]{:S(2)}, u32[]{:S(2)}) collective-permute-start(bf16[9,16,512]{2,1,0:T(8,128)(2,1)S(1)} %get-tuple-element.19), channel_id=1, source_target_pairs={{0,4},{2,6},{4,0},{6,2},{8,12},{10,14},{12,8},{14,10},{1,5},{3,7},... | collective-permute-start | bytes 442376 | tf_op jit(solution)/shard_map/ppermute | solution.py:374
  20.1 0.0 collective-permute-start.6
  20.1 1.9 %collective-permute-start.1 = (bf16[9,16,512]{2,1,0:T(8,128)(2,1)S(1)}, bf16[9,16,512]{2,1,0:T(8,128)(2,1)S(1)}, u32[]{:S(2)}, u32[]{:S(2)}) collective-permute-start(bf16[9,16,512]{2,1,0:T(8,128)(2,1)S(1)} %get-tuple-element.14), channel_id=1, source_target_pairs={{0,2},{2,0},{4,6},{6,4},{8,10},{10,8},{12,14},{14,12},{1,3},{3,1},... | collective-permute-start | bytes 442376 | tf_op jit(solution)/shard_map/ppermute | solution.py:374
  22.0 1.6 %collective-permute-start.2 = (bf16[9,16,512]{2,1,0:T(8,128)(2,1)S(1)}, bf16[9,16,512]{2,1,0:T(8,128)(2,1)S(1)}, u32[]{:S(2)}, u32[]{:S(2)}) collective-permute-start(bf16[9,16,512]{2,1,0:T(8,128)(2,1)S(1)} %get-tuple-element.15), channel_id=1, source_target_pairs={{0,4},{2,6},{4,0},{6,2},{8,12},{10,14},{12,8},{14,10},{1,5},{3,7},... | collective-permute-start | bytes 442376 | tf_op jit(solution)/shard_map/ppermute | solution.py:374
  23.6 0.0 collective-permute-done.4.refs_1_
  23.6 2.6 %collective-permute-start.3 = (bf16[9,16,512]{2,1,0:T(8,128)(2,1)S(1)}, bf16[9,16,512]{2,1,0:T(8,128)(2,1)S(1)}, u32[]{:S(2)}, u32[]{:S(2)}) collective-permute-start(bf16[9,16,512]{2,1,0:T(8,128)(2,1)S(1)} %get-tuple-element.16), channel_id=1, source_target_pairs={{0,6},{2,4},{4,2},{6,0},{8,14},{10,12},{12,10},{14,8},{1,7},{3,5},... | collective-permute-start | bytes 442376 | tf_op jit(solution)/shard_map/ppermute | solution.py:374
  26.2 0.0 collective-permute-done.5.refs_2_
  26.2 1.6 %collective-permute-done.6.refs_3_ = bf16[9,16,512]{2,1,0:T(8,128)(2,1)S(1)} collective-permute-done((bf16[9,16,512]{2,1,0:T(8,128)(2,1)S(1)}, bf16[9,16,512]{2,1,0:T(8,128)(2,1)S(1)}, u32[]{:S(2)}, u32[]{:S(2)}) %collective-permute-start.6) | collective-permute-done | bytes 147488 | tf_op jit(solution)/shard_map/ppermute | solution.py:374
  27.8 0.3 merge_lists.1
  28.1 3.0 %collective-permute-start.7 = (bf16[9,16,512]{2,1,0:T(8,128)(2,1)S(1)}, bf16[9,16,512]{2,1,0:T(8,128)(2,1)S(1)}, u32[]{:S(2)}, u32[]{:S(2)}) collective-permute-start(bf16[9,16,512]{2,1,0:T(8,128)(2,1)S(1)} %merge_lists.1), channel_id=1, source_target_pairs={{0,8},{2,10},{4,12},{6,14},{8,0},{10,2},{12,4},{14,6},{1,9},{3,11}... | collective-permute-start | bytes 442376 | tf_op jit(solution)/shard_map/ppermute | solution.py:374
  31.1 0.0 collective-permute-done.1.refs_1_
  31.1 3.6 %collective-permute-done.2.refs_2_ = bf16[9,16,512]{2,1,0:T(8,128)(2,1)S(1)} collective-permute-done((bf16[9,16,512]{2,1,0:T(8,128)(2,1)S(1)}, bf16[9,16,512]{2,1,0:T(8,128)(2,1)S(1)}, u32[]{:S(2)}, u32[]{:S(2)}) %collective-permute-start.2) | collective-permute-done | bytes 147488 | tf_op jit(solution)/shard_map/ppermute | solution.py:374
  34.7 1.7 %collective-permute-done.3.refs_3_ = bf16[9,16,512]{2,1,0:T(8,128)(2,1)S(1)} collective-permute-done((bf16[9,16,512]{2,1,0:T(8,128)(2,1)S(1)}, bf16[9,16,512]{2,1,0:T(8,128)(2,1)S(1)}, u32[]{:S(2)}, u32[]{:S(2)}) %collective-permute-start.3) | collective-permute-done | bytes 147488 | tf_op jit(solution)/shard_map/ppermute | solution.py:374
  36.5 0.0 collective-permute-done.7.refs_4_
  36.5 1.0 %finish_pixels.1 = (f32[16,512]{1,0:T(8,128)}, s32[16,512]{1,0:T(8,128)}) custom-call(bf16[9,16,512]{2,1,0:T(8,128)(2,1)S(1)} %get-tuple-element.13.refs_0_, bf16[9,16,512]{2,1,0:T(8,128)(2,1)S(1)} %collective-permute-done.1.refs_1_, bf16[9,16,512]{2,1,0:T(8,128)(2,1)S(1)} %collective-permute-done.2.refs_2_, ...), custom_call_target="tpu_custom_call" | custom-call | tf_op jit(solution)/shard_map/finish_pixels/pallas_call | solution.py:359
Async XLA Ops:
  1.7 1.9 %collective-permute-start = (bf16[24,16,512]{2,1,0:T(8,128)(2,1)S(1)}, bf16[24,16,512]{2,1,0:T(8,128)(2,1)S(1)}, u32[]{:S(2)}, u32[]{:S(2)}) collective-permute-start(bf16[24,16,512]{2,1,0:T(8,128)(2,1)S(1)} %constant_dynamic-slice_fusion), channel_id=1, source_target_pairs={{0,1},{1,0},{2,3},{3,2},{4,5},{5,4},{6,7},{7,6},{8,9},{9,8},{10,11... | collective-permute-start | bytes 1179656 | tf_op jit(solution)/shard_map/ppermute | solution.py:374
  15.6 8.0 %collective-permute-start.4 = (bf16[9,16,512]{2,1,0:T(8,128)(2,1)S(1)}, bf16[9,16,512]{2,1,0:T(8,128)(2,1)S(1)}, u32[]{:S(2)}, u32[]{:S(2)}) collective-permute-start(bf16[9,16,512]{2,1,0:T(8,128)(2,1)S(1)} %get-tuple-element.18), channel_id=1, source_target_pairs={{0,2},{2,0},{4,6},{6,4},{8,10},{10,8},{12,14},{14,12},{1,3},{3,1},... | collective-permute-start | bytes 442376 | tf_op jit(solution)/shard_map/ppermute | solution.py:374
  18.5 7.7 %collective-permute-start.5 = (bf16[9,16,512]{2,1,0:T(8,128)(2,1)S(1)}, bf16[9,16,512]{2,1,0:T(8,128)(2,1)S(1)}, u32[]{:S(2)}, u32[]{:S(2)}) collective-permute-start(bf16[9,16,512]{2,1,0:T(8,128)(2,1)S(1)} %get-tuple-element.19), channel_id=1, source_target_pairs={{0,4},{2,6},{4,0},{6,2},{8,12},{10,14},{12,8},{14,10},{1,5},{3,7},... | collective-permute-start | bytes 442376 | tf_op jit(solution)/shard_map/ppermute | solution.py:374
  20.1 7.7 %collective-permute-start.6 = (bf16[9,16,512]{2,1,0:T(8,128)(2,1)S(1)}, bf16[9,16,512]{2,1,0:T(8,128)(2,1)S(1)}, u32[]{:S(2)}, u32[]{:S(2)}) collective-permute-start(bf16[9,16,512]{2,1,0:T(8,128)(2,1)S(1)} %get-tuple-element.20), channel_id=1, source_target_pairs={{0,6},{2,4},{4,2},{6,0},{8,14},{10,12},{12,10},{14,8},{1,7},{3,5},... | collective-permute-start | bytes 442376 | tf_op jit(solution)/shard_map/ppermute | solution.py:374
  20.1 11.0 %collective-permute-start.1 = (bf16[9,16,512]{2,1,0:T(8,128)(2,1)S(1)}, bf16[9,16,512]{2,1,0:T(8,128)(2,1)S(1)}, u32[]{:S(2)}, u32[]{:S(2)}) collective-permute-start(bf16[9,16,512]{2,1,0:T(8,128)(2,1)S(1)} %get-tuple-element.14), channel_id=1, source_target_pairs={{0,2},{2,0},{4,6},{6,4},{8,10},{10,8},{12,14},{14,12},{1,3},{3,1},... | collective-permute-start | bytes 442376 | tf_op jit(solution)/shard_map/ppermute | solution.py:374
  22.0 12.7 %collective-permute-start.2 = (bf16[9,16,512]{2,1,0:T(8,128)(2,1)S(1)}, bf16[9,16,512]{2,1,0:T(8,128)(2,1)S(1)}, u32[]{:S(2)}, u32[]{:S(2)}) collective-permute-start(bf16[9,16,512]{2,1,0:T(8,128)(2,1)S(1)} %get-tuple-element.15), channel_id=1, source_target_pairs={{0,4},{2,6},{4,0},{6,2},{8,12},{10,14},{12,8},{14,10},{1,5},{3,7},... | collective-permute-start | bytes 442376 | tf_op jit(solution)/shard_map/ppermute | solution.py:374
  23.6 12.9 %collective-permute-start.3 = (bf16[9,16,512]{2,1,0:T(8,128)(2,1)S(1)}, bf16[9,16,512]{2,1,0:T(8,128)(2,1)S(1)}, u32[]{:S(2)}, u32[]{:S(2)}) collective-permute-start(bf16[9,16,512]{2,1,0:T(8,128)(2,1)S(1)} %get-tuple-element.16), channel_id=1, source_target_pairs={{0,6},{2,4},{4,2},{6,0},{8,14},{10,12},{12,10},{14,8},{1,7},{3,5},... | collective-permute-start | bytes 442376 | tf_op jit(solution)/shard_map/ppermute | solution.py:374
  28.1 8.3 %collective-permute-start.7 = (bf16[9,16,512]{2,1,0:T(8,128)(2,1)S(1)}, bf16[9,16,512]{2,1,0:T(8,128)(2,1)S(1)}, u32[]{:S(2)}, u32[]{:S(2)}) collective-permute-start(bf16[9,16,512]{2,1,0:T(8,128)(2,1)S(1)} %merge_lists.1), channel_id=1, source_target_pairs={{0,8},{2,10},{4,12},{6,14},{8,0},{10,2},{12,4},{14,6},{1,9},{3,11}... | collective-permute-start | bytes 442376 | tf_op jit(solution)/shard_map/ppermute | solution.py:374

commit v3 on v1

v3 whole, which is shorter than its diff:
```python
import functools

import jax
import jax.numpy as jnp
from jax import lax
from jax.experimental import pallas as pl
from jax.experimental.pallas import tpu as pltpu
from jax.sharding import PartitionSpec as P

BAND_COLS = 128
TAPS = 21
REJECT = 4
MIN_VALID = 12

SENTINEL = 1e30

TILE_ROWS = 16
PAD = 16
SQUARE = 4
KERNEL_VMEM = 8 * 1024 * 1024
LISTS = 2 * REJECT + 1


def sort_pair(entries, first, second, up):
    a, b = entries[first], entries[second]
    hi, lo = jnp.maximum(a, b), jnp.minimum(a, b)
    entries[first], entries[second] = (hi, lo) if up else (lo, hi)


def sorted_four(entries, up):
    entries = list(entries)
    for first, second in ((0, 1), (2, 3), (0, 2), (1, 3), (1, 2)):
        sort_pair(entries, first, second, up)
    return entries


def merged_four(left, right, up, ordered=True):
    pick = jnp.maximum if up else jnp.minimum
    entries = [pick(left[i], right[REJECT - 1 - i]) for i in range(REJECT)]
    if ordered:
        for first, second in ((0, 2), (1, 3), (0, 1), (2, 3)):
            sort_pair(entries, first, second, up)
    return entries


def extremes_sum(highs, lows):
    pairs = [h.astype(jnp.float32) + l.astype(jnp.float32) for h, l in zip(highs, lows, strict=True)]
    return functools.reduce(jnp.add, pairs)


def banded_pair(line):
    offset = lax.broadcasted_iota(jnp.int32, (BAND_COLS, BAND_COLS), 1) - (
        lax.broadcasted_iota(jnp.int32, (BAND_COLS, BAND_COLS), 0)
    )
    inside = jnp.abs(offset) < BAND_COLS // 2
    banded = pltpu.roll(
        jnp.broadcast_to(line, (BAND_COLS, BAND_COLS)), 0, 1, stride=1, stride_axis=0
    )
    return jnp.where(inside, banded, 0.0), jnp.where(inside, 0.0, banded)


def prepare_kernel(
    bands,
    kernels,
    rows_out,
    exposures_ref,
    slot_hbm,
    choice_hbm,
    bad_hbm,
    range_hbm,
    flux_hbm,
    vert_hbm,
    horiz_hbm,
    pictures,
    bank_v,
    bank_h,
    count_ref,
    slot_ref,
    choice_ref,
    bad_ref,
    range_ref,
    flux_ref,
    taps,
    sem,
    table_sems,
):
    rows = exposures_ref.shape[1]
    exposures_total = range_ref.shape[1]
    margin = TAPS // 2
    place = lax.axis_index("expo")
    sky_place = lax.axis_index("sky")
    tables = [
        pltpu.make_async_copy(source, target, table_sems.at[i])
        for i, (source, target) in enumerate(
            (
                (vert_hbm, taps.at[0]),
                (horiz_hbm, taps.at[1]),
                (slot_hbm, slot_ref),
                (choice_hbm, choice_ref),
                (bad_hbm, bad_ref),
                (range_hbm, range_ref),
                (flux_hbm, flux_ref),
            )
        )
    ]
    for copy in tables:
        copy.start()
    body_copy = pltpu.make_async_copy(exposures_ref, pictures, sem)
    body_copy.start()

    tables[0].wait()
    tables[1].wait()
    wide = ((0, 0), (0, BAND_COLS - TAPS))
    vert_lines = jnp.pad(taps[0].astype(jnp.float32), wide)
    vert_lines = pltpu.roll(vert_lines, BAND_COLS - margin, 1)
    horiz_lines = jnp.pad(taps[1].astype(jnp.float32), wide)
    horiz_lines = pltpu.roll(horiz_lines, BAND_COLS - margin, 1)
    turn = PAD * sky_place
    for kernel in range(kernels):
        main, edge = banded_pair(vert_lines[kernel : kernel + 1])
        bank_v[kernel, :, :BAND_COLS] = main.astype(jnp.bfloat16)
        bank_v[kernel, :, BAND_COLS:] = pltpu.roll(edge, turn, 1)[:, :PAD].astype(jnp.bfloat16)
        main, edge = banded_pair(horiz_lines[kernel : kernel + 1])
        edge = edge.T
        early = lax.broadcasted_iota(jnp.int32, edge.shape, 0) < BAND_COLS // 2
        before = jnp.where(early, 0.0, edge)
        after = jnp.where(early, edge, 0.0)
        for index, part in enumerate((before, main.T, after)):
            bank_h[kernel, index * BAND_COLS : (index + 1) * BAND_COLS] = part.astype(jnp.bfloat16)
    for copy in tables[2:]:
        copy.wait()

    first_out = sky_place * rows + place * rows_out
    out_row = first_out + lax.broadcasted_iota(jnp.int32, (rows_out, exposures_total), 0)
    covered = (out_row >= range_ref[0:1, :]) & (out_row < range_ref[1:2, :])
    for band in range(bands):
        both = covered & (bad_ref[band : band + 1, :] == 0)
        number = jnp.sum(both.astype(jnp.float32), axis=1, keepdims=True)
        count_ref[:, band * BAND_COLS : (band + 1) * BAND_COLS] = jnp.broadcast_to(
            number.astype(jnp.int32), (rows_out, BAND_COLS)
        )
    body_copy.wait()


def prepare(rows_out, exposures, slot_ids, choice, bad, span, flux, vert, horiz):
    rows, columns = exposures.shape[1:]
    kernels = vert.shape[0]
    bands = columns // BAND_COLS
    tables = [jax.ShapeDtypeStruct(t.shape, t.dtype) for t in (slot_ids, choice, bad, span, flux)]
    hbm = pl.BlockSpec(memory_space=pltpu.HBM)
    vmem = pl.BlockSpec(memory_space=pltpu.VMEM)
    return pl.pallas_call(
        functools.partial(prepare_kernel, bands, kernels, rows_out),
        out_shape=[
            jax.ShapeDtypeStruct(exposures.shape, jnp.bfloat16),
            jax.ShapeDtypeStruct((kernels, rows, BAND_COLS + PAD), jnp.bfloat16),
            jax.ShapeDtypeStruct((kernels, 3 * BAND_COLS, BAND_COLS), jnp.bfloat16),
            jax.ShapeDtypeStruct((rows_out, columns), jnp.int32),
        ]
        + tables,
        in_specs=[hbm] * 8,
        out_specs=[vmem] * 9,
        scratch_shapes=[
            pltpu.VMEM((2,) + vert.shape, jnp.bfloat16),
            pltpu.SemaphoreType.DMA,
            pltpu.SemaphoreType.DMA((7,)),
        ],
        compiler_params=pltpu.CompilerParams(vmem_limit_bytes=KERNEL_VMEM),
        cost_estimate=pl.CostEstimate(flops=1 << 20, bytes_accessed=4 << 20, transcendentals=0),
        name="prepare",
    )(
        *[
            pltpu.with_memory_space_constraint(value, pltpu.HBM)
            for value in (exposures, slot_ids, choice, bad, span, flux, vert, horiz)
        ]
    )


def select_chunk(top, high, low, total, out):
    slots, columns = high.shape[0], high.shape[2]

    def tiles(step, carry):
        for part in range(2):
            window = pl.ds(pl.multiple_of((2 * step + part) * BAND_COLS, BAND_COLS), BAND_COLS)
            sides = []
            for source, up in ((high, True), (low, False)):
                best = None
                for piece in range(slots // REJECT):
                    entries = [
                        source[piece * REJECT + i, pl.ds(top, TILE_ROWS), window]
                        for i in range(REJECT)
                    ]
                    entries = sorted_four(entries, up)
                    best = entries if best is None else merged_four(best, entries, up)
                sides.append(best)
            left = total[pl.ds(top, TILE_ROWS), window] - extremes_sum(*sides)
            for index, value in enumerate(sides[0] + sides[1]):
                out[index, :, window] = value
            out[2 * REJECT, :, window] = left.astype(jnp.bfloat16)
        return carry

    lax.fori_loop(0, columns // (2 * BAND_COLS), tiles, 0)


def filter_kernel(
    chunk_of,
    pictures,
    halo,
    bank_v,
    bank_h,
    slot_vmem,
    choice_vmem,
    bad_vmem,
    range_vmem,
    flux_vmem,
    high,
    low,
    total,
    *rest,
):
    *outs, slot_ref, choice_ref, bad_ref, range_ref, flux_ref, sems = rest
    slots, rows, columns = pictures.shape
    bands = columns // BAND_COLS
    exposures_total = range_vmem.shape[1]
    place = lax.axis_index("expo")
    sky_place = lax.axis_index("sky")
    tables = [
        pltpu.make_async_copy(source, target, sems.at[i])
        for i, (source, target) in enumerate(
            (
                (slot_vmem, slot_ref),
                (choice_vmem, choice_ref),
                (bad_vmem, bad_ref),
                (range_vmem, range_ref),
                (flux_vmem, flux_ref),
            )
        )
    ]
    for copy in tables:
        copy.start()
    total[...] = jnp.zeros_like(total)
    for copy in tables:
        copy.wait()

    row_index = sky_place * rows + lax.broadcasted_iota(jnp.int32, (rows, BAND_COLS), 0)
    lane = lax.broadcasted_iota(jnp.int32, (rows, BAND_COLS), 1)

    def one_slot(slot):
        ident = slot_ref[place, slot]
        k = jnp.minimum(ident, exposures_total - 1)
        begin = range_ref[0, k]
        end = jnp.where(ident < exposures_total, range_ref[1, k], 0)
        factor = flux_ref[k]
        chosen = [choice_ref[band, k] for band in range(bands)]
        verticals = []
        for band in range(bands):
            window = pl.ds(band * BAND_COLS, BAND_COLS)
            picture = jnp.concatenate([pictures[slot, :, window], halo[slot, :, window]], 0)
            vertical = jnp.dot(bank_v[chosen[band]], picture, preferred_element_type=jnp.float32)
            verticals.append(vertical.astype(jnp.bfloat16))
        filtered = []
        for band in range(0, bands, 2):
            pair = jnp.dot(
                jnp.concatenate(verticals[band : band + 2], 1),
                jnp.concatenate(
                    [bank_h[chosen[band], BAND_COLS:], bank_h[chosen[band + 1], : 2 * BAND_COLS]], 1
                ),
                preferred_element_type=jnp.float32,
            )
            filtered += [pair[:, :BAND_COLS], pair[:, BAND_COLS:]]
        for band in range(2, bands, 2):
            seam = jnp.dot(
                jnp.where(lane < BAND_COLS // 2, verticals[band], verticals[band - 1]),
                jnp.concatenate(
                    [
                        bank_h[chosen[band - 1], 2 * BAND_COLS :],
                        bank_h[chosen[band], :BAND_COLS],
                    ],
                    1,
                ),
                preferred_element_type=jnp.float32,
            )
            filtered[band - 1] += seam[:, :BAND_COLS]
            filtered[band] += seam[:, BAND_COLS:]
        for band in range(bands):
            plane = (filtered[band] * factor).astype(jnp.bfloat16).astype(jnp.float32)
            stop = jnp.where(bad_ref[band, k] == 0, end, 0)
            usable = (row_index >= begin) & (row_index < stop)
            window = pl.ds(band * BAND_COLS, BAND_COLS)
            total[:, window] += jnp.where(usable, plane, 0.0)
            high[slot, :, window] = jnp.where(usable, plane, -SENTINEL).astype(jnp.bfloat16)
            low[slot, :, window] = jnp.where(usable, plane, SENTINEL).astype(jnp.bfloat16)

    def body(step, carry):
        one_slot(2 * step)
        one_slot(2 * step + 1)
        return carry

    lax.fori_loop(0, slots // 2, body, 0)
    for position, out in enumerate(outs):
        top = pl.multiple_of(chunk_of(place, position) * TILE_ROWS, TILE_ROWS)
        select_chunk(top, high, low, total, out)


def filter_slots(chunk_of, chunks, pictures, halo, bank_v, bank_h, tables):
    slots, rows, columns = pictures.shape
    vmem = pl.BlockSpec(memory_space=pltpu.VMEM)
    return pl.pallas_call(
        functools.partial(filter_kernel, chunk_of),
        out_shape=[
            jax.ShapeDtypeStruct(pictures.shape, jnp.bfloat16),
            jax.ShapeDtypeStruct(pictures.shape, jnp.bfloat16),
            jax.ShapeDtypeStruct((rows, columns), jnp.float32),
        ]
        + [jax.ShapeDtypeStruct((LISTS, TILE_ROWS, columns), jnp.bfloat16)] * chunks,
        in_specs=[vmem] * (4 + len(tables)),
        out_specs=[vmem] * (3 + chunks),
        scratch_shapes=[pltpu.SMEM(table.shape, table.dtype) for table in tables]
        + [pltpu.SemaphoreType.DMA((len(tables),))],
        compiler_params=pltpu.CompilerParams(vmem_limit_bytes=KERNEL_VMEM),
        cost_estimate=pl.CostEstimate(
            flops=4 * slots * rows * columns * 256, bytes_accessed=8 << 20, transcendentals=0
        ),
        name="filter_slots",
    )(
        *[
            pltpu.with_memory_space_constraint(value, pltpu.VMEM)
            for value in (pictures, halo, bank_v, bank_h, *tables)
        ]
    )


def select_kernel(chunk_of, high, low, total, *outs):
    place = lax.axis_index("expo")
    for position, out in enumerate(outs):
        top = pl.multiple_of(chunk_of(place, position) * TILE_ROWS, TILE_ROWS)
        select_chunk(top, high, low, total, out)


def select(chunk_of, chunks, high, low, total):
    vmem = pl.BlockSpec(memory_space=pltpu.VMEM)
    return pl.pallas_call(
        functools.partial(select_kernel, chunk_of),
        out_shape=[jax.ShapeDtypeStruct((LISTS, TILE_ROWS, high.shape[2]), jnp.bfloat16)] * chunks,
        in_specs=[vmem] * 3,
        out_specs=[vmem] * chunks,
        compiler_params=pltpu.CompilerParams(vmem_limit_bytes=KERNEL_VMEM),
        cost_estimate=pl.CostEstimate(flops=1 << 24, bytes_accessed=4 << 20, transcendentals=0),
        name="select_rows",
    )(*[pltpu.with_memory_space_constraint(value, pltpu.VMEM) for value in (high, low, total)])


def merged_lists(refs, window, ordered):
    sides = []
    for base, up in ((0, True), (REJECT, False)):
        lists = [[ref[base + i, :, window] for i in range(REJECT)] for ref in refs]
        while len(lists) > 1:
            keep = ordered or len(lists) > 2
            paired = [
                merged_four(lists[i], lists[i + 1], up, keep)
                for i in range(0, len(lists) - 1, 2)
            ]
            lists = paired + (lists[-1:] if len(lists) % 2 else [])
        sides.append(lists[0])
    grand = None
    for ref in refs:
        part = ref[2 * REJECT, :, window].astype(jnp.float32) + extremes_sum(
            [ref[i, :, window] for i in range(REJECT)],
            [ref[REJECT + i, :, window] for i in range(REJECT)],
        )
        grand = part if grand is None else grand + part
    return sides, grand


def merge_kernel(*refs):
    *sources, out = refs
    for band in range(out.shape[-1] // BAND_COLS):
        window = pl.ds(band * BAND_COLS, BAND_COLS)
        sides, grand = merged_lists(sources, window, True)
        for index, value in enumerate(sides[0] + sides[1]):
            out[index, :, window] = value
        out[2 * REJECT, :, window] = (grand - extremes_sum(*sides)).astype(jnp.bfloat16)


def merge(parts):
    vmem = pl.BlockSpec(memory_space=pltpu.VMEM)
    return pl.pallas_call(
        merge_kernel,
        out_shape=jax.ShapeDtypeStruct(parts[0].shape, jnp.bfloat16),
        in_specs=[vmem] * len(parts),
        out_specs=vmem,
        compiler_params=pltpu.CompilerParams(vmem_limit_bytes=KERNEL_VMEM),
        name="merge_lists",
    )(*parts)


def finish_kernel(exposures_total, *refs):
    *sources, count_ref, coadd_ref, rejected_ref = refs
    for band in range(coadd_ref.shape[-1] // BAND_COLS):
        window = pl.ds(band * BAND_COLS, BAND_COLS)
        sides, grand = merged_lists(sources, window, False)
        extremes = extremes_sum(*sides)
        count = count_ref[:, window]
        clipped = count >= MIN_VALID
        used = jnp.where(clipped, count - 2 * REJECT, count)
        kept = jnp.where(clipped, grand - extremes, grand)
        coadd_ref[:, window] = kept / jnp.maximum(used, 1).astype(jnp.float32)
        rejected_ref[:, window] = exposures_total - used


def finish(parts, count, exposures_total):
    vmem = pl.BlockSpec(memory_space=pltpu.VMEM)
    return pl.pallas_call(
        functools.partial(finish_kernel, exposures_total),
        out_shape=[
            jax.ShapeDtypeStruct(count.shape, jnp.float32),
            jax.ShapeDtypeStruct(count.shape, jnp.int32),
        ],
        in_specs=[vmem] * (len(parts) + 1),
        out_specs=[vmem, vmem],
        compiler_params=pltpu.CompilerParams(vmem_limit_bytes=KERNEL_VMEM),
        name="finish_pixels",
    )(*parts, count)


def swapped(value, axis, distance):
    count = lax.axis_size(axis)
    return lax.ppermute(value, axis, [(i, i ^ distance) for i in range(count)])


def shards(
    exposures, slot_ids, row_range, bad_bands, kernel_choice, flux_scale, vert_taps, horiz_taps
):
    slot_count, row_dev, columns = exposures.shape
    exposures_total = flux_scale.shape[0]
    expo_size = lax.axis_size("expo")
    sky_place = lax.axis_index("sky")
    rows_out = row_dev // expo_size

    edge_rows = lax.dynamic_slice_in_dim(exposures, (1 - sky_place) * (row_dev - PAD), PAD, 1)
    halo = swapped(edge_rows, "sky", 1)

    pictures, bank_v, bank_h, count, *tables = prepare(
        rows_out,
        exposures,
        slot_ids,
        kernel_choice.T,
        bad_bands.T,
        row_range.T,
        flux_scale,
        vert_taps,
        horiz_taps,
    )

    if rows_out == TILE_ROWS and expo_size == 2 * SQUARE:
        high, low, total, *far = filter_slots(
            lambda place, i: place ^ i ^ SQUARE, SQUARE, pictures, halo, bank_v, bank_h, tables
        )
        far = far[:1] + [swapped(part, "expo", 1 + i) for i, part in enumerate(far[1:])]
        near = list(select(lambda place, i: place ^ i, SQUARE, high, low, total))
        near = near[:1] + [swapped(part, "expo", 1 + i) for i, part in enumerate(near[1:])]
        across = swapped(merge(far), "expo", SQUARE)
        coadd_plane, rejected_count = finish(near + [across], count, exposures_total)
    else:
        chunks = row_dev // TILE_ROWS
        high, low, total, *lists = filter_slots(
            lambda place, i: i, chunks, pictures, halo, bank_v, bank_h, tables
        )
        whole = jnp.concatenate(lists, 1)
        arrived = lax.all_to_all(whole, "expo", split_axis=1, concat_axis=0, tiled=True)
        arrived = arrived.reshape(expo_size, LISTS, rows_out, columns)
        coadd_plane, rejected_count = finish(
            [arrived[i] for i in range(expo_size)], count, exposures_total
        )
    return (coadd_plane[None], rejected_count[None])


def solution(mesh):
    in_specs = (
        P(("groups", "expo"), "sky", None),
        P("groups", None),
        P("groups", None),
        P("groups", None),
        P("groups", None),
        P("groups"),
        P("groups", None),
        P("groups", None),
    )
    out_specs = (P(("groups", "sky"), "expo", None), P(("groups", "sky"), "expo", None))
    return jax.shard_map(shards, mesh=mesh, in_specs=in_specs, out_specs=out_specs, check_vma=False)
```

time: 44.1 us -> 35.7 us (0.81)
  local copies, waits for them, and re-layouts: 7.68 us -> 1.03 us
  starting transfers between devices: 14.2 us -> 12.3 us
  Pallas kernels: 12.9 us -> 13.7 us
    unnamed x16 -> x0, local copies, waits for them, and re-layouts: 6.64 us -> none
    ppermute x8, starting transfers between devices: 14.2 us -> 12.3 us  [swapped(): return lax.ppermute(value, axis, [(i, i ^ distance) for i in range(count)])]
    pallas_call x1 -> x3, Pallas kernels: 11.6 us -> 12.6 us  [the longest x1 9.33 us: filter_slots(): pl.pallas_call(functools.partial(filter_kernel, chunk_of), out_shape=[jax...]
  transfers between devices with their start and end apart: 8 -> 8, of which waited for: 4 -> 3; matrix products, arithmetic and copies ran while one was open for 0% -> 0% of each run, Pallas kernels for 1% -> 10%
where the time goes in v3:
time: 35.7 us; the launch traced here: 35.5 us
  Pallas kernels  13.7 us (38%)
  starting transfers between devices  12.3 us (34%)
  waiting for transfers between devices  7.87 us (22%)
  local copies, waits for them, and re-layouts  1.03 us (3%)
  between operations  0.68 us (2%)
    ppermute x8, starting transfers between devices, swapped(): return lax.ppermute(value, axis, [(i, i ^ distance) for i in range(count)])  12.3 us
    pallas_call x1, Pallas kernels, filter_slots(): pl.pallas_call(functools.partial(filter_kernel, chunk_of), out_shape=[jax...  9.33 us
    ppermute x8, waiting for transfers between devices, swapped(): return lax.ppermute(value, axis, [(i, i ^ distance) for i in range(count)])  7.87 us
    pallas_call x1, Pallas kernels, prepare(): pl.pallas_call(functools.partial(prepare_kernel, bands, kernels, rows_out...  2.07 us
    pallas_call x1, Pallas kernels, select(): pl.pallas_call(functools.partial(select_kernel, chunk_of), out_shape=[jax...  1.2 us
    dynamic_slice x1, local copies, waits for them, and re-layouts, shards(): lax.dynamic_slice_in_dim(exposures, (1 - sky_place) * (row_dev - PAD), PA...  1.03 us
    pallas_call x1, Pallas kernels, finish(): pl.pallas_call(functools.partial(finish_kernel, exposures_total), out_sha...  0.86 us
  transfers between devices with their start and end apart: 8, of which 3 were waited for; matrix products, arithmetic and copies ran while one was open for 0% of the time, Pallas kernels for 10%

profile of v3, /device:TPU:0, one launch (start us, length us, event | category | flops | bytes accessed | tf_op | source)
XLA Modules:
  0.0 35.5 jit_solution(3293059500210756707)
XLA Ops:
  0.6 1.0 %constant_dynamic-slice_fusion = bf16[24,16,512]{2,1,0:T(8,128)(2,1)S(1)} fusion(bf16[24,128,512]{2,1,0:T(8,128)(2,1)} %exposures_ref.1, s32[]{:T(128)S(6)} %select_n.3), kind=kLoop, calls=%fused_computation | loop fusion | bytes 786436 | tf_op jit(solution)/shard_map/dynamic_slice | solution.py:440
  1.7 0.5 %collective-permute-start = (bf16[24,16,512]{2,1,0:T(8,128)(2,1)S(1)}, bf16[24,16,512]{2,1,0:T(8,128)(2,1)S(1)}, u32[]{:S(2)}, u32[]{:S(2)}) collective-permute-start(bf16[24,16,512]{2,1,0:T(8,128)(2,1)S(1)} %constant_dynamic-slice_fusion), channel_id=1, source_target_pairs={{0,1},{1,0},{2,3},{3,2},{4,5},{5,4},{6,7},{7,6},{8,9},{9,8},{10,11... | collective-permute-start | bytes 1179656 | tf_op jit(solution)/shard_map/ppermute | solution.py:428
  2.2 2.1 %prepare.1 = (bf16[24,128,512]{2,1,0:T(8,128)(2,1)S(1)}, bf16[10,128,144]{2,1,0:T(8,128)(2,1)S(1)}, bf16[10,384,128]{2,1,0:T(8,128)(2,1)S(1)}, s32[16,512]{1,0:T...) custom-call(bf16[24,128,512]{2,1,0:T(8,128)(2,1)} %exposures_ref.1, ...), custom_call_target="tpu_custom_call" | custom-call | flops 1048576 | bytes 4194304 | tf_op jit(solution)/shard_map/prepare/pallas_call | solution.py:152
  4.3 0.0 collective-permute-done.halo
  4.3 9.3 %filter_slots.1 = (bf16[24,128,512]{2,1,0:T(8,128)(2,1)S(1)}, bf16[24,128,512]{2,1,0:T(8,128)(2,1)S(1)}, f32[128,512]{1,0:T(8,128)S(1)}, bf16[9,16,512]{2,1,0:T(...) custom-call(bf16[24,128,512]{2,1,0:T(8,128)(2,1)S(1)} %get-tuple-ele, ...), custom_call_target="tpu_custom_call" | custom-call | flops 1610612736 | bytes 8388608 | tf_op jit(solution)/shard_map/filter_slots/pallas_call | solution.py:308
  13.6 2.6 %collective-permute-start.4 = (bf16[9,16,512]{2,1,0:T(8,128)(2,1)S(1)}, bf16[9,16,512]{2,1,0:T(8,128)(2,1)S(1)}, u32[]{:S(2)}, u32[]{:S(2)}) collective-permute-start(bf16[9,16,512]{2,1,0:T(8,128)(2,1)S(1)} %get-tuple-element.40), channel_id=1, source_target_pairs={{0,2},{2,0},{4,6},{6,4},{8,10},{10,8},{12,14},{14,12},{1,3},{3,1},... | collective-permute-start | bytes 442376 | tf_op jit(solution)/shard_map/ppermute | solution.py:428
  16.2 1.6 %collective-permute-start.5 = (bf16[9,16,512]{2,1,0:T(8,128)(2,1)S(1)}, bf16[9,16,512]{2,1,0:T(8,128)(2,1)S(1)}, u32[]{:S(2)}, u32[]{:S(2)}) collective-permute-start(bf16[9,16,512]{2,1,0:T(8,128)(2,1)S(1)} %get-tuple-element.41), channel_id=1, source_target_pairs={{0,4},{2,6},{4,0},{6,2},{8,12},{10,14},{12,8},{14,10},{1,5},{3,7},... | collective-permute-start | bytes 442376 | tf_op jit(solution)/shard_map/ppermute | solution.py:428
  17.8 0.0 collective-permute-start.6
  17.8 1.2 %select_rows.1 = (bf16[9,16,512]{2,1,0:T(8,128)(2,1)S(1)}, bf16[9,16,512]{2,1,0:T(8,128)(2,1)S(1)}, bf16[9,16,512]{2,1,0:T(8,128)(2,1)S(1)}, bf16[9,16,512]{2,1,0:T(8,128)(2,1)S(1)}) custom-call(bf16[24,128,512]{2,1,0:T(8,128)(2,1)S(1)} %get-tuple-element.32.high, bf16[24,128,512]{2,1,0:T(8,128)(2,1)S(1)} %get-tuple-element.33.low, ...), custom_call_target="tpu_custom_call" | custom-call | flops 16777216 | bytes 4194304 | tf_op jit(solution)/shard_map/select_rows/pallas_call | solution.py:342
  19.0 2.0 %collective-permute-start.1 = (bf16[9,16,512]{2,1,0:T(8,128)(2,1)S(1)}, bf16[9,16,512]{2,1,0:T(8,128)(2,1)S(1)}, u32[]{:S(2)}, u32[]{:S(2)}) collective-permute-start(bf16[9,16,512]{2,1,0:T(8,128)(2,1)S(1)} %get-tuple-element.36), channel_id=1, source_target_pairs={{0,2},{2,0},{4,6},{6,4},{8,10},{10,8},{12,14},{14,12},{1,3},{3,1},... | collective-permute-start | bytes 442376 | tf_op jit(solution)/shard_map/ppermute | solution.py:428
  21.0 1.6 %collective-permute-start.2 = (bf16[9,16,512]{2,1,0:T(8,128)(2,1)S(1)}, bf16[9,16,512]{2,1,0:T(8,128)(2,1)S(1)}, u32[]{:S(2)}, u32[]{:S(2)}) collective-permute-start(bf16[9,16,512]{2,1,0:T(8,128)(2,1)S(1)} %get-tuple-element.37), channel_id=1, source_target_pairs={{0,4},{2,6},{4,0},{6,2},{8,12},{10,14},{12,8},{14,10},{1,5},{3,7},... | collective-permute-start | bytes 442376 | tf_op jit(solution)/shard_map/ppermute | solution.py:428
  22.6 0.0 collective-permute-done.4.refs_1_
  22.6 0.9 %collective-permute-start.3 = (bf16[9,16,512]{2,1,0:T(8,128)(2,1)S(1)}, bf16[9,16,512]{2,1,0:T(8,128)(2,1)S(1)}, u32[]{:S(2)}, u32[]{:S(2)}) collective-permute-start(bf16[9,16,512]{2,1,0:T(8,128)(2,1)S(1)} %get-tuple-element.38), channel_id=1, source_target_pairs={{0,6},{2,4},{4,2},{6,0},{8,14},{10,12},{12,10},{14,8},{1,7},{3,5},... | collective-permute-start | bytes 442376 | tf_op jit(solution)/shard_map/ppermute | solution.py:428
  23.5 0.0 collective-permute-done.5.refs_2_
  23.5 2.1 %collective-permute-done.6.refs_3_ = bf16[9,16,512]{2,1,0:T(8,128)(2,1)S(1)} collective-permute-done((bf16[9,16,512]{2,1,0:T(8,128)(2,1)S(1)}, bf16[9,16,512]{2,1,0:T(8,128)(2,1)S(1)}, u32[]{:S(2)}, u32[]{:S(2)}) %collective-permute-start.6) | collective-permute-done | bytes 147488 | tf_op jit(solution)/shard_map/ppermute | solution.py:428
  25.6 0.2 merge_lists.1
  25.8 3.1 %collective-permute-start.7 = (bf16[9,16,512]{2,1,0:T(8,128)(2,1)S(1)}, bf16[9,16,512]{2,1,0:T(8,128)(2,1)S(1)}, u32[]{:S(2)}, u32[]{:S(2)}) collective-permute-start(bf16[9,16,512]{2,1,0:T(8,128)(2,1)S(1)} %merge_lists.1), channel_id=1, source_target_pairs={{0,8},{2,10},{4,12},{6,14},{8,0},{10,2},{12,4},{14,6},{1,9},{3,11}... | collective-permute-start | bytes 442376 | tf_op jit(solution)/shard_map/ppermute | solution.py:428
  28.9 0.0 collective-permute-done.1.refs_1_
  28.9 3.5 %collective-permute-done.2.refs_2_ = bf16[9,16,512]{2,1,0:T(8,128)(2,1)S(1)} collective-permute-done((bf16[9,16,512]{2,1,0:T(8,128)(2,1)S(1)}, bf16[9,16,512]{2,1,0:T(8,128)(2,1)S(1)}, u32[]{:S(2)}, u32[]{:S(2)}) %collective-permute-start.2) | collective-permute-done | bytes 147488 | tf_op jit(solution)/shard_map/ppermute | solution.py:428
  32.4 2.2 %collective-permute-done.3.refs_3_ = bf16[9,16,512]{2,1,0:T(8,128)(2,1)S(1)} collective-permute-done((bf16[9,16,512]{2,1,0:T(8,128)(2,1)S(1)}, bf16[9,16,512]{2,1,0:T(8,128)(2,1)S(1)}, u32[]{:S(2)}, u32[]{:S(2)}) %collective-permute-start.3) | collective-permute-done | bytes 147488 | tf_op jit(solution)/shard_map/ppermute | solution.py:428
  34.7 0.0 collective-permute-done.7.refs_4_
  34.7 0.9 %finish_pixels.1 = (f32[16,512]{1,0:T(8,128)}, s32[16,512]{1,0:T(8,128)}) custom-call(bf16[9,16,512]{2,1,0:T(8,128)(2,1)S(1)} %get-tuple-element.35.refs_0_, bf16[9,16,512]{2,1,0:T(8,128)(2,1)S(1)} %collective-permute-done.1.refs_1_, bf16[9,16,512]{2,1,0:T(8,128)(2,1)S(1)} %collective-permute-done.2.refs_2_, ...), custom_call_target="tpu_custom_call" | custom-call | tf_op jit(solution)/shard_map/finish_pixels/pallas_call | solution.py:413
Async XLA Ops:
  1.7 2.6 %collective-permute-start = (bf16[24,16,512]{2,1,0:T(8,128)(2,1)S(1)}, bf16[24,16,512]{2,1,0:T(8,128)(2,1)S(1)}, u32[]{:S(2)}, u32[]{:S(2)}) collective-permute-start(bf16[24,16,512]{2,1,0:T(8,128)(2,1)S(1)} %constant_dynamic-slice_fusion), channel_id=1, source_target_pairs={{0,1},{1,0},{2,3},{3,2},{4,5},{5,4},{6,7},{7,6},{8,9},{9,8},{10,11... | collective-permute-start | bytes 1179656 | tf_op jit(solution)/shard_map/ppermute | solution.py:428
  13.6 8.9 %collective-permute-start.4 = (bf16[9,16,512]{2,1,0:T(8,128)(2,1)S(1)}, bf16[9,16,512]{2,1,0:T(8,128)(2,1)S(1)}, u32[]{:S(2)}, u32[]{:S(2)}) collective-permute-start(bf16[9,16,512]{2,1,0:T(8,128)(2,1)S(1)} %get-tuple-element.40), channel_id=1, source_target_pairs={{0,2},{2,0},{4,6},{6,4},{8,10},{10,8},{12,14},{14,12},{1,3},{3,1},... | collective-permute-start | bytes 442376 | tf_op jit(solution)/shard_map/ppermute | solution.py:428
  16.2 7.3 %collective-permute-start.5 = (bf16[9,16,512]{2,1,0:T(8,128)(2,1)S(1)}, bf16[9,16,512]{2,1,0:T(8,128)(2,1)S(1)}, u32[]{:S(2)}, u32[]{:S(2)}) collective-permute-start(bf16[9,16,512]{2,1,0:T(8,128)(2,1)S(1)} %get-tuple-element.41), channel_id=1, source_target_pairs={{0,4},{2,6},{4,0},{6,2},{8,12},{10,14},{12,8},{14,10},{1,5},{3,7},... | collective-permute-start | bytes 442376 | tf_op jit(solution)/shard_map/ppermute | solution.py:428
  17.8 7.8 %collective-permute-start.6 = (bf16[9,16,512]{2,1,0:T(8,128)(2,1)S(1)}, bf16[9,16,512]{2,1,0:T(8,128)(2,1)S(1)}, u32[]{:S(2)}, u32[]{:S(2)}) collective-permute-start(bf16[9,16,512]{2,1,0:T(8,128)(2,1)S(1)} %get-tuple-element.42), channel_id=1, source_target_pairs={{0,6},{2,4},{4,2},{6,0},{8,14},{10,12},{12,10},{14,8},{1,7},{3,5},... | collective-permute-start | bytes 442376 | tf_op jit(solution)/shard_map/ppermute | solution.py:428
  19.0 9.9 %collective-permute-start.1 = (bf16[9,16,512]{2,1,0:T(8,128)(2,1)S(1)}, bf16[9,16,512]{2,1,0:T(8,128)(2,1)S(1)}, u32[]{:S(2)}, u32[]{:S(2)}) collective-permute-start(bf16[9,16,512]{2,1,0:T(8,128)(2,1)S(1)} %get-tuple-element.36), channel_id=1, source_target_pairs={{0,2},{2,0},{4,6},{6,4},{8,10},{10,8},{12,14},{14,12},{1,3},{3,1},... | collective-permute-start | bytes 442376 | tf_op jit(solution)/shard_map/ppermute | solution.py:428
  21.0 11.4 %collective-permute-start.2 = (bf16[9,16,512]{2,1,0:T(8,128)(2,1)S(1)}, bf16[9,16,512]{2,1,0:T(8,128)(2,1)S(1)}, u32[]{:S(2)}, u32[]{:S(2)}) collective-permute-start(bf16[9,16,512]{2,1,0:T(8,128)(2,1)S(1)} %get-tuple-element.37), channel_id=1, source_target_pairs={{0,4},{2,6},{4,0},{6,2},{8,12},{10,14},{12,8},{14,10},{1,5},{3,7},... | collective-permute-start | bytes 442376 | tf_op jit(solution)/shard_map/ppermute | solution.py:428
  22.6 12.1 %collective-permute-start.3 = (bf16[9,16,512]{2,1,0:T(8,128)(2,1)S(1)}, bf16[9,16,512]{2,1,0:T(8,128)(2,1)S(1)}, u32[]{:S(2)}, u32[]{:S(2)}) collective-permute-start(bf16[9,16,512]{2,1,0:T(8,128)(2,1)S(1)} %get-tuple-element.38), channel_id=1, source_target_pairs={{0,6},{2,4},{4,2},{6,0},{8,14},{10,12},{12,10},{14,8},{1,7},{3,5},... | collective-permute-start | bytes 442376 | tf_op jit(solution)/shard_map/ppermute | solution.py:428
  25.8 8.9 %collective-permute-start.7 = (bf16[9,16,512]{2,1,0:T(8,128)(2,1)S(1)}, bf16[9,16,512]{2,1,0:T(8,128)(2,1)S(1)}, u32[]{:S(2)}, u32[]{:S(2)}) collective-permute-start(bf16[9,16,512]{2,1,0:T(8,128)(2,1)S(1)} %merge_lists.1), channel_id=1, source_target_pairs={{0,8},{2,10},{4,12},{6,14},{8,0},{10,2},{12,4},{14,6},{1,9},{3,11}... | collective-permute-start | bytes 442376 | tf_op jit(solution)/shard_map/ppermute | solution.py:428

commit v4 on v3

--- a/solution.py
+++ b/solution.py
@@ -16,6 +16,8 @@
 
 TILE_ROWS = 16
 PAD = 16
+STRIDE = 8
+FAR_PARTS = 2
 SQUARE = 4
 KERNEL_VMEM = 8 * 1024 * 1024
 LISTS = 2 * REJECT + 1
@@ -176,34 +178,39 @@
     )
 
 
-def select_chunk(top, high, low, total, out):
-    slots, columns = high.shape[0], high.shape[2]
-
-    def tiles(step, carry):
-        for part in range(2):
-            window = pl.ds(pl.multiple_of((2 * step + part) * BAND_COLS, BAND_COLS), BAND_COLS)
-            sides = []
-            for source, up in ((high, True), (low, False)):
-                best = None
-                for piece in range(slots // REJECT):
-                    entries = [
-                        source[piece * REJECT + i, pl.ds(top, TILE_ROWS), window]
-                        for i in range(REJECT)
-                    ]
-                    entries = sorted_four(entries, up)
-                    best = entries if best is None else merged_four(best, entries, up)
-                sides.append(best)
-            left = total[pl.ds(top, TILE_ROWS), window] - extremes_sum(*sides)
-            for index, value in enumerate(sides[0] + sides[1]):
-                out[index, :, window] = value
-            out[2 * REJECT, :, window] = left.astype(jnp.bfloat16)
-        return carry
-
-    lax.fori_loop(0, columns // (2 * BAND_COLS), tiles, 0)
+def select_chunk(top, high, low, total, outs):
+    slots, _, columns = high.shape
+    windows = [pl.ds(start, BAND_COLS) for start in range(0, columns, BAND_COLS)]
+    streams = [(w, source, up) for w in windows for source, up in ((high, True), (low, False))]
+    best = [None] * len(streams)
+    for piece in range(slots // REJECT):
+        for n, (window, source, up) in enumerate(streams):
+            entries = [
+                source[piece * REJECT + i, pl.ds(top, TILE_ROWS), window] for i in range(REJECT)
+            ]
+            entries = sorted_four(entries, up)
+            best[n] = entries if best[n] is None else merged_four(best[n], entries, up)
+    bands_each = len(windows) // len(outs)
+    for n, window in enumerate(windows):
+        sides = best[2 * n : 2 * n + 2]
+        left = total[pl.ds(top, TILE_ROWS), window] - extremes_sum(*sides)
+        out = outs[n // bands_each]
+        place = pl.ds((n % bands_each) * BAND_COLS, BAND_COLS)
+        for index, value in enumerate(sides[0] + sides[1]):
+            out[index, :, place] = value
+        out[2 * REJECT, :, place] = left.astype(jnp.bfloat16)
+
+
+def select_chunks(chunk_of, parts, high, low, total, outs):
+    place = lax.axis_index("expo")
+    for position in range(len(outs) // parts):
+        top = pl.multiple_of(chunk_of(place, position) * TILE_ROWS, TILE_ROWS)
+        select_chunk(top, high, low, total, outs[position * parts : (position + 1) * parts])
 
 
 def filter_kernel(
     chunk_of,
+    parts,
     pictures,
     halo,
     bank_v,
@@ -242,10 +249,13 @@
     for copy in tables:
         copy.wait()
 
-    row_index = sky_place * rows + lax.broadcasted_iota(jnp.int32, (rows, BAND_COLS), 0)
+    row_index = lax.broadcasted_iota(jnp.int32, (rows, BAND_COLS), 0)
+    row_index = (row_index + sky_place * rows).astype(jnp.float32).astype(jnp.bfloat16)
+    zero = jnp.zeros((), jnp.bfloat16)
+    sentinel = jnp.asarray(SENTINEL, jnp.bfloat16)
     lane = lax.broadcasted_iota(jnp.int32, (rows, BAND_COLS), 1)
 
-    def one_slot(slot):
+    def first_pass(slot):
         ident = slot_ref[place, slot]
         k = jnp.minimum(ident, exposures_total - 1)
         begin = range_ref[0, k]
@@ -258,6 +268,9 @@
             picture = jnp.concatenate([pictures[slot, :, window], halo[slot, :, window]], 0)
             vertical = jnp.dot(bank_v[chosen[band]], picture, preferred_element_type=jnp.float32)
             verticals.append(vertical.astype(jnp.bfloat16))
+        return k, factor, chosen, begin, end, verticals
+
+    def second_pass(slot, k, factor, chosen, begin, end, verticals):
         filtered = []
         for band in range(0, bands, 2):
             pair = jnp.dot(
@@ -282,39 +295,42 @@
             )
             filtered[band - 1] += seam[:, :BAND_COLS]
             filtered[band] += seam[:, BAND_COLS:]
+        first_row = begin.astype(jnp.float32).astype(jnp.bfloat16)
         for band in range(bands):
-            plane = (filtered[band] * factor).astype(jnp.bfloat16).astype(jnp.float32)
-            stop = jnp.where(bad_ref[band, k] == 0, end, 0)
-            usable = (row_index >= begin) & (row_index < stop)
+            plane = (filtered[band] * factor).astype(jnp.bfloat16)
+            stop = jnp.where(bad_ref[band, k] == 0, end, 0).astype(jnp.float32)
+            usable = (row_index >= first_row) & (row_index < stop.astype(jnp.bfloat16))
             window = pl.ds(band * BAND_COLS, BAND_COLS)
-            total[:, window] += jnp.where(usable, plane, 0.0)
-            high[slot, :, window] = jnp.where(usable, plane, -SENTINEL).astype(jnp.bfloat16)
-            low[slot, :, window] = jnp.where(usable, plane, SENTINEL).astype(jnp.bfloat16)
+            total[:, window] += jnp.where(usable, plane, zero).astype(jnp.float32)
+            high[slot, :, window] = jnp.where(usable, plane, -sentinel)
+            low[slot, :, window] = jnp.where(usable, plane, sentinel)
 
     def body(step, carry):
-        one_slot(2 * step)
-        one_slot(2 * step + 1)
+        held = first_pass(STRIDE * step)
+        for i in range(STRIDE):
+            ahead = first_pass(STRIDE * step + i + 1) if i + 1 < STRIDE else None
+            second_pass(STRIDE * step + i, *held)
+            held = ahead
         return carry
 
-    lax.fori_loop(0, slots // 2, body, 0)
-    for position, out in enumerate(outs):
-        top = pl.multiple_of(chunk_of(place, position) * TILE_ROWS, TILE_ROWS)
-        select_chunk(top, high, low, total, out)
-
-
-def filter_slots(chunk_of, chunks, pictures, halo, bank_v, bank_h, tables):
+    lax.fori_loop(0, slots // STRIDE, body, 0)
+    select_chunks(chunk_of, parts, high, low, total, outs)
+
+
+def filter_slots(chunk_of, chunks, parts, pictures, halo, bank_v, bank_h, tables):
     slots, rows, columns = pictures.shape
     vmem = pl.BlockSpec(memory_space=pltpu.VMEM)
     return pl.pallas_call(
-        functools.partial(filter_kernel, chunk_of),
+        functools.partial(filter_kernel, chunk_of, parts),
         out_shape=[
             jax.ShapeDtypeStruct(pictures.shape, jnp.bfloat16),
             jax.ShapeDtypeStruct(pictures.shape, jnp.bfloat16),
             jax.ShapeDtypeStruct((rows, columns), jnp.float32),
         ]
-        + [jax.ShapeDtypeStruct((LISTS, TILE_ROWS, columns), jnp.bfloat16)] * chunks,
+        + [jax.ShapeDtypeStruct((LISTS, TILE_ROWS, columns // parts), jnp.bfloat16)]
+        * (chunks * parts),
         in_specs=[vmem] * (4 + len(tables)),
-        out_specs=[vmem] * (3 + chunks),
+        out_specs=[vmem] * (3 + chunks * parts),
         scratch_shapes=[pltpu.SMEM(table.shape, table.dtype) for table in tables]
         + [pltpu.SemaphoreType.DMA((len(tables),))],
         compiler_params=pltpu.CompilerParams(vmem_limit_bytes=KERNEL_VMEM),
@@ -330,30 +346,30 @@
     )
 
 
-def select_kernel(chunk_of, high, low, total, *outs):
-    place = lax.axis_index("expo")
-    for position, out in enumerate(outs):
-        top = pl.multiple_of(chunk_of(place, position) * TILE_ROWS, TILE_ROWS)
-        select_chunk(top, high, low, total, out)
-
-
-def select(chunk_of, chunks, high, low, total):
+def select_kernel(chunk_of, parts, high, low, total, *outs):
+    select_chunks(chunk_of, parts, high, low, total, outs)
+
+
+def select(chunk_of, chunks, parts, high, low, total):
     vmem = pl.BlockSpec(memory_space=pltpu.VMEM)
     return pl.pallas_call(
-        functools.partial(select_kernel, chunk_of),
-        out_shape=[jax.ShapeDtypeStruct((LISTS, TILE_ROWS, high.shape[2]), jnp.bfloat16)] * chunks,
+        functools.partial(select_kernel, chunk_of, parts),
+        out_shape=[
+            jax.ShapeDtypeStruct((LISTS, TILE_ROWS, high.shape[2] // parts), jnp.bfloat16)
+        ]
+        * (chunks * parts),
         in_specs=[vmem] * 3,
-        out_specs=[vmem] * chunks,
+        out_specs=[vmem] * (chunks * parts),
         compiler_params=pltpu.CompilerParams(vmem_limit_bytes=KERNEL_VMEM),
         cost_estimate=pl.CostEstimate(flops=1 << 24, bytes_accessed=4 << 20, transcendentals=0),
         name="select_rows",
     )(*[pltpu.with_memory_space_constraint(value, pltpu.VMEM) for value in (high, low, total)])
 
 
-def merged_lists(refs, window, ordered):
+def merged_lists(sources, ordered):
     sides = []
     for base, up in ((0, True), (REJECT, False)):
-        lists = [[ref[base + i, :, window] for i in range(REJECT)] for ref in refs]
+        lists = [[ref[base + i, :, window] for i in range(REJECT)] for ref, window in sources]
         while len(lists) > 1:
             keep = ordered or len(lists) > 2
             paired = [
@@ -363,7 +379,7 @@
             lists = paired + (lists[-1:] if len(lists) % 2 else [])
         sides.append(lists[0])
     grand = None
-    for ref in refs:
+    for ref, window in sources:
         part = ref[2 * REJECT, :, window].astype(jnp.float32) + extremes_sum(
             [ref[i, :, window] for i in range(REJECT)],
             [ref[REJECT + i, :, window] for i in range(REJECT)],
@@ -376,7 +392,7 @@
     *sources, out = refs
     for band in range(out.shape[-1] // BAND_COLS):
         window = pl.ds(band * BAND_COLS, BAND_COLS)
-        sides, grand = merged_lists(sources, window, True)
+        sides, grand = merged_lists([(ref, window) for ref in sources], True)
         for index, value in enumerate(sides[0] + sides[1]):
             out[index, :, window] = value
         out[2 * REJECT, :, window] = (grand - extremes_sum(*sides)).astype(jnp.bfloat16)
@@ -394,11 +410,17 @@
     )(*parts)
 
 
-def finish_kernel(exposures_total, *refs):
+def finish_kernel(exposures_total, whole, *refs):
     *sources, count_ref, coadd_ref, rejected_ref = refs
+    whole, parts = sources[:whole], sources[whole:]
     for band in range(coadd_ref.shape[-1] // BAND_COLS):
         window = pl.ds(band * BAND_COLS, BAND_COLS)
-        sides, grand = merged_lists(sources, window, False)
+        here = [(ref, window) for ref in whole]
+        for index, ref in enumerate(parts):
+            first, held = index * ref.shape[-1], ref.shape[-1]
+            if first <= band * BAND_COLS < first + held:
+                here.append((ref, pl.ds(band * BAND_COLS - first, BAND_COLS)))
+        sides, grand = merged_lists(here, False)
         extremes = extremes_sum(*sides)
         count = count_ref[:, window]
         clipped = count >= MIN_VALID
@@ -408,19 +430,19 @@
         rejected_ref[:, window] = exposures_total - used
 
 
-def finish(parts, count, exposures_total):
+def finish(whole, parts, count, exposures_total):
     vmem = pl.BlockSpec(memory_space=pltpu.VMEM)
     return pl.pallas_call(
-        functools.partial(finish_kernel, exposures_total),
+        functools.partial(finish_kernel, exposures_total, len(whole)),
         out_shape=[
             jax.ShapeDtypeStruct(count.shape, jnp.float32),
             jax.ShapeDtypeStruct(count.shape, jnp.int32),
         ],
-        in_specs=[vmem] * (len(parts) + 1),
+        in_specs=[vmem] * (len(whole) + len(parts) + 1),
         out_specs=[vmem, vmem],
         compiler_params=pltpu.CompilerParams(vmem_limit_bytes=KERNEL_VMEM),
         name="finish_pixels",
-    )(*parts, count)
+    )(*whole, *parts, count)
 
 
 def swapped(value, axis, distance):
@@ -454,23 +476,33 @@
 
     if rows_out == TILE_ROWS and expo_size == 2 * SQUARE:
         high, low, total, *far = filter_slots(
-            lambda place, i: place ^ i ^ SQUARE, SQUARE, pictures, halo, bank_v, bank_h, tables
-        )
-        far = far[:1] + [swapped(part, "expo", 1 + i) for i, part in enumerate(far[1:])]
-        near = list(select(lambda place, i: place ^ i, SQUARE, high, low, total))
+            lambda place, i: place ^ i ^ SQUARE,
+            SQUARE,
+            FAR_PARTS,
+            pictures,
+            halo,
+            bank_v,
+            bank_h,
+            tables,
+        )
+        across = []
+        for part in range(FAR_PARTS):
+            own, *sent = far[part::FAR_PARTS]
+            got = [swapped(sent[i], "expo", 1 + i) for i in reversed(range(SQUARE - 1))]
+            across.append(swapped(merge([own] + got), "expo", SQUARE))
+        near = list(select(lambda place, i: place ^ i, SQUARE, 1, high, low, total))
         near = near[:1] + [swapped(part, "expo", 1 + i) for i, part in enumerate(near[1:])]
-        across = swapped(merge(far), "expo", SQUARE)
-        coadd_plane, rejected_count = finish(near + [across], count, exposures_total)
+        coadd_plane, rejected_count = finish(near, across, count, exposures_total)
     else:
         chunks = row_dev // TILE_ROWS
         high, low, total, *lists = filter_slots(
-            lambda place, i: i, chunks, pictures, halo, bank_v, bank_h, tables
+            lambda place, i: i, chunks, 1, pictures, halo, bank_v, bank_h, tables
         )
         whole = jnp.concatenate(lists, 1)
         arrived = lax.all_to_all(whole, "expo", split_axis=1, concat_axis=0, tiled=True)
         arrived = arrived.reshape(expo_size, LISTS, rows_out, columns)
         coadd_plane, rejected_count = finish(
-            [arrived[i] for i in range(expo_size)], count, exposures_total
+            [arrived[i] for i in range(expo_size)], [], count, exposures_total
         )
     return (coadd_plane[None], rejected_count[None])
 

time: 35.7 us -> 32.5 us (0.910)
  Pallas kernels: 13.7 us -> 9.89 us
  starting transfers between devices: 12.3 us -> 15.7 us
  waiting for transfers between devices: 7.87 us -> 5.07 us
    pallas_call x3, Pallas kernels: 11.4 us -> 7.61 us  [the longest x1 5.65 us: filter_slots(): pl.pallas_call(functools.partial(filter_kernel, chunk_of, parts), out_sha...]
    ppermute x8 -> x12, starting transfers between devices: 12.3 us -> 15.7 us  [swapped(): return lax.ppermute(value, axis, [(i, i ^ distance) for i in range(count)])]
    ppermute x8 -> x12, waiting for transfers between devices: 7.87 us -> 5.07 us  [swapped(): return lax.ppermute(value, axis, [(i, i ^ distance) for i in range(count)])]
  transfers between devices with their start and end apart: 8 -> 12, of which waited for: 3 -> 2; matrix products, arithmetic and copies ran while one was open for 0% -> 0% of each run, Pallas kernels for 10% -> 10%
where the time goes in v4:
time: 32.5 us; the launch traced here: 32.4 us
  starting transfers between devices  15.7 us (48%)
  Pallas kernels  9.89 us (30%)
  waiting for transfers between devices  5.07 us (16%)
  local copies, waits for them, and re-layouts  1.03 us (3%)
  between operations  0.69 us (2%)
    ppermute x12, starting transfers between devices, swapped(): return lax.ppermute(value, axis, [(i, i ^ distance) for i in range(count)])  15.7 us
    pallas_call x1, Pallas kernels, filter_slots(): pl.pallas_call(functools.partial(filter_kernel, chunk_of, parts), out_sha...  5.65 us
    ppermute x12, waiting for transfers between devices, swapped(): return lax.ppermute(value, axis, [(i, i ^ distance) for i in range(count)])  5.07 us
    pallas_call x1, Pallas kernels, prepare(): pl.pallas_call(functools.partial(prepare_kernel, bands, kernels, rows_out...  2.07 us
    pallas_call x1, Pallas kernels, select(): pl.pallas_call(functools.partial(select_kernel, chunk_of, parts), out_sha...  1.1 us
    dynamic_slice x1, local copies, waits for them, and re-layouts, shards(): lax.dynamic_slice_in_dim(exposures, (1 - sky_place) * (row_dev - PAD), PA...  1.03 us
    pallas_call x1, Pallas kernels, finish(): pl.pallas_call(functools.partial(finish_kernel, exposures_total, len(whol...  0.86 us
  transfers between devices with their start and end apart: 12, of which 2 were waited for; matrix products, arithmetic and copies ran while one was open for 0% of the time, Pallas kernels for 10%

profile of v4, /device:TPU:0, one launch (start us, length us, event | category | flops | bytes accessed | tf_op | source)
XLA Modules:
  0.0 32.4 jit_solution(6078036161495392608)
XLA Ops:
  0.6 1.0 %constant_dynamic-slice_fusion = bf16[24,16,512]{2,1,0:T(8,128)(2,1)S(1)} fusion(bf16[24,128,512]{2,1,0:T(8,128)(2,1)} %exposures_ref.1, s32[]{:T(128)S(6)} %select_n.3), kind=kLoop, calls=%fused_computation | loop fusion | bytes 786436 | tf_op jit(solution)/shard_map/dynamic_slice | solution.py:462
  1.7 0.5 %collective-permute-start = (bf16[24,16,512]{2,1,0:T(8,128)(2,1)S(1)}, bf16[24,16,512]{2,1,0:T(8,128)(2,1)S(1)}, u32[]{:S(2)}, u32[]{:S(2)}) collective-permute-start(bf16[24,16,512]{2,1,0:T(8,128)(2,1)S(1)} %constant_dynamic-slice_fusion), channel_id=1, source_target_pairs={{0,1},{1,0},{2,3},{3,2},{4,5},{5,4},{6,7},{7,6},{8,9},{9,8},{10,11... | collective-permute-start | bytes 1179656 | tf_op jit(solution)/shard_map/ppermute | solution.py:450
  2.2 2.1 %prepare.1 = (bf16[24,128,512]{2,1,0:T(8,128)(2,1)S(1)}, bf16[10,128,144]{2,1,0:T(8,128)(2,1)S(1)}, bf16[10,384,128]{2,1,0:T(8,128)(2,1)S(1)}, s32[16,512]{1,0:T...) custom-call(bf16[24,128,512]{2,1,0:T(8,128)(2,1)} %exposures_ref.1, ...), custom_call_target="tpu_custom_call" | custom-call | flops 1048576 | bytes 4194304 | tf_op jit(solution)/shard_map/prepare/pallas_call | solution.py:154
  4.3 0.0 collective-permute-done.halo
  4.3 5.7 %filter_slots.1 = (bf16[24,128,512]{2,1,0:T(8,128)(2,1)S(1)}, bf16[24,128,512]{2,1,0:T(8,128)(2,1)S(1)}, f32[128,512]{1,0:T(8,128)S(1)}, bf16[9,16,256]{2,1,0:T(...) custom-call(bf16[24,128,512]{2,1,0:T(8,128)(2,1)S(1)} %get-tuple-ele, ...), custom_call_target="tpu_custom_call" | custom-call | flops 1610612736 | bytes 8388608 | tf_op jit(solution)/shard_map/filter_slots/pallas_call | solution.py:323
  9.9 3.6 %collective-permute-start.4 = (bf16[9,16,256]{2,1,0:T(8,128)(2,1)S(1)}, bf16[9,16,256]{2,1,0:T(8,128)(2,1)S(1)}, u32[]{:S(2)}, u32[]{:S(2)}) collective-permute-start(bf16[9,16,256]{2,1,0:T(8,128)(2,1)S(1)} %get-tuple-element.44), channel_id=1, source_target_pairs={{0,6},{2,4},{4,2},{6,0},{8,14},{10,12},{12,10},{14,8},{1,7},{3,5},... | collective-permute-start | bytes 221192 | tf_op jit(solution)/shard_map/ppermute | solution.py:450
  13.5 0.5 %collective-permute-start.5 = (bf16[9,16,256]{2,1,0:T(8,128)(2,1)S(1)}, bf16[9,16,256]{2,1,0:T(8,128)(2,1)S(1)}, u32[]{:S(2)}, u32[]{:S(2)}) collective-permute-start(bf16[9,16,256]{2,1,0:T(8,128)(2,1)S(1)} %get-tuple-element.45), channel_id=1, source_target_pairs={{0,4},{2,6},{4,0},{6,2},{8,12},{10,14},{12,8},{14,10},{1,5},{3,7},... | collective-permute-start | bytes 221192 | tf_op jit(solution)/shard_map/ppermute | solution.py:450
  14.0 0.2 collective-permute-start.6
  14.2 2.8 %collective-permute-start.8 = (bf16[9,16,256]{2,1,0:T(8,128)(2,1)S(1)}, bf16[9,16,256]{2,1,0:T(8,128)(2,1)S(1)}, u32[]{:S(2)}, u32[]{:S(2)}) collective-permute-start(bf16[9,16,256]{2,1,0:T(8,128)(2,1)S(1)} %get-tuple-element.48), channel_id=1, source_target_pairs={{0,6},{2,4},{4,2},{6,0},{8,14},{10,12},{12,10},{14,8},{1,7},{3,5},... | collective-permute-start | bytes 221192 | tf_op jit(solution)/shard_map/ppermute | solution.py:450
  17.0 0.5 %collective-permute-start.9 = (bf16[9,16,256]{2,1,0:T(8,128)(2,1)S(1)}, bf16[9,16,256]{2,1,0:T(8,128)(2,1)S(1)}, u32[]{:S(2)}, u32[]{:S(2)}) collective-permute-start(bf16[9,16,256]{2,1,0:T(8,128)(2,1)S(1)} %get-tuple-element.49), channel_id=1, source_target_pairs={{0,4},{2,6},{4,0},{6,2},{8,12},{10,14},{12,8},{14,10},{1,5},{3,7},... | collective-permute-start | bytes 221192 | tf_op jit(solution)/shard_map/ppermute | solution.py:450
  17.5 1.1 %select_rows.1 = (bf16[9,16,512]{2,1,0:T(8,128)(2,1)S(1)}, bf16[9,16,512]{2,1,0:T(8,128)(2,1)S(1)}, bf16[9,16,512]{2,1,0:T(8,128)(2,1)S(1)}, bf16[9,16,512]{2,1,0:T(8,128)(2,1)S(1)}) custom-call(bf16[24,128,512]{2,1,0:T(8,128)(2,1)S(1)} %get-tuple-element.36.high, bf16[24,128,512]{2,1,0:T(8,128)(2,1)S(1)} %get-tuple-element.37.low, ...), custom_call_target="tpu_custom_call" | custom-call | flops 16777216 | bytes 4194304 | tf_op jit(solution)/shard_map/select_rows/pallas_call | solution.py:355
  18.6 0.0 collective-permute-done.4.refs_1_
  18.6 0.3 collective-permute-start.10
  18.9 0.0 collective-permute-done.5.refs_2_
  18.9 1.8 %collective-permute-start.1 = (bf16[9,16,512]{2,1,0:T(8,128)(2,1)S(1)}, bf16[9,16,512]{2,1,0:T(8,128)(2,1)S(1)}, u32[]{:S(2)}, u32[]{:S(2)}) collective-permute-start(bf16[9,16,512]{2,1,0:T(8,128)(2,1)S(1)} %get-tuple-element.40), channel_id=1, source_target_pairs={{0,2},{2,0},{4,6},{6,4},{8,10},{10,8},{12,14},{14,12},{1,3},{3,1},... | collective-permute-start | bytes 442376 | tf_op jit(solution)/shard_map/ppermute | solution.py:450
  20.7 0.0 collective-permute-done.6.refs_3_
  20.7 1.6 %collective-permute-start.2 = (bf16[9,16,512]{2,1,0:T(8,128)(2,1)S(1)}, bf16[9,16,512]{2,1,0:T(8,128)(2,1)S(1)}, u32[]{:S(2)}, u32[]{:S(2)}) collective-permute-start(bf16[9,16,512]{2,1,0:T(8,128)(2,1)S(1)} %get-tuple-element.41), channel_id=1, source_target_pairs={{0,4},{2,6},{4,0},{6,2},{8,12},{10,14},{12,8},{14,10},{1,5},{3,7},... | collective-permute-start | bytes 442376 | tf_op jit(solution)/shard_map/ppermute | solution.py:450
  22.3 0.0 collective-permute-done.8.refs_1_
  22.3 0.9 %collective-permute-start.3 = (bf16[9,16,512]{2,1,0:T(8,128)(2,1)S(1)}, bf16[9,16,512]{2,1,0:T(8,128)(2,1)S(1)}, u32[]{:S(2)}, u32[]{:S(2)}) collective-permute-start(bf16[9,16,512]{2,1,0:T(8,128)(2,1)S(1)} %get-tuple-element.42), channel_id=1, source_target_pairs={{0,6},{2,4},{4,2},{6,0},{8,14},{10,12},{12,10},{14,8},{1,7},{3,5},... | collective-permute-start | bytes 442376 | tf_op jit(solution)/shard_map/ppermute | solution.py:450
  23.2 0.1 merge_lists.2
  23.3 0.0 collective-permute-done.9.refs_2_
  23.3 2.7 %collective-permute-start.7 = (bf16[9,16,256]{2,1,0:T(8,128)(2,1)S(1)}, bf16[9,16,256]{2,1,0:T(8,128)(2,1)S(1)}, u32[]{:S(2)}, u32[]{:S(2)}) collective-permute-start(bf16[9,16,256]{2,1,0:T(8,128)(2,1)S(1)} %merge_lists.2), channel_id=1, source_target_pairs={{0,8},{2,10},{4,12},{6,14},{8,0},{10,2},{12,4},{14,6},{1,9},{3,11}... | collective-permute-start | bytes 221192 | tf_op jit(solution)/shard_map/ppermute | solution.py:450
  25.9 0.0 collective-permute-done.10.refs_3_
  25.9 0.1 merge_lists.3
  26.0 0.4 %collective-permute-start.11 = (bf16[9,16,256]{2,1,0:T(8,128)(2,1)S(1)}, bf16[9,16,256]{2,1,0:T(8,128)(2,1)S(1)}, u32[]{:S(2)}, u32[]{:S(2)}) collective-permute-start(bf16[9,16,256]{2,1,0:T(8,128)(2,1)S(1)} %merge_lists.3), channel_id=1, source_target_pairs={{0,8},{2,10},{4,12},{6,14},{8,0},{10,2},{12,4},{14,6},{1,9},{3,11}... | collective-permute-start | bytes 221192 | tf_op jit(solution)/shard_map/ppermute | solution.py:450
  26.4 3.4 %collective-permute-done.7.refs_4_ = bf16[9,16,256]{2,1,0:T(8,128)(2,1)S(1)} collective-permute-done((bf16[9,16,256]{2,1,0:T(8,128)(2,1)S(1)}, bf16[9,16,256]{2,1,0:T(8,128)(2,1)S(1)}, u32[]{:S(2)}, u32[]{:S(2)}) %collective-permute-start.7) | collective-permute-done | bytes 73760 | tf_op jit(solution)/shard_map/ppermute | solution.py:450
  29.8 1.6 %collective-permute-done.11.refs_5_ = bf16[9,16,256]{2,1,0:T(8,128)(2,1)S(1)} collective-permute-done((bf16[9,16,256]{2,1,0:T(8,128)(2,1)S(1)}, bf16[9,16,256]{2,1,0:T(8,128)(2,1)S(1)}, u32[]{:S(2)}, u32[]{:S(2)}) %collective-permute-start.11) | collective-permute-done | bytes 73760 | tf_op jit(solution)/shard_map/ppermute | solution.py:450
  31.5 0.0 collective-permute-done.1.refs_1_
  31.5 0.0 collective-permute-done.2.refs_2_
  31.5 0.0 collective-permute-done.3.refs_3_
  31.5 0.9 %finish_pixels.1 = (f32[16,512]{1,0:T(8,128)}, s32[16,512]{1,0:T(8,128)}) custom-call(bf16[9,16,512]{2,1,0:T(8,128)(2,1)S(1)} %get-tuple-element.39.refs_0_, bf16[9,16,512]{2,1,0:T(8,128)(2,1)S(1)} %collective-permute-done.1.refs_1_, bf16[9,16,512]{2,1,0:T(8,128)(2,1)S(1)} %collective-permute-done.2.refs_2_, ...), custom_call_target="tpu_custom_call" | custom-call | tf_op jit(solution)/shard_map/finish_pixels/pallas_call | solution.py:435
Async XLA Ops:
  1.7 2.6 %collective-permute-start = (bf16[24,16,512]{2,1,0:T(8,128)(2,1)S(1)}, bf16[24,16,512]{2,1,0:T(8,128)(2,1)S(1)}, u32[]{:S(2)}, u32[]{:S(2)}) collective-permute-start(bf16[24,16,512]{2,1,0:T(8,128)(2,1)S(1)} %constant_dynamic-slice_fusion), channel_id=1, source_target_pairs={{0,1},{1,0},{2,3},{3,2},{4,5},{5,4},{6,7},{7,6},{8,9},{9,8},{10,11... | collective-permute-start | bytes 1179656 | tf_op jit(solution)/shard_map/ppermute | solution.py:450
  9.9 8.7 %collective-permute-start.4 = (bf16[9,16,256]{2,1,0:T(8,128)(2,1)S(1)}, bf16[9,16,256]{2,1,0:T(8,128)(2,1)S(1)}, u32[]{:S(2)}, u32[]{:S(2)}) collective-permute-start(bf16[9,16,256]{2,1,0:T(8,128)(2,1)S(1)} %get-tuple-element.44), channel_id=1, source_target_pairs={{0,6},{2,4},{4,2},{6,0},{8,14},{10,12},{12,10},{14,8},{1,7},{3,5},... | collective-permute-start | bytes 221192 | tf_op jit(solution)/shard_map/ppermute | solution.py:450
  13.5 5.3 %collective-permute-start.5 = (bf16[9,16,256]{2,1,0:T(8,128)(2,1)S(1)}, bf16[9,16,256]{2,1,0:T(8,128)(2,1)S(1)}, u32[]{:S(2)}, u32[]{:S(2)}) collective-permute-start(bf16[9,16,256]{2,1,0:T(8,128)(2,1)S(1)} %get-tuple-element.45), channel_id=1, source_target_pairs={{0,4},{2,6},{4,0},{6,2},{8,12},{10,14},{12,8},{14,10},{1,5},{3,7},... | collective-permute-start | bytes 221192 | tf_op jit(solution)/shard_map/ppermute | solution.py:450
  14.0 6.7 %collective-permute-start.6 = (bf16[9,16,256]{2,1,0:T(8,128)(2,1)S(1)}, bf16[9,16,256]{2,1,0:T(8,128)(2,1)S(1)}, u32[]{:S(2)}, u32[]{:S(2)}) collective-permute-start(bf16[9,16,256]{2,1,0:T(8,128)(2,1)S(1)} %get-tuple-element.46), channel_id=1, source_target_pairs={{0,2},{2,0},{4,6},{6,4},{8,10},{10,8},{12,14},{14,12},{1,3},{3,1},... | collective-permute-start | bytes 221192 | tf_op jit(solution)/shard_map/ppermute | solution.py:450
  14.2 8.1 %collective-permute-start.8 = (bf16[9,16,256]{2,1,0:T(8,128)(2,1)S(1)}, bf16[9,16,256]{2,1,0:T(8,128)(2,1)S(1)}, u32[]{:S(2)}, u32[]{:S(2)}) collective-permute-start(bf16[9,16,256]{2,1,0:T(8,128)(2,1)S(1)} %get-tuple-element.48), channel_id=1, source_target_pairs={{0,6},{2,4},{4,2},{6,0},{8,14},{10,12},{12,10},{14,8},{1,7},{3,5},... | collective-permute-start | bytes 221192 | tf_op jit(solution)/shard_map/ppermute | solution.py:450
  17.0 6.2 %collective-permute-start.9 = (bf16[9,16,256]{2,1,0:T(8,128)(2,1)S(1)}, bf16[9,16,256]{2,1,0:T(8,128)(2,1)S(1)}, u32[]{:S(2)}, u32[]{:S(2)}) collective-permute-start(bf16[9,16,256]{2,1,0:T(8,128)(2,1)S(1)} %get-tuple-element.49), channel_id=1, source_target_pairs={{0,4},{2,6},{4,0},{6,2},{8,12},{10,14},{12,8},{14,10},{1,5},{3,7},... | collective-permute-start | bytes 221192 | tf_op jit(solution)/shard_map/ppermute | solution.py:450
  18.6 7.3 %collective-permute-start.10 = (bf16[9,16,256]{2,1,0:T(8,128)(2,1)S(1)}, bf16[9,16,256]{2,1,0:T(8,128)(2,1)S(1)}, u32[]{:S(2)}, u32[]{:S(2)}) collective-permute-start(bf16[9,16,256]{2,1,0:T(8,128)(2,1)S(1)} %get-tuple-element.50), channel_id=1, source_target_pairs={{0,2},{2,0},{4,6},{6,4},{8,10},{10,8},{12,14},{14,12},{1,3},{3,1},... | collective-permute-start | bytes 221192 | tf_op jit(solution)/shard_map/ppermute | solution.py:450
  18.9 12.6 %collective-permute-start.1 = (bf16[9,16,512]{2,1,0:T(8,128)(2,1)S(1)}, bf16[9,16,512]{2,1,0:T(8,128)(2,1)S(1)}, u32[]{:S(2)}, u32[]{:S(2)}) collective-permute-start(bf16[9,16,512]{2,1,0:T(8,128)(2,1)S(1)} %get-tuple-element.40), channel_id=1, source_target_pairs={{0,2},{2,0},{4,6},{6,4},{8,10},{10,8},{12,14},{14,12},{1,3},{3,1},... | collective-permute-start | bytes 442376 | tf_op jit(solution)/shard_map/ppermute | solution.py:450
  20.7 10.8 %collective-permute-start.2 = (bf16[9,16,512]{2,1,0:T(8,128)(2,1)S(1)}, bf16[9,16,512]{2,1,0:T(8,128)(2,1)S(1)}, u32[]{:S(2)}, u32[]{:S(2)}) collective-permute-start(bf16[9,16,512]{2,1,0:T(8,128)(2,1)S(1)} %get-tuple-element.41), channel_id=1, source_target_pairs={{0,4},{2,6},{4,0},{6,2},{8,12},{10,14},{12,8},{14,10},{1,5},{3,7},... | collective-permute-start | bytes 442376 | tf_op jit(solution)/shard_map/ppermute | solution.py:450
  22.3 9.2 %collective-permute-start.3 = (bf16[9,16,512]{2,1,0:T(8,128)(2,1)S(1)}, bf16[9,16,512]{2,1,0:T(8,128)(2,1)S(1)}, u32[]{:S(2)}, u32[]{:S(2)}) collective-permute-start(bf16[9,16,512]{2,1,0:T(8,128)(2,1)S(1)} %get-tuple-element.42), channel_id=1, source_target_pairs={{0,6},{2,4},{4,2},{6,0},{8,14},{10,12},{12,10},{14,8},{1,7},{3,5},... | collective-permute-start | bytes 442376 | tf_op jit(solution)/shard_map/ppermute | solution.py:450
  23.3 6.6 %collective-permute-start.7 = (bf16[9,16,256]{2,1,0:T(8,128)(2,1)S(1)}, bf16[9,16,256]{2,1,0:T(8,128)(2,1)S(1)}, u32[]{:S(2)}, u32[]{:S(2)}) collective-permute-start(bf16[9,16,256]{2,1,0:T(8,128)(2,1)S(1)} %merge_lists.2), channel_id=1, source_target_pairs={{0,8},{2,10},{4,12},{6,14},{8,0},{10,2},{12,4},{14,6},{1,9},{3,11}... | collective-permute-start | bytes 221192 | tf_op jit(solution)/shard_map/ppermute | solution.py:450
  26.0 5.4 %collective-permute-start.11 = (bf16[9,16,256]{2,1,0:T(8,128)(2,1)S(1)}, bf16[9,16,256]{2,1,0:T(8,128)(2,1)S(1)}, u32[]{:S(2)}, u32[]{:S(2)}) collective-permute-start(bf16[9,16,256]{2,1,0:T(8,128)(2,1)S(1)} %merge_lists.3), channel_id=1, source_target_pairs={{0,8},{2,10},{4,12},{6,14},{8,0},{10,2},{12,4},{14,6},{1,9},{3,11}... | collective-permute-start | bytes 221192 | tf_op jit(solution)/shard_map/ppermute | solution.py:450

commit v5 on v4

--- a/solution.py
+++ b/solution.py
@@ -17,7 +17,7 @@
 TILE_ROWS = 16
 PAD = 16
 STRIDE = 8
-FAR_PARTS = 2
+FAR_PARTS = 1
 SQUARE = 4
 KERNEL_VMEM = 8 * 1024 * 1024
 LISTS = 2 * REJECT + 1
@@ -61,9 +61,51 @@
     return jnp.where(inside, banded, 0.0), jnp.where(inside, 0.0, banded)
 
 
+def bank_lines(taps, margin):
+    lines = jnp.pad(taps.astype(jnp.float32), ((0, 0), (0, BAND_COLS - TAPS)))
+    return pltpu.roll(lines, BAND_COLS - margin, 1)
+
+
+def edge_kernel(exposures_ref, vert_hbm, edge_ref, bank_v, taps, sems):
+    rows = exposures_ref.shape[1]
+    sky_place = lax.axis_index("sky")
+    start = pl.multiple_of((1 - sky_place) * (rows - PAD), TILE_ROWS)
+    edge_copy = pltpu.make_async_copy(
+        exposures_ref.at[:, pl.ds(start, PAD), :], edge_ref, sems.at[0]
+    )
+    taps_copy = pltpu.make_async_copy(vert_hbm, taps, sems.at[1])
+    taps_copy.start()
+    edge_copy.start()
+    taps_copy.wait()
+    lines = bank_lines(taps[...], TAPS // 2)
+    turn = PAD * sky_place
+    for kernel in range(taps.shape[0]):
+        main, edge = banded_pair(lines[kernel : kernel + 1])
+        bank_v[kernel, :, :BAND_COLS] = main.astype(jnp.bfloat16)
+        bank_v[kernel, :, BAND_COLS:] = pltpu.roll(edge, turn, 1)[:, :PAD].astype(jnp.bfloat16)
+    edge_copy.wait()
+
+
+def window_edges(exposures, vert):
+    slots, rows, columns = exposures.shape
+    hbm = pl.BlockSpec(memory_space=pltpu.HBM)
+    vmem = pl.BlockSpec(memory_space=pltpu.VMEM)
+    return pl.pallas_call(
+        edge_kernel,
+        out_shape=[
+            jax.ShapeDtypeStruct((slots, PAD, columns), jnp.bfloat16),
+            jax.ShapeDtypeStruct((vert.shape[0], rows, BAND_COLS + PAD), jnp.bfloat16),
+        ],
+        in_specs=[hbm] * 2,
+        out_specs=[vmem] * 2,
+        scratch_shapes=[pltpu.VMEM(vert.shape, jnp.bfloat16), pltpu.SemaphoreType.DMA((2,))],
+        compiler_params=pltpu.CompilerParams(vmem_limit_bytes=KERNEL_VMEM),
+        name="window_edges",
+    )(*[pltpu.with_memory_space_constraint(value, pltpu.HBM) for value in (exposures, vert)])
+
+
 def prepare_kernel(
     bands,
-    kernels,
     rows_out,
     exposures_ref,
     slot_hbm,
@@ -71,10 +113,8 @@
     bad_hbm,
     range_hbm,
     flux_hbm,
-    vert_hbm,
     horiz_hbm,
     pictures,
-    bank_v,
     bank_h,
     count_ref,
     slot_ref,
@@ -88,15 +128,13 @@
 ):
     rows = exposures_ref.shape[1]
     exposures_total = range_ref.shape[1]
-    margin = TAPS // 2
     place = lax.axis_index("expo")
     sky_place = lax.axis_index("sky")
     tables = [
         pltpu.make_async_copy(source, target, table_sems.at[i])
         for i, (source, target) in enumerate(
             (
-                (vert_hbm, taps.at[0]),
-                (horiz_hbm, taps.at[1]),
+                (horiz_hbm, taps),
                 (slot_hbm, slot_ref),
                 (choice_hbm, choice_ref),
                 (bad_hbm, bad_ref),
@@ -107,29 +145,22 @@
     ]
     for copy in tables:
         copy.start()
-    body_copy = pltpu.make_async_copy(exposures_ref, pictures, sem)
+    body_copy = pltpu.make_async_copy(
+        exposures_ref.at[pl.ds(0, STRIDE)], pictures.at[pl.ds(0, STRIDE)], sem
+    )
     body_copy.start()
 
     tables[0].wait()
-    tables[1].wait()
-    wide = ((0, 0), (0, BAND_COLS - TAPS))
-    vert_lines = jnp.pad(taps[0].astype(jnp.float32), wide)
-    vert_lines = pltpu.roll(vert_lines, BAND_COLS - margin, 1)
-    horiz_lines = jnp.pad(taps[1].astype(jnp.float32), wide)
-    horiz_lines = pltpu.roll(horiz_lines, BAND_COLS - margin, 1)
-    turn = PAD * sky_place
-    for kernel in range(kernels):
-        main, edge = banded_pair(vert_lines[kernel : kernel + 1])
-        bank_v[kernel, :, :BAND_COLS] = main.astype(jnp.bfloat16)
-        bank_v[kernel, :, BAND_COLS:] = pltpu.roll(edge, turn, 1)[:, :PAD].astype(jnp.bfloat16)
-        main, edge = banded_pair(horiz_lines[kernel : kernel + 1])
+    lines = bank_lines(taps[...], TAPS // 2)
+    for kernel in range(taps.shape[0]):
+        main, edge = banded_pair(lines[kernel : kernel + 1])
         edge = edge.T
         early = lax.broadcasted_iota(jnp.int32, edge.shape, 0) < BAND_COLS // 2
         before = jnp.where(early, 0.0, edge)
         after = jnp.where(early, edge, 0.0)
         for index, part in enumerate((before, main.T, after)):
             bank_h[kernel, index * BAND_COLS : (index + 1) * BAND_COLS] = part.astype(jnp.bfloat16)
-    for copy in tables[2:]:
+    for copy in tables[1:]:
         copy.wait()
 
     first_out = sky_place * rows + place * rows_out
@@ -144,28 +175,27 @@
     body_copy.wait()
 
 
-def prepare(rows_out, exposures, slot_ids, choice, bad, span, flux, vert, horiz):
-    rows, columns = exposures.shape[1:]
-    kernels = vert.shape[0]
+def prepare(rows_out, exposures, slot_ids, choice, bad, span, flux, horiz):
+    columns = exposures.shape[2]
+    kernels = horiz.shape[0]
     bands = columns // BAND_COLS
     tables = [jax.ShapeDtypeStruct(t.shape, t.dtype) for t in (slot_ids, choice, bad, span, flux)]
     hbm = pl.BlockSpec(memory_space=pltpu.HBM)
     vmem = pl.BlockSpec(memory_space=pltpu.VMEM)
     return pl.pallas_call(
-        functools.partial(prepare_kernel, bands, kernels, rows_out),
+        functools.partial(prepare_kernel, bands, rows_out),
         out_shape=[
             jax.ShapeDtypeStruct(exposures.shape, jnp.bfloat16),
-            jax.ShapeDtypeStruct((kernels, rows, BAND_COLS + PAD), jnp.bfloat16),
             jax.ShapeDtypeStruct((kernels, 3 * BAND_COLS, BAND_COLS), jnp.bfloat16),
             jax.ShapeDtypeStruct((rows_out, columns), jnp.int32),
         ]
         + tables,
-        in_specs=[hbm] * 8,
-        out_specs=[vmem] * 9,
+        in_specs=[hbm] * 7,
+        out_specs=[vmem] * 8,
         scratch_shapes=[
-            pltpu.VMEM((2,) + vert.shape, jnp.bfloat16),
+            pltpu.VMEM(horiz.shape, jnp.bfloat16),
             pltpu.SemaphoreType.DMA,
-            pltpu.SemaphoreType.DMA((7,)),
+            pltpu.SemaphoreType.DMA((6,)),
         ],
         compiler_params=pltpu.CompilerParams(vmem_limit_bytes=KERNEL_VMEM),
         cost_estimate=pl.CostEstimate(flops=1 << 20, bytes_accessed=4 << 20, transcendentals=0),
@@ -173,7 +203,7 @@
     )(
         *[
             pltpu.with_memory_space_constraint(value, pltpu.HBM)
-            for value in (exposures, slot_ids, choice, bad, span, flux, vert, horiz)
+            for value in (exposures, slot_ids, choice, bad, span, flux, horiz)
         ]
     )
 
@@ -211,7 +241,8 @@
 def filter_kernel(
     chunk_of,
     parts,
-    pictures,
+    exposures_ref,
+    _,
     halo,
     bank_v,
     bank_h,
@@ -220,12 +251,13 @@
     bad_vmem,
     range_vmem,
     flux_vmem,
+    pictures,
     high,
     low,
     total,
     *rest,
 ):
-    *outs, slot_ref, choice_ref, bad_ref, range_ref, flux_ref, sems = rest
+    *outs, slot_ref, choice_ref, bad_ref, range_ref, flux_ref, sems, body_sems = rest
     slots, rows, columns = pictures.shape
     bands = columns // BAND_COLS
     exposures_total = range_vmem.shape[1]
@@ -245,6 +277,15 @@
     ]
     for copy in tables:
         copy.start()
+
+    def body_copy(step):
+        window = pl.ds(step * STRIDE, STRIDE)
+        return pltpu.make_async_copy(
+            exposures_ref.at[window], pictures.at[window], body_sems.at[step]
+        )
+
+    for step in range(1, slots // STRIDE):
+        body_copy(step).start()
     total[...] = jnp.zeros_like(total)
     for copy in tables:
         copy.wait()
@@ -306,6 +347,10 @@
             low[slot, :, window] = jnp.where(usable, plane, sentinel)
 
     def body(step, carry):
+        @pl.when(step > 0)
+        def _():
+            body_copy(step).wait()
+
         held = first_pass(STRIDE * step)
         for i in range(STRIDE):
             ahead = first_pass(STRIDE * step + i + 1) if i + 1 < STRIDE else None
@@ -317,7 +362,7 @@
     select_chunks(chunk_of, parts, high, low, total, outs)
 
 
-def filter_slots(chunk_of, chunks, parts, pictures, halo, bank_v, bank_h, tables):
+def filter_slots(chunk_of, chunks, parts, exposures, pictures, halo, bank_v, bank_h, tables):
     slots, rows, columns = pictures.shape
     vmem = pl.BlockSpec(memory_space=pltpu.VMEM)
     return pl.pallas_call(
@@ -325,25 +370,31 @@
         out_shape=[
             jax.ShapeDtypeStruct(pictures.shape, jnp.bfloat16),
             jax.ShapeDtypeStruct(pictures.shape, jnp.bfloat16),
+            jax.ShapeDtypeStruct(pictures.shape, jnp.bfloat16),
             jax.ShapeDtypeStruct((rows, columns), jnp.float32),
         ]
         + [jax.ShapeDtypeStruct((LISTS, TILE_ROWS, columns // parts), jnp.bfloat16)]
         * (chunks * parts),
-        in_specs=[vmem] * (4 + len(tables)),
-        out_specs=[vmem] * (3 + chunks * parts),
+        in_specs=[pl.BlockSpec(memory_space=pltpu.HBM)] + [vmem] * (4 + len(tables)),
+        out_specs=[vmem] * (4 + chunks * parts),
+        input_output_aliases={1: 0},
         scratch_shapes=[pltpu.SMEM(table.shape, table.dtype) for table in tables]
-        + [pltpu.SemaphoreType.DMA((len(tables),))],
+        + [
+            pltpu.SemaphoreType.DMA((len(tables),)),
+            pltpu.SemaphoreType.DMA((slots // STRIDE,)),
+        ],
         compiler_params=pltpu.CompilerParams(vmem_limit_bytes=KERNEL_VMEM),
         cost_estimate=pl.CostEstimate(
             flops=4 * slots * rows * columns * 256, bytes_accessed=8 << 20, transcendentals=0
         ),
         name="filter_slots",
     )(
+        pltpu.with_memory_space_constraint(exposures, pltpu.HBM),
         *[
             pltpu.with_memory_space_constraint(value, pltpu.VMEM)
             for value in (pictures, halo, bank_v, bank_h, *tables)
-        ]
-    )
+        ],
+    )[1:]
 
 
 def select_kernel(chunk_of, parts, high, low, total, *outs):
@@ -456,13 +507,11 @@
     slot_count, row_dev, columns = exposures.shape
     exposures_total = flux_scale.shape[0]
     expo_size = lax.axis_size("expo")
-    sky_place = lax.axis_index("sky")
     rows_out = row_dev // expo_size
 
-    edge_rows = lax.dynamic_slice_in_dim(exposures, (1 - sky_place) * (row_dev - PAD), PAD, 1)
-    halo = swapped(edge_rows, "sky", 1)
-
-    pictures, bank_v, bank_h, count, *tables = prepare(
+    edges, bank_v = window_edges(exposures, vert_taps)
+    halo = swapped(edges, "sky", 1)
+    pictures, bank_h, count, *tables = prepare(
         rows_out,
         exposures,
         slot_ids,
@@ -470,7 +519,6 @@
         bad_bands.T,
         row_range.T,
         flux_scale,
-        vert_taps,
         horiz_taps,
     )
 
@@ -479,6 +527,7 @@
             lambda place, i: place ^ i ^ SQUARE,
             SQUARE,
             FAR_PARTS,
+            exposures,
             pictures,
             halo,
             bank_v,
@@ -496,7 +545,7 @@
     else:
         chunks = row_dev // TILE_ROWS
         high, low, total, *lists = filter_slots(
-            lambda place, i: i, chunks, 1, pictures, halo, bank_v, bank_h, tables
+            lambda place, i: i, chunks, 1, exposures, pictures, halo, bank_v, bank_h, tables
         )
         whole = jnp.concatenate(lists, 1)
         arrived = lax.all_to_all(whole, "expo", split_axis=1, concat_axis=0, tiled=True)

time: 32.5 us -> 31 us (0.954)
  starting transfers between devices: 15.7 us -> 13.6 us
  waiting for transfers between devices: 5.07 us -> 6.37 us
  local copies, waits for them, and re-layouts: 1.03 us -> 0 us
    ppermute x12 -> x8, starting transfers between devices: 15.7 us -> 13.6 us  [swapped(): return lax.ppermute(value, axis, [(i, i ^ distance) for i in range(count)])]
    ppermute x12 -> x8, waiting for transfers between devices: 5.07 us -> 6.37 us  [swapped(): return lax.ppermute(value, axis, [(i, i ^ distance) for i in range(count)])]
    dynamic_slice x1 -> x0, local copies, waits for them, and re-layouts: 1.03 us -> none  [shards(): lax.dynamic_slice_in_dim(exposures, (1 - sky_place) * (row_dev - PAD), PA...]
    pallas_call x1 -> x2, Pallas kernels: 2.07 us -> 2.47 us  [the longest x1 1.38 us: prepare(): pl.pallas_call(functools.partial(prepare_kernel, bands, rows_out), out_sh...]
  transfers between devices with their start and end apart: 12 -> 8, of which waited for: 2 -> 3; matrix products, arithmetic and copies ran while one was open for 0% -> 0% of each run, Pallas kernels for 10% -> 9%
where the time goes in v5:
time: 31 us; the launch traced here: 30.8 us
  starting transfers between devices  13.6 us (44%)
  Pallas kernels  10.2 us (33%)
  waiting for transfers between devices  6.37 us (21%)
  between operations  0.67 us (2%)
    ppermute x8, starting transfers between devices, swapped(): return lax.ppermute(value, axis, [(i, i ^ distance) for i in range(count)])  13.6 us
    ppermute x8, waiting for transfers between devices, swapped(): return lax.ppermute(value, axis, [(i, i ^ distance) for i in range(count)])  6.37 us
    pallas_call x1, Pallas kernels, filter_slots(): pl.pallas_call(functools.partial(filter_kernel, chunk_of, parts), out_sha...  5.54 us
    pallas_call x1, Pallas kernels, prepare(): pl.pallas_call(functools.partial(prepare_kernel, bands, rows_out), out_sh...  1.38 us
    pallas_call x1, Pallas kernels, select(): pl.pallas_call(functools.partial(select_kernel, chunk_of, parts), out_sha...  1.1 us
    pallas_call x1, Pallas kernels, window_edges(): pl.pallas_call(edge_kernel, out_shape=[jax.ShapeDtypeStruct((slots, PAD,...  1.09 us
    pallas_call x1, Pallas kernels, finish(): pl.pallas_call(functools.partial(finish_kernel, exposures_total, len(whol...  0.86 us
  transfers between devices with their start and end apart: 8, of which 3 were waited for; matrix products, arithmetic and copies ran while one was open for 0% of the time, Pallas kernels for 9%

profile of v5, /device:TPU:0, one launch (start us, length us, event | category | flops | bytes accessed | tf_op | source)
XLA Modules:
  0.0 30.8 jit_solution(16836200907905683085)
XLA Ops:
  0.6 1.1 %window_edges.1 = (bf16[24,16,512]{2,1,0:T(8,128)(2,1)S(1)}, bf16[10,128,144]{2,1,0:T(8,128)(2,1)S(1)}) custom-call(bf16[24,128,512]{2,1,0:T(8,128)(2,1)} %exposures_ref.5, bf16[10,21]{1,0:T(8,128)(2,1)} %vert_hbm.1), custom_call_target="tpu_custom_call" | custom-call | tf_op jit(solution)/shard_map/window_edges/pallas_call | solution.py:93
  1.7 0.5 %collective-permute-start = (bf16[24,16,512]{2,1,0:T(8,128)(2,1)S(1)}, bf16[24,16,512]{2,1,0:T(8,128)(2,1)S(1)}, u32[]{:S(2)}, u32[]{:S(2)}) collective-permute-start(bf16[24,16,512]{2,1,0:T(8,128)(2,1)S(1)} %get-tuple-element.26), channel_id=1, source_target_pairs={{0,1},{1,0},{2,3},{3,2},{4,5},{5,4},{6,7},{7,6},{8,9},{9,8},{10,11... | collective-permute-start | bytes 1179656 | tf_op jit(solution)/shard_map/ppermute | solution.py:501
  2.2 1.4 %prepare.1 = (bf16[24,128,512]{2,1,0:T(8,128)(2,1)S(1)}, bf16[10,384,128]{2,1,0:T(8,128)(2,1)S(1)}, s32[16,512]{1,0:T(8,128)S(1)}, s32[8,24]{1,0:T(8,128)S(1)}, ...) custom-call(bf16[24,128,512]{2,1,0:T(8,128)(2,1)} %exposures_ref.5, ...), custom_call_target="tpu_custom_call" | custom-call | flops 1048576 | bytes 4194304 | tf_op jit(solution)/shard_map/prepare/pallas_call | solution.py:185
  3.6 0.0 collective-permute-done.halo
  3.6 5.5 %filter_slots.1 = (bf16[24,128,512]{2,1,0:T(8,128)(2,1)S(1)}, bf16[24,128,512]{2,1,0:T(8,128)(2,1)S(1)}, bf16[24,128,512]{2,1,0:T(8,128)(2,1)S(1)}, f32[128,512]...) custom-call(bf16[24,128,512]{2,1,0:T(8,128)(2,1)} %exposures_ref.5, ...), custom_call_target="tpu_custom_call", output_to_operand_aliasing={{0}: (1, {})} | custom-call | flops 1610612736 | bytes 8388608 | tf_op jit(solution)/shard_map/filter_slots/pallas_call | solution.py:368
  9.2 3.9 %collective-permute-start.4 = (bf16[9,16,512]{2,1,0:T(8,128)(2,1)S(1)}, bf16[9,16,512]{2,1,0:T(8,128)(2,1)S(1)}, u32[]{:S(2)}, u32[]{:S(2)}) collective-permute-start(bf16[9,16,512]{2,1,0:T(8,128)(2,1)S(1)} %get-tuple-element.42), channel_id=1, source_target_pairs={{0,6},{2,4},{4,2},{6,0},{8,14},{10,12},{12,10},{14,8},{1,7},{3,5},... | collective-permute-start | bytes 442376 | tf_op jit(solution)/shard_map/ppermute | solution.py:501
  13.1 0.4 %collective-permute-start.5 = (bf16[9,16,512]{2,1,0:T(8,128)(2,1)S(1)}, bf16[9,16,512]{2,1,0:T(8,128)(2,1)S(1)}, u32[]{:S(2)}, u32[]{:S(2)}) collective-permute-start(bf16[9,16,512]{2,1,0:T(8,128)(2,1)S(1)} %get-tuple-element.43), channel_id=1, source_target_pairs={{0,4},{2,6},{4,0},{6,2},{8,12},{10,14},{12,8},{14,10},{1,5},{3,7},... | collective-permute-start | bytes 442376 | tf_op jit(solution)/shard_map/ppermute | solution.py:501
  13.6 0.2 collective-permute-start.6
  13.7 1.1 %select_rows.1 = (bf16[9,16,512]{2,1,0:T(8,128)(2,1)S(1)}, bf16[9,16,512]{2,1,0:T(8,128)(2,1)S(1)}, bf16[9,16,512]{2,1,0:T(8,128)(2,1)S(1)}, bf16[9,16,512]{2,1,0:T(8,128)(2,1)S(1)}) custom-call(bf16[24,128,512]{2,1,0:T(8,128)(2,1)S(1)} %get-tuple-element.34.high, bf16[24,128,512]{2,1,0:T(8,128)(2,1)S(1)} %get-tuple-element.35.low, ...), custom_call_target="tpu_custom_call" | custom-call | flops 16777216 | bytes 4194304 | tf_op jit(solution)/shard_map/select_rows/pallas_call | solution.py:406
  14.9 1.9 %collective-permute-start.1 = (bf16[9,16,512]{2,1,0:T(8,128)(2,1)S(1)}, bf16[9,16,512]{2,1,0:T(8,128)(2,1)S(1)}, u32[]{:S(2)}, u32[]{:S(2)}) collective-permute-start(bf16[9,16,512]{2,1,0:T(8,128)(2,1)S(1)} %get-tuple-element.38), channel_id=1, source_target_pairs={{0,2},{2,0},{4,6},{6,4},{8,10},{10,8},{12,14},{14,12},{1,3},{3,1},... | collective-permute-start | bytes 442376 | tf_op jit(solution)/shard_map/ppermute | solution.py:501
  16.7 1.6 %collective-permute-start.2 = (bf16[9,16,512]{2,1,0:T(8,128)(2,1)S(1)}, bf16[9,16,512]{2,1,0:T(8,128)(2,1)S(1)}, u32[]{:S(2)}, u32[]{:S(2)}) collective-permute-start(bf16[9,16,512]{2,1,0:T(8,128)(2,1)S(1)} %get-tuple-element.39), channel_id=1, source_target_pairs={{0,4},{2,6},{4,0},{6,2},{8,12},{10,14},{12,8},{14,10},{1,5},{3,7},... | collective-permute-start | bytes 442376 | tf_op jit(solution)/shard_map/ppermute | solution.py:501
  18.3 0.0 collective-permute-done.4.refs_1_
  18.3 2.4 %collective-permute-start.3 = (bf16[9,16,512]{2,1,0:T(8,128)(2,1)S(1)}, bf16[9,16,512]{2,1,0:T(8,128)(2,1)S(1)}, u32[]{:S(2)}, u32[]{:S(2)}) collective-permute-start(bf16[9,16,512]{2,1,0:T(8,128)(2,1)S(1)} %get-tuple-element.40), channel_id=1, source_target_pairs={{0,6},{2,4},{4,2},{6,0},{8,14},{10,12},{12,10},{14,8},{1,7},{3,5},... | collective-permute-start | bytes 442376 | tf_op jit(solution)/shard_map/ppermute | solution.py:501
  20.7 0.7 %collective-permute-done.5.refs_2_ = bf16[9,16,512]{2,1,0:T(8,128)(2,1)S(1)} collective-permute-done((bf16[9,16,512]{2,1,0:T(8,128)(2,1)S(1)}, bf16[9,16,512]{2,1,0:T(8,128)(2,1)S(1)}, u32[]{:S(2)}, u32[]{:S(2)}) %collective-permute-start.5) | collective-permute-done | bytes 147488 | tf_op jit(solution)/shard_map/ppermute | solution.py:501
  21.4 0.0 collective-permute-done.6.refs_3_
  21.4 0.2 merge_lists.1
  21.6 2.7 %collective-permute-start.7 = (bf16[9,16,512]{2,1,0:T(8,128)(2,1)S(1)}, bf16[9,16,512]{2,1,0:T(8,128)(2,1)S(1)}, u32[]{:S(2)}, u32[]{:S(2)}) collective-permute-start(bf16[9,16,512]{2,1,0:T(8,128)(2,1)S(1)} %merge_lists.1), channel_id=1, source_target_pairs={{0,8},{2,10},{4,12},{6,14},{8,0},{10,2},{12,4},{14,6},{1,9},{3,11}... | collective-permute-start | bytes 442376 | tf_op jit(solution)/shard_map/ppermute | solution.py:501
  24.3 0.0 collective-permute-done.1.refs_1_
  24.3 3.5 %collective-permute-done.2.refs_2_ = bf16[9,16,512]{2,1,0:T(8,128)(2,1)S(1)} collective-permute-done((bf16[9,16,512]{2,1,0:T(8,128)(2,1)S(1)}, bf16[9,16,512]{2,1,0:T(8,128)(2,1)S(1)}, u32[]{:S(2)}, u32[]{:S(2)}) %collective-permute-start.2) | collective-permute-done | bytes 147488 | tf_op jit(solution)/shard_map/ppermute | solution.py:501
  27.7 2.2 %collective-permute-done.3.refs_3_ = bf16[9,16,512]{2,1,0:T(8,128)(2,1)S(1)} collective-permute-done((bf16[9,16,512]{2,1,0:T(8,128)(2,1)S(1)}, bf16[9,16,512]{2,1,0:T(8,128)(2,1)S(1)}, u32[]{:S(2)}, u32[]{:S(2)}) %collective-permute-start.3) | collective-permute-done | bytes 147488 | tf_op jit(solution)/shard_map/ppermute | solution.py:501
  30.0 0.0 collective-permute-done.7.refs_4_
  30.0 0.9 %finish_pixels.1 = (f32[16,512]{1,0:T(8,128)}, s32[16,512]{1,0:T(8,128)}) custom-call(bf16[9,16,512]{2,1,0:T(8,128)(2,1)S(1)} %get-tuple-element.37.refs_0_, bf16[9,16,512]{2,1,0:T(8,128)(2,1)S(1)} %collective-permute-done.1.refs_1_, bf16[9,16,512]{2,1,0:T(8,128)(2,1)S(1)} %collective-permute-done.2.refs_2_, ...), custom_call_target="tpu_custom_call" | custom-call | tf_op jit(solution)/shard_map/finish_pixels/pallas_call | solution.py:486
Async XLA Ops:
  1.7 1.9 %collective-permute-start = (bf16[24,16,512]{2,1,0:T(8,128)(2,1)S(1)}, bf16[24,16,512]{2,1,0:T(8,128)(2,1)S(1)}, u32[]{:S(2)}, u32[]{:S(2)}) collective-permute-start(bf16[24,16,512]{2,1,0:T(8,128)(2,1)S(1)} %get-tuple-element.26), channel_id=1, source_target_pairs={{0,1},{1,0},{2,3},{3,2},{4,5},{5,4},{6,7},{7,6},{8,9},{9,8},{10,11... | collective-permute-start | bytes 1179656 | tf_op jit(solution)/shard_map/ppermute | solution.py:501
  9.2 9.1 %collective-permute-start.4 = (bf16[9,16,512]{2,1,0:T(8,128)(2,1)S(1)}, bf16[9,16,512]{2,1,0:T(8,128)(2,1)S(1)}, u32[]{:S(2)}, u32[]{:S(2)}) collective-permute-start(bf16[9,16,512]{2,1,0:T(8,128)(2,1)S(1)} %get-tuple-element.42), channel_id=1, source_target_pairs={{0,6},{2,4},{4,2},{6,0},{8,14},{10,12},{12,10},{14,8},{1,7},{3,5},... | collective-permute-start | bytes 442376 | tf_op jit(solution)/shard_map/ppermute | solution.py:501
  13.1 8.3 %collective-permute-start.5 = (bf16[9,16,512]{2,1,0:T(8,128)(2,1)S(1)}, bf16[9,16,512]{2,1,0:T(8,128)(2,1)S(1)}, u32[]{:S(2)}, u32[]{:S(2)}) collective-permute-start(bf16[9,16,512]{2,1,0:T(8,128)(2,1)S(1)} %get-tuple-element.43), channel_id=1, source_target_pairs={{0,4},{2,6},{4,0},{6,2},{8,12},{10,14},{12,8},{14,10},{1,5},{3,7},... | collective-permute-start | bytes 442376 | tf_op jit(solution)/shard_map/ppermute | solution.py:501
  13.6 7.9 %collective-permute-start.6 = (bf16[9,16,512]{2,1,0:T(8,128)(2,1)S(1)}, bf16[9,16,512]{2,1,0:T(8,128)(2,1)S(1)}, u32[]{:S(2)}, u32[]{:S(2)}) collective-permute-start(bf16[9,16,512]{2,1,0:T(8,128)(2,1)S(1)} %get-tuple-element.44), channel_id=1, source_target_pairs={{0,2},{2,0},{4,6},{6,4},{8,10},{10,8},{12,14},{14,12},{1,3},{3,1},... | collective-permute-start | bytes 442376 | tf_op jit(solution)/shard_map/ppermute | solution.py:501
  14.9 9.4 %collective-permute-start.1 = (bf16[9,16,512]{2,1,0:T(8,128)(2,1)S(1)}, bf16[9,16,512]{2,1,0:T(8,128)(2,1)S(1)}, u32[]{:S(2)}, u32[]{:S(2)}) collective-permute-start(bf16[9,16,512]{2,1,0:T(8,128)(2,1)S(1)} %get-tuple-element.38), channel_id=1, source_target_pairs={{0,2},{2,0},{4,6},{6,4},{8,10},{10,8},{12,14},{14,12},{1,3},{3,1},... | collective-permute-start | bytes 442376 | tf_op jit(solution)/shard_map/ppermute | solution.py:501
  16.7 11.0 %collective-permute-start.2 = (bf16[9,16,512]{2,1,0:T(8,128)(2,1)S(1)}, bf16[9,16,512]{2,1,0:T(8,128)(2,1)S(1)}, u32[]{:S(2)}, u32[]{:S(2)}) collective-permute-start(bf16[9,16,512]{2,1,0:T(8,128)(2,1)S(1)} %get-tuple-element.39), channel_id=1, source_target_pairs={{0,4},{2,6},{4,0},{6,2},{8,12},{10,14},{12,8},{14,10},{1,5},{3,7},... | collective-permute-start | bytes 442376 | tf_op jit(solution)/shard_map/ppermute | solution.py:501
  18.3 11.6 %collective-permute-start.3 = (bf16[9,16,512]{2,1,0:T(8,128)(2,1)S(1)}, bf16[9,16,512]{2,1,0:T(8,128)(2,1)S(1)}, u32[]{:S(2)}, u32[]{:S(2)}) collective-permute-start(bf16[9,16,512]{2,1,0:T(8,128)(2,1)S(1)} %get-tuple-element.40), channel_id=1, source_target_pairs={{0,6},{2,4},{4,2},{6,0},{8,14},{10,12},{12,10},{14,8},{1,7},{3,5},... | collective-permute-start | bytes 442376 | tf_op jit(solution)/shard_map/ppermute | solution.py:501
  21.6 8.3 %collective-permute-start.7 = (bf16[9,16,512]{2,1,0:T(8,128)(2,1)S(1)}, bf16[9,16,512]{2,1,0:T(8,128)(2,1)S(1)}, u32[]{:S(2)}, u32[]{:S(2)}) collective-permute-start(bf16[9,16,512]{2,1,0:T(8,128)(2,1)S(1)} %merge_lists.1), channel_id=1, source_target_pairs={{0,8},{2,10},{4,12},{6,14},{8,0},{10,2},{12,4},{14,6},{1,9},{3,11}... | collective-permute-start | bytes 442376 | tf_op jit(solution)/shard_map/ppermute | solution.py:501

commit v6 on v5

--- a/solution.py
+++ b/solution.py
@@ -523,10 +523,10 @@
     )
 
     if rows_out == TILE_ROWS and expo_size == 2 * SQUARE:
-        high, low, total, *far = filter_slots(
-            lambda place, i: place ^ i ^ SQUARE,
-            SQUARE,
-            FAR_PARTS,
+        high, low, total, *sent = filter_slots(
+            lambda place, i: place ^ (i + 1) ^ SQUARE,
+            SQUARE - 1,
+            1,
             exposures,
             pictures,
             halo,
@@ -534,14 +534,20 @@
             bank_h,
             tables,
         )
-        across = []
-        for part in range(FAR_PARTS):
-            own, *sent = far[part::FAR_PARTS]
-            got = [swapped(sent[i], "expo", 1 + i) for i in reversed(range(SQUARE - 1))]
-            across.append(swapped(merge([own] + got), "expo", SQUARE))
-        near = list(select(lambda place, i: place ^ i, SQUARE, 1, high, low, total))
+        got = [swapped(sent[i], "expo", 1 + i) for i in reversed(range(SQUARE - 1))]
+        kept, *near = select(
+            lambda place, i: place ^ (SQUARE if i == 0 else i - 1),
+            SQUARE + 1,
+            1,
+            high,
+            low,
+            total,
+        )
         near = near[:1] + [swapped(part, "expo", 1 + i) for i, part in enumerate(near[1:])]
-        coadd_plane, rejected_count = finish(near, across, count, exposures_total)
+        across = swapped(merge([kept] + got), "expo", SQUARE)
+        coadd_plane, rejected_count = finish(
+            [merge(near[:-1]), near[-1], across], [], count, exposures_total
+        )
     else:
         chunks = row_dev // TILE_ROWS
         high, low, total, *lists = filter_slots(

time: 31 us -> 30.6 us (0.987)
  transfers between devices with their start and end apart: 8 -> 8, of which waited for: 3 -> 3; matrix products, arithmetic and copies ran while one was open for 0% -> 0% of each run, Pallas kernels for 9% -> 10%
where the time goes in v6:
time: 30.6 us; the launch traced here: 30.4 us
  starting transfers between devices  13.3 us (43%)
  Pallas kernels  10.2 us (33%)
  waiting for transfers between devices  6.22 us (20%)
  between operations  0.67 us (2%)
    ppermute x8, starting transfers between devices, swapped(): return lax.ppermute(value, axis, [(i, i ^ distance) for i in range(count)])  13.3 us
    ppermute x8, waiting for transfers between devices, swapped(): return lax.ppermute(value, axis, [(i, i ^ distance) for i in range(count)])  6.22 us
    pallas_call x1, Pallas kernels, filter_slots(): pl.pallas_call(functools.partial(filter_kernel, chunk_of, parts), out_sha...  5.27 us
    pallas_call x1, Pallas kernels, prepare(): pl.pallas_call(functools.partial(prepare_kernel, bands, rows_out), out_sh...  1.38 us
    pallas_call x1, Pallas kernels, select(): pl.pallas_call(functools.partial(select_kernel, chunk_of, parts), out_sha...  1.37 us
    pallas_call x1, Pallas kernels, window_edges(): pl.pallas_call(edge_kernel, out_shape=[jax.ShapeDtypeStruct((slots, PAD,...  1.09 us
    pallas_call x1, Pallas kernels, finish(): pl.pallas_call(functools.partial(finish_kernel, exposures_total, len(whol...  0.75 us
  transfers between devices with their start and end apart: 8, of which 3 were waited for; matrix products, arithmetic and copies ran while one was open for 0% of the time, Pallas kernels for 10%

profile of v6, /device:TPU:0, one launch (start us, length us, event | category | flops | bytes accessed | tf_op | source)
XLA Modules:
  0.0 30.4 jit_solution(1706607061230694016)
XLA Ops:
  0.6 1.1 %window_edges.1 = (bf16[24,16,512]{2,1,0:T(8,128)(2,1)S(1)}, bf16[10,128,144]{2,1,0:T(8,128)(2,1)S(1)}) custom-call(bf16[24,128,512]{2,1,0:T(8,128)(2,1)} %exposures_ref.5, bf16[10,21]{1,0:T(8,128)(2,1)} %vert_hbm.1), custom_call_target="tpu_custom_call" | custom-call | tf_op jit(solution)/shard_map/window_edges/pallas_call | solution.py:93
  1.7 0.5 %collective-permute-start = (bf16[24,16,512]{2,1,0:T(8,128)(2,1)S(1)}, bf16[24,16,512]{2,1,0:T(8,128)(2,1)S(1)}, u32[]{:S(2)}, u32[]{:S(2)}) collective-permute-start(bf16[24,16,512]{2,1,0:T(8,128)(2,1)S(1)} %get-tuple-element.26), channel_id=1, source_target_pairs={{0,1},{1,0},{2,3},{3,2},{4,5},{5,4},{6,7},{7,6},{8,9},{9,8},{10,11... | collective-permute-start | bytes 1179656 | tf_op jit(solution)/shard_map/ppermute | solution.py:501
  2.2 1.4 %prepare.1 = (bf16[24,128,512]{2,1,0:T(8,128)(2,1)S(1)}, bf16[10,384,128]{2,1,0:T(8,128)(2,1)S(1)}, s32[16,512]{1,0:T(8,128)S(1)}, s32[8,24]{1,0:T(8,128)S(1)}, ...) custom-call(bf16[24,128,512]{2,1,0:T(8,128)(2,1)} %exposures_ref.5, ...), custom_call_target="tpu_custom_call" | custom-call | flops 1048576 | bytes 4194304 | tf_op jit(solution)/shard_map/prepare/pallas_call | solution.py:185
  3.6 0.0 collective-permute-done.halo
  3.6 5.3 %filter_slots.1 = (bf16[24,128,512]{2,1,0:T(8,128)(2,1)S(1)}, bf16[24,128,512]{2,1,0:T(8,128)(2,1)S(1)}, bf16[24,128,512]{2,1,0:T(8,128)(2,1)S(1)}, f32[128,512]...) custom-call(bf16[24,128,512]{2,1,0:T(8,128)(2,1)} %exposures_ref.5, ...), custom_call_target="tpu_custom_call", output_to_operand_aliasing={{0}: (1, {})} | custom-call | flops 1610612736 | bytes 8388608 | tf_op jit(solution)/shard_map/filter_slots/pallas_call | solution.py:368
  8.9 3.9 %collective-permute-start.4 = (bf16[9,16,512]{2,1,0:T(8,128)(2,1)S(1)}, bf16[9,16,512]{2,1,0:T(8,128)(2,1)S(1)}, u32[]{:S(2)}, u32[]{:S(2)}) collective-permute-start(bf16[9,16,512]{2,1,0:T(8,128)(2,1)S(1)} %get-tuple-element.42), channel_id=1, source_target_pairs={{0,6},{2,4},{4,2},{6,0},{8,14},{10,12},{12,10},{14,8},{1,7},{3,5},... | collective-permute-start | bytes 442376 | tf_op jit(solution)/shard_map/ppermute | solution.py:501
  12.8 0.4 %collective-permute-start.5 = (bf16[9,16,512]{2,1,0:T(8,128)(2,1)S(1)}, bf16[9,16,512]{2,1,0:T(8,128)(2,1)S(1)}, u32[]{:S(2)}, u32[]{:S(2)}) collective-permute-start(bf16[9,16,512]{2,1,0:T(8,128)(2,1)S(1)} %get-tuple-element.43), channel_id=1, source_target_pairs={{0,4},{2,6},{4,0},{6,2},{8,12},{10,14},{12,8},{14,10},{1,5},{3,7},... | collective-permute-start | bytes 442376 | tf_op jit(solution)/shard_map/ppermute | solution.py:501
  13.3 0.2 collective-permute-start.6
  13.5 1.4 %select_rows.1 = (bf16[9,16,512]{2,1,0:T(8,128)(2,1)S(1)}, bf16[9,16,512]{2,1,0:T(8,128)(2,1)S(1)}, bf16[9,16,512]{2,1,0:T(8,128)(2,1)S(1)}, bf16[9,16,512]{2,1,0:T(8,128)(2,1)S(1)}, bf16[9,16,512]{2,1,0:T(8,128)(2,1)S(1)}) custom-call(bf16[24,128,512]{2,1,0:T(8,128)(2,1)S(1)} %get-tuple-element.34.high, bf16[24,128,512]{2,1,0:T(8,128)(2,1)S(1)} %get-tuple-element.35.low, ...), custom_call_target="tpu_custom_call" | custom-call | flops 16777216 | bytes 4194304 | tf_op jit(solution)/shard_map/select_rows/pallas_call | solution.py:406
  14.8 1.9 %collective-permute-start.1 = (bf16[9,16,512]{2,1,0:T(8,128)(2,1)S(1)}, bf16[9,16,512]{2,1,0:T(8,128)(2,1)S(1)}, u32[]{:S(2)}, u32[]{:S(2)}) collective-permute-start(bf16[9,16,512]{2,1,0:T(8,128)(2,1)S(1)} %get-tuple-element.38), channel_id=1, source_target_pairs={{0,2},{2,0},{4,6},{6,4},{8,10},{10,8},{12,14},{14,12},{1,3},{3,1},... | collective-permute-start | bytes 442376 | tf_op jit(solution)/shard_map/ppermute | solution.py:501
  16.7 1.6 %collective-permute-start.2 = (bf16[9,16,512]{2,1,0:T(8,128)(2,1)S(1)}, bf16[9,16,512]{2,1,0:T(8,128)(2,1)S(1)}, u32[]{:S(2)}, u32[]{:S(2)}) collective-permute-start(bf16[9,16,512]{2,1,0:T(8,128)(2,1)S(1)} %get-tuple-element.39), channel_id=1, source_target_pairs={{0,4},{2,6},{4,0},{6,2},{8,12},{10,14},{12,8},{14,10},{1,5},{3,7},... | collective-permute-start | bytes 442376 | tf_op jit(solution)/shard_map/ppermute | solution.py:501
  18.3 0.0 collective-permute-done.4.refs_1_
  18.3 2.1 %collective-permute-start.3 = (bf16[9,16,512]{2,1,0:T(8,128)(2,1)S(1)}, bf16[9,16,512]{2,1,0:T(8,128)(2,1)S(1)}, u32[]{:S(2)}, u32[]{:S(2)}) collective-permute-start(bf16[9,16,512]{2,1,0:T(8,128)(2,1)S(1)} %get-tuple-element.40), channel_id=1, source_target_pairs={{0,6},{2,4},{4,2},{6,0},{8,14},{10,12},{12,10},{14,8},{1,7},{3,5},... | collective-permute-start | bytes 442376 | tf_op jit(solution)/shard_map/ppermute | solution.py:501
  20.5 0.7 %collective-permute-done.5.refs_2_ = bf16[9,16,512]{2,1,0:T(8,128)(2,1)S(1)} collective-permute-done((bf16[9,16,512]{2,1,0:T(8,128)(2,1)S(1)}, bf16[9,16,512]{2,1,0:T(8,128)(2,1)S(1)}, u32[]{:S(2)}, u32[]{:S(2)}) %collective-permute-start.5) | collective-permute-done | bytes 147488 | tf_op jit(solution)/shard_map/ppermute | solution.py:501
  21.1 0.0 collective-permute-done.6.refs_3_
  21.1 0.2 merge_lists.3
  21.3 2.7 %collective-permute-start.7 = (bf16[9,16,512]{2,1,0:T(8,128)(2,1)S(1)}, bf16[9,16,512]{2,1,0:T(8,128)(2,1)S(1)}, u32[]{:S(2)}, u32[]{:S(2)}) collective-permute-start(bf16[9,16,512]{2,1,0:T(8,128)(2,1)S(1)} %merge_lists.3), channel_id=1, source_target_pairs={{0,8},{2,10},{4,12},{6,14},{8,0},{10,2},{12,4},{14,6},{1,9},{3,11}... | collective-permute-start | bytes 442376 | tf_op jit(solution)/shard_map/ppermute | solution.py:501
  24.0 0.0 collective-permute-done.1.refs_1_
  24.0 3.5 %collective-permute-done.2.refs_2_ = bf16[9,16,512]{2,1,0:T(8,128)(2,1)S(1)} collective-permute-done((bf16[9,16,512]{2,1,0:T(8,128)(2,1)S(1)}, bf16[9,16,512]{2,1,0:T(8,128)(2,1)S(1)}, u32[]{:S(2)}, u32[]{:S(2)}) %collective-permute-start.2) | collective-permute-done | bytes 147488 | tf_op jit(solution)/shard_map/ppermute | solution.py:501
  27.5 0.1 merge_lists.2.refs_0_
  27.6 2.1 %collective-permute-done.3.refs_1_ = bf16[9,16,512]{2,1,0:T(8,128)(2,1)S(1)} collective-permute-done((bf16[9,16,512]{2,1,0:T(8,128)(2,1)S(1)}, bf16[9,16,512]{2,1,0:T(8,128)(2,1)S(1)}, u32[]{:S(2)}, u32[]{:S(2)}) %collective-permute-start.3) | collective-permute-done | bytes 147488 | tf_op jit(solution)/shard_map/ppermute | solution.py:501
  29.7 0.0 collective-permute-done.7.refs_2_
  29.7 0.8 %finish_pixels.1 = (f32[16,512]{1,0:T(8,128)}, s32[16,512]{1,0:T(8,128)}) custom-call(bf16[9,16,512]{2,1,0:T(8,128)(2,1)S(1)} %merge_lists.2.refs_0_, bf16[9,16,512]{2,1,0:T(8,128)(2,1)S(1)} %collective-permute-done.3.refs_1_, bf16[9,16,512]{2,1,0:T(8,128)(2,1)S(1)} %collective-permute-done.7.refs_2_, s32[16,512]{1,0:T(8,128)S(1)} %get-tuple-element.45.refs_3_), custom_call_target="tpu_custom_call" | custom-call | tf_op jit(solution)/shard_map/finish_pixels/pallas_call | solution.py:486
Async XLA Ops:
  1.7 1.9 %collective-permute-start = (bf16[24,16,512]{2,1,0:T(8,128)(2,1)S(1)}, bf16[24,16,512]{2,1,0:T(8,128)(2,1)S(1)}, u32[]{:S(2)}, u32[]{:S(2)}) collective-permute-start(bf16[24,16,512]{2,1,0:T(8,128)(2,1)S(1)} %get-tuple-element.26), channel_id=1, source_target_pairs={{0,1},{1,0},{2,3},{3,2},{4,5},{5,4},{6,7},{7,6},{8,9},{9,8},{10,11... | collective-permute-start | bytes 1179656 | tf_op jit(solution)/shard_map/ppermute | solution.py:501
  8.9 9.4 %collective-permute-start.4 = (bf16[9,16,512]{2,1,0:T(8,128)(2,1)S(1)}, bf16[9,16,512]{2,1,0:T(8,128)(2,1)S(1)}, u32[]{:S(2)}, u32[]{:S(2)}) collective-permute-start(bf16[9,16,512]{2,1,0:T(8,128)(2,1)S(1)} %get-tuple-element.42), channel_id=1, source_target_pairs={{0,6},{2,4},{4,2},{6,0},{8,14},{10,12},{12,10},{14,8},{1,7},{3,5},... | collective-permute-start | bytes 442376 | tf_op jit(solution)/shard_map/ppermute | solution.py:501
  12.8 8.3 %collective-permute-start.5 = (bf16[9,16,512]{2,1,0:T(8,128)(2,1)S(1)}, bf16[9,16,512]{2,1,0:T(8,128)(2,1)S(1)}, u32[]{:S(2)}, u32[]{:S(2)}) collective-permute-start(bf16[9,16,512]{2,1,0:T(8,128)(2,1)S(1)} %get-tuple-element.43), channel_id=1, source_target_pairs={{0,4},{2,6},{4,0},{6,2},{8,12},{10,14},{12,8},{14,10},{1,5},{3,7},... | collective-permute-start | bytes 442376 | tf_op jit(solution)/shard_map/ppermute | solution.py:501
  13.3 7.9 %collective-permute-start.6 = (bf16[9,16,512]{2,1,0:T(8,128)(2,1)S(1)}, bf16[9,16,512]{2,1,0:T(8,128)(2,1)S(1)}, u32[]{:S(2)}, u32[]{:S(2)}) collective-permute-start(bf16[9,16,512]{2,1,0:T(8,128)(2,1)S(1)} %get-tuple-element.44), channel_id=1, source_target_pairs={{0,2},{2,0},{4,6},{6,4},{8,10},{10,8},{12,14},{14,12},{1,3},{3,1},... | collective-permute-start | bytes 442376 | tf_op jit(solution)/shard_map/ppermute | solution.py:501
  14.8 9.2 %collective-permute-start.1 = (bf16[9,16,512]{2,1,0:T(8,128)(2,1)S(1)}, bf16[9,16,512]{2,1,0:T(8,128)(2,1)S(1)}, u32[]{:S(2)}, u32[]{:S(2)}) collective-permute-start(bf16[9,16,512]{2,1,0:T(8,128)(2,1)S(1)} %get-tuple-element.38), channel_id=1, source_target_pairs={{0,2},{2,0},{4,6},{6,4},{8,10},{10,8},{12,14},{14,12},{1,3},{3,1},... | collective-permute-start | bytes 442376 | tf_op jit(solution)/shard_map/ppermute | solution.py:501
  16.7 10.7 %collective-permute-start.2 = (bf16[9,16,512]{2,1,0:T(8,128)(2,1)S(1)}, bf16[9,16,512]{2,1,0:T(8,128)(2,1)S(1)}, u32[]{:S(2)}, u32[]{:S(2)}) collective-permute-start(bf16[9,16,512]{2,1,0:T(8,128)(2,1)S(1)} %get-tuple-element.39), channel_id=1, source_target_pairs={{0,4},{2,6},{4,0},{6,2},{8,12},{10,14},{12,8},{14,10},{1,5},{3,7},... | collective-permute-start | bytes 442376 | tf_op jit(solution)/shard_map/ppermute | solution.py:501
  18.3 11.3 %collective-permute-start.3 = (bf16[9,16,512]{2,1,0:T(8,128)(2,1)S(1)}, bf16[9,16,512]{2,1,0:T(8,128)(2,1)S(1)}, u32[]{:S(2)}, u32[]{:S(2)}) collective-permute-start(bf16[9,16,512]{2,1,0:T(8,128)(2,1)S(1)} %get-tuple-element.40), channel_id=1, source_target_pairs={{0,6},{2,4},{4,2},{6,0},{8,14},{10,12},{12,10},{14,8},{1,7},{3,5},... | collective-permute-start | bytes 442376 | tf_op jit(solution)/shard_map/ppermute | solution.py:501
  21.3 8.3 %collective-permute-start.7 = (bf16[9,16,512]{2,1,0:T(8,128)(2,1)S(1)}, bf16[9,16,512]{2,1,0:T(8,128)(2,1)S(1)}, u32[]{:S(2)}, u32[]{:S(2)}) collective-permute-start(bf16[9,16,512]{2,1,0:T(8,128)(2,1)S(1)} %merge_lists.3), channel_id=1, source_target_pairs={{0,8},{2,10},{4,12},{6,14},{8,0},{10,2},{12,4},{14,6},{1,9},{3,11}... | collective-permute-start | bytes 442376 | tf_op jit(solution)/shard_map/ppermute | solution.py:501

commit v7 on v6

--- a/solution.py
+++ b/solution.py
@@ -523,9 +523,9 @@
     )
 
     if rows_out == TILE_ROWS and expo_size == 2 * SQUARE:
-        high, low, total, *sent = filter_slots(
-            lambda place, i: place ^ (i + 1) ^ SQUARE,
-            SQUARE - 1,
+        high, low, total, far_z, far_both = filter_slots(
+            lambda place, i: place ^ (i + 2) ^ SQUARE,
+            SQUARE - 2,
             1,
             exposures,
             pictures,
@@ -534,15 +534,18 @@
             bank_h,
             tables,
         )
-        got = [swapped(sent[i], "expo", 1 + i) for i in reversed(range(SQUARE - 1))]
-        kept, *near = select(
-            lambda place, i: place ^ (SQUARE if i == 0 else i - 1),
-            SQUARE + 1,
+        got = [swapped(far_both, "expo", 3), swapped(far_z, "expo", 2)]
+        far_y, kept = select(lambda place, i: place ^ (SQUARE + 1 - i), 2, 1, high, low, total)
+        near = select(
+            lambda place, i: place ^ i,
+            SQUARE,
             1,
             high,
             low,
             total,
         )
+        near = list(near)
+        got.append(swapped(far_y, "expo", 1))
         near = near[:1] + [swapped(part, "expo", 1 + i) for i, part in enumerate(near[1:])]
         across = swapped(merge([kept] + got), "expo", SQUARE)
         coadd_plane, rejected_count = finish(

time: 30.6 us -> 30.5 us (level)
    ppermute x8, starting transfers between devices: 13.3 us -> 13 us  [swapped(): return lax.ppermute(value, axis, [(i, i ^ distance) for i in range(count)])]
    pallas_call x1 -> x2, Pallas kernels: 1.37 us -> 1.65 us  [select(): pl.pallas_call(functools.partial(select_kernel, chunk_of, parts), out_sha...]
  transfers between devices with their start and end apart: 8 -> 8, of which waited for: 3 -> 3; matrix products, arithmetic and copies ran while one was open for 0% -> 0% of each run, Pallas kernels for 10% -> 11%
where the time goes in v7:
time: 30.5 us; the launch traced here: 30.3 us
  starting transfers between devices  13 us (43%)
  Pallas kernels  10.3 us (34%)
  waiting for transfers between devices  6.26 us (21%)
  between operations  0.67 us (2%)
    ppermute x8, starting transfers between devices, swapped(): return lax.ppermute(value, axis, [(i, i ^ distance) for i in range(count)])  13 us
    ppermute x8, waiting for transfers between devices, swapped(): return lax.ppermute(value, axis, [(i, i ^ distance) for i in range(count)])  6.26 us
    pallas_call x1, Pallas kernels, filter_slots(): pl.pallas_call(functools.partial(filter_kernel, chunk_of, parts), out_sha...  5.13 us
    pallas_call x2, Pallas kernels, select(): pl.pallas_call(functools.partial(select_kernel, chunk_of, parts), out_sha...  1.65 us
    pallas_call x1, Pallas kernels, prepare(): pl.pallas_call(functools.partial(prepare_kernel, bands, rows_out), out_sh...  1.38 us
    pallas_call x1, Pallas kernels, window_edges(): pl.pallas_call(edge_kernel, out_shape=[jax.ShapeDtypeStruct((slots, PAD,...  1.09 us
    pallas_call x1, Pallas kernels, finish(): pl.pallas_call(functools.partial(finish_kernel, exposures_total, len(whol...  0.75 us
  transfers between devices with their start and end apart: 8, of which 3 were waited for; matrix products, arithmetic and copies ran while one was open for 0% of the time, Pallas kernels for 11%

profile of v7, /device:TPU:0, one launch (start us, length us, event | category | flops | bytes accessed | tf_op | source)
XLA Modules:
  0.0 30.3 jit_solution(11276262405865906466)
XLA Ops:
  0.6 1.1 %window_edges.1 = (bf16[24,16,512]{2,1,0:T(8,128)(2,1)S(1)}, bf16[10,128,144]{2,1,0:T(8,128)(2,1)S(1)}) custom-call(bf16[24,128,512]{2,1,0:T(8,128)(2,1)} %exposures_ref.5, bf16[10,21]{1,0:T(8,128)(2,1)} %vert_hbm.1), custom_call_target="tpu_custom_call" | custom-call | tf_op jit(solution)/shard_map/window_edges/pallas_call | solution.py:93
  1.7 0.5 %collective-permute-start = (bf16[24,16,512]{2,1,0:T(8,128)(2,1)S(1)}, bf16[24,16,512]{2,1,0:T(8,128)(2,1)S(1)}, u32[]{:S(2)}, u32[]{:S(2)}) collective-permute-start(bf16[24,16,512]{2,1,0:T(8,128)(2,1)S(1)} %get-tuple-element.26), channel_id=1, source_target_pairs={{0,1},{1,0},{2,3},{3,2},{4,5},{5,4},{6,7},{7,6},{8,9},{9,8},{10,11... | collective-permute-start | bytes 1179656 | tf_op jit(solution)/shard_map/ppermute | solution.py:501
  2.2 1.4 %prepare.1 = (bf16[24,128,512]{2,1,0:T(8,128)(2,1)S(1)}, bf16[10,384,128]{2,1,0:T(8,128)(2,1)S(1)}, s32[16,512]{1,0:T(8,128)S(1)}, s32[8,24]{1,0:T(8,128)S(1)}, ...) custom-call(bf16[24,128,512]{2,1,0:T(8,128)(2,1)} %exposures_ref.5, ...), custom_call_target="tpu_custom_call" | custom-call | flops 1048576 | bytes 4194304 | tf_op jit(solution)/shard_map/prepare/pallas_call | solution.py:185
  3.6 0.0 collective-permute-done.halo
  3.6 5.1 %filter_slots.1 = (bf16[24,128,512]{2,1,0:T(8,128)(2,1)S(1)}, bf16[24,128,512]{2,1,0:T(8,128)(2,1)S(1)}, bf16[24,128,512]{2,1,0:T(8,128)(2,1)S(1)}, f32[128,512]...) custom-call(bf16[24,128,512]{2,1,0:T(8,128)(2,1)} %exposures_ref.5, ...), custom_call_target="tpu_custom_call", output_to_operand_aliasing={{0}: (1, {})} | custom-call | flops 1610612736 | bytes 8388608 | tf_op jit(solution)/shard_map/filter_slots/pallas_call | solution.py:368
  8.8 3.9 %collective-permute-start.4 = (bf16[9,16,512]{2,1,0:T(8,128)(2,1)S(1)}, bf16[9,16,512]{2,1,0:T(8,128)(2,1)S(1)}, u32[]{:S(2)}, u32[]{:S(2)}) collective-permute-start(bf16[9,16,512]{2,1,0:T(8,128)(2,1)S(1)} %get-tuple-element.42), channel_id=1, source_target_pairs={{0,6},{2,4},{4,2},{6,0},{8,14},{10,12},{12,10},{14,8},{1,7},{3,5},... | collective-permute-start | bytes 442376 | tf_op jit(solution)/shard_map/ppermute | solution.py:501
  12.7 0.4 %collective-permute-start.5 = (bf16[9,16,512]{2,1,0:T(8,128)(2,1)S(1)}, bf16[9,16,512]{2,1,0:T(8,128)(2,1)S(1)}, u32[]{:S(2)}, u32[]{:S(2)}) collective-permute-start(bf16[9,16,512]{2,1,0:T(8,128)(2,1)S(1)} %get-tuple-element.43), channel_id=1, source_target_pairs={{0,4},{2,6},{4,0},{6,2},{8,12},{10,14},{12,8},{14,10},{1,5},{3,7},... | collective-permute-start | bytes 442376 | tf_op jit(solution)/shard_map/ppermute | solution.py:501
  13.1 0.6 %select_rows.3 = (bf16[9,16,512]{2,1,0:T(8,128)(2,1)S(1)}, bf16[9,16,512]{2,1,0:T(8,128)(2,1)S(1)}) custom-call(bf16[24,128,512]{2,1,0:T(8,128)(2,1)S(1)} %get-tuple-element.34.high, bf16[24,128,512]{2,1,0:T(8,128)(2,1)S(1)} %get-tuple-element.35.low, f32[128,512]{1,0:T(8,128)S(1)} %get-tuple-element.36.total), custom_call_target="tpu_custom_call" | custom-call | flops 16777216 | bytes 4194304 | tf_op jit(solution)/shard_map/select_rows/pallas_call | solution.py:406
  13.7 0.3 collective-permute-start.6
  14.0 1.1 %select_rows.2 = (bf16[9,16,512]{2,1,0:T(8,128)(2,1)S(1)}, bf16[9,16,512]{2,1,0:T(8,128)(2,1)S(1)}, bf16[9,16,512]{2,1,0:T(8,128)(2,1)S(1)}, bf16[9,16,512]{2,1,0:T(8,128)(2,1)S(1)}) custom-call(bf16[24,128,512]{2,1,0:T(8,128)(2,1)S(1)} %get-tuple-element.34.high, bf16[24,128,512]{2,1,0:T(8,128)(2,1)S(1)} %get-tuple-element.35.low, ...), custom_call_target="tpu_custom_call" | custom-call | flops 16777216 | bytes 4194304 | tf_op jit(solution)/shard_map/select_rows/pallas_call | solution.py:406
  15.1 1.9 %collective-permute-start.1 = (bf16[9,16,512]{2,1,0:T(8,128)(2,1)S(1)}, bf16[9,16,512]{2,1,0:T(8,128)(2,1)S(1)}, u32[]{:S(2)}, u32[]{:S(2)}) collective-permute-start(bf16[9,16,512]{2,1,0:T(8,128)(2,1)S(1)} %get-tuple-element.38), channel_id=1, source_target_pairs={{0,2},{2,0},{4,6},{6,4},{8,10},{10,8},{12,14},{14,12},{1,3},{3,1},... | collective-permute-start | bytes 442376 | tf_op jit(solution)/shard_map/ppermute | solution.py:501
  17.0 1.6 %collective-permute-start.2 = (bf16[9,16,512]{2,1,0:T(8,128)(2,1)S(1)}, bf16[9,16,512]{2,1,0:T(8,128)(2,1)S(1)}, u32[]{:S(2)}, u32[]{:S(2)}) collective-permute-start(bf16[9,16,512]{2,1,0:T(8,128)(2,1)S(1)} %get-tuple-element.39), channel_id=1, source_target_pairs={{0,4},{2,6},{4,0},{6,2},{8,12},{10,14},{12,8},{14,10},{1,5},{3,7},... | collective-permute-start | bytes 442376 | tf_op jit(solution)/shard_map/ppermute | solution.py:501
  18.5 0.0 collective-permute-done.4.refs_1_
  18.5 1.7 %collective-permute-start.3 = (bf16[9,16,512]{2,1,0:T(8,128)(2,1)S(1)}, bf16[9,16,512]{2,1,0:T(8,128)(2,1)S(1)}, u32[]{:S(2)}, u32[]{:S(2)}) collective-permute-start(bf16[9,16,512]{2,1,0:T(8,128)(2,1)S(1)} %get-tuple-element.40), channel_id=1, source_target_pairs={{0,6},{2,4},{4,2},{6,0},{8,14},{10,12},{12,10},{14,8},{1,7},{3,5},... | collective-permute-start | bytes 442376 | tf_op jit(solution)/shard_map/ppermute | solution.py:501
  20.3 0.7 %collective-permute-done.5.refs_2_ = bf16[9,16,512]{2,1,0:T(8,128)(2,1)S(1)} collective-permute-done((bf16[9,16,512]{2,1,0:T(8,128)(2,1)S(1)}, bf16[9,16,512]{2,1,0:T(8,128)(2,1)S(1)}, u32[]{:S(2)}, u32[]{:S(2)}) %collective-permute-start.5) | collective-permute-done | bytes 147488 | tf_op jit(solution)/shard_map/ppermute | solution.py:501
  21.0 0.0 collective-permute-done.6.refs_3_
  21.0 0.2 merge_lists.3
  21.2 2.7 %collective-permute-start.7 = (bf16[9,16,512]{2,1,0:T(8,128)(2,1)S(1)}, bf16[9,16,512]{2,1,0:T(8,128)(2,1)S(1)}, u32[]{:S(2)}, u32[]{:S(2)}) collective-permute-start(bf16[9,16,512]{2,1,0:T(8,128)(2,1)S(1)} %merge_lists.3), channel_id=1, source_target_pairs={{0,8},{2,10},{4,12},{6,14},{8,0},{10,2},{12,4},{14,6},{1,9},{3,11}... | collective-permute-start | bytes 442376 | tf_op jit(solution)/shard_map/ppermute | solution.py:501
  23.8 0.0 collective-permute-done.1.refs_1_
  23.8 1.9 %collective-permute-done.2.refs_2_ = bf16[9,16,512]{2,1,0:T(8,128)(2,1)S(1)} collective-permute-done((bf16[9,16,512]{2,1,0:T(8,128)(2,1)S(1)}, bf16[9,16,512]{2,1,0:T(8,128)(2,1)S(1)}, u32[]{:S(2)}, u32[]{:S(2)}) %collective-permute-start.2) | collective-permute-done | bytes 147488 | tf_op jit(solution)/shard_map/ppermute | solution.py:501
  25.7 0.1 merge_lists.2.refs_0_
  25.9 3.7 %collective-permute-done.3.refs_1_ = bf16[9,16,512]{2,1,0:T(8,128)(2,1)S(1)} collective-permute-done((bf16[9,16,512]{2,1,0:T(8,128)(2,1)S(1)}, bf16[9,16,512]{2,1,0:T(8,128)(2,1)S(1)}, u32[]{:S(2)}, u32[]{:S(2)}) %collective-permute-start.3) | collective-permute-done | bytes 147488 | tf_op jit(solution)/shard_map/ppermute | solution.py:501
  29.5 0.0 collective-permute-done.7.refs_2_
  29.5 0.8 %finish_pixels.1 = (f32[16,512]{1,0:T(8,128)}, s32[16,512]{1,0:T(8,128)}) custom-call(bf16[9,16,512]{2,1,0:T(8,128)(2,1)S(1)} %merge_lists.2.refs_0_, bf16[9,16,512]{2,1,0:T(8,128)(2,1)S(1)} %collective-permute-done.3.refs_1_, bf16[9,16,512]{2,1,0:T(8,128)(2,1)S(1)} %collective-permute-done.7.refs_2_, s32[16,512]{1,0:T(8,128)S(1)} %get-tuple-element.45.refs_3_), custom_call_target="tpu_custom_call" | custom-call | tf_op jit(solution)/shard_map/finish_pixels/pallas_call | solution.py:486
Async XLA Ops:
  1.7 1.9 %collective-permute-start = (bf16[24,16,512]{2,1,0:T(8,128)(2,1)S(1)}, bf16[24,16,512]{2,1,0:T(8,128)(2,1)S(1)}, u32[]{:S(2)}, u32[]{:S(2)}) collective-permute-start(bf16[24,16,512]{2,1,0:T(8,128)(2,1)S(1)} %get-tuple-element.26), channel_id=1, source_target_pairs={{0,1},{1,0},{2,3},{3,2},{4,5},{5,4},{6,7},{7,6},{8,9},{9,8},{10,11... | collective-permute-start | bytes 1179656 | tf_op jit(solution)/shard_map/ppermute | solution.py:501
  8.8 9.8 %collective-permute-start.4 = (bf16[9,16,512]{2,1,0:T(8,128)(2,1)S(1)}, bf16[9,16,512]{2,1,0:T(8,128)(2,1)S(1)}, u32[]{:S(2)}, u32[]{:S(2)}) collective-permute-start(bf16[9,16,512]{2,1,0:T(8,128)(2,1)S(1)} %get-tuple-element.42), channel_id=1, source_target_pairs={{0,6},{2,4},{4,2},{6,0},{8,14},{10,12},{12,10},{14,8},{1,7},{3,5},... | collective-permute-start | bytes 442376 | tf_op jit(solution)/shard_map/ppermute | solution.py:501
  12.7 8.3 %collective-permute-start.5 = (bf16[9,16,512]{2,1,0:T(8,128)(2,1)S(1)}, bf16[9,16,512]{2,1,0:T(8,128)(2,1)S(1)}, u32[]{:S(2)}, u32[]{:S(2)}) collective-permute-start(bf16[9,16,512]{2,1,0:T(8,128)(2,1)S(1)} %get-tuple-element.43), channel_id=1, source_target_pairs={{0,4},{2,6},{4,0},{6,2},{8,12},{10,14},{12,8},{14,10},{1,5},{3,7},... | collective-permute-start | bytes 442376 | tf_op jit(solution)/shard_map/ppermute | solution.py:501
  13.7 7.3 %collective-permute-start.6 = (bf16[9,16,512]{2,1,0:T(8,128)(2,1)S(1)}, bf16[9,16,512]{2,1,0:T(8,128)(2,1)S(1)}, u32[]{:S(2)}, u32[]{:S(2)}) collective-permute-start(bf16[9,16,512]{2,1,0:T(8,128)(2,1)S(1)} %get-tuple-element.44), channel_id=1, source_target_pairs={{0,2},{2,0},{4,6},{6,4},{8,10},{10,8},{12,14},{14,12},{1,3},{3,1},... | collective-permute-start | bytes 442376 | tf_op jit(solution)/shard_map/ppermute | solution.py:501
  15.1 8.8 %collective-permute-start.1 = (bf16[9,16,512]{2,1,0:T(8,128)(2,1)S(1)}, bf16[9,16,512]{2,1,0:T(8,128)(2,1)S(1)}, u32[]{:S(2)}, u32[]{:S(2)}) collective-permute-start(bf16[9,16,512]{2,1,0:T(8,128)(2,1)S(1)} %get-tuple-element.38), channel_id=1, source_target_pairs={{0,2},{2,0},{4,6},{6,4},{8,10},{10,8},{12,14},{14,12},{1,3},{3,1},... | collective-permute-start | bytes 442376 | tf_op jit(solution)/shard_map/ppermute | solution.py:501
  17.0 8.8 %collective-permute-start.2 = (bf16[9,16,512]{2,1,0:T(8,128)(2,1)S(1)}, bf16[9,16,512]{2,1,0:T(8,128)(2,1)S(1)}, u32[]{:S(2)}, u32[]{:S(2)}) collective-permute-start(bf16[9,16,512]{2,1,0:T(8,128)(2,1)S(1)} %get-tuple-element.39), channel_id=1, source_target_pairs={{0,4},{2,6},{4,0},{6,2},{8,12},{10,14},{12,8},{14,10},{1,5},{3,7},... | collective-permute-start | bytes 442376 | tf_op jit(solution)/shard_map/ppermute | solution.py:501
  18.5 11.0 %collective-permute-start.3 = (bf16[9,16,512]{2,1,0:T(8,128)(2,1)S(1)}, bf16[9,16,512]{2,1,0:T(8,128)(2,1)S(1)}, u32[]{:S(2)}, u32[]{:S(2)}) collective-permute-start(bf16[9,16,512]{2,1,0:T(8,128)(2,1)S(1)} %get-tuple-element.40), channel_id=1, source_target_pairs={{0,6},{2,4},{4,2},{6,0},{8,14},{10,12},{12,10},{14,8},{1,7},{3,5},... | collective-permute-start | bytes 442376 | tf_op jit(solution)/shard_map/ppermute | solution.py:501
  21.2 8.4 %collective-permute-start.7 = (bf16[9,16,512]{2,1,0:T(8,128)(2,1)S(1)}, bf16[9,16,512]{2,1,0:T(8,128)(2,1)S(1)}, u32[]{:S(2)}, u32[]{:S(2)}) collective-permute-start(bf16[9,16,512]{2,1,0:T(8,128)(2,1)S(1)} %merge_lists.3), channel_id=1, source_target_pairs={{0,8},{2,10},{4,12},{6,14},{8,0},{10,2},{12,4},{14,6},{1,9},{3,11}... | collective-permute-start | bytes 442376 | tf_op jit(solution)/shard_map/ppermute | solution.py:501
